TPU v7x, 32 devices: a whole 2x2x4 slice. The times are simulated.
32 devices in a mesh: dp: 8 (over z, x), tensor: 4 (over y, core).
Axes of the slice: x: 2, y: 2, z: 4, core: 2. Of those that a mesh axis runs over, the one named last changes fastest.
Arguments:
- tokens: bfloat16 [15360, 1024], P(('dp', 'tensor')), may hold values from -6 to 6
- token_kinds: int32 [24, 640], P('dp'), may hold values 0 or 1
- segment_ids: int32 [24, 640], P('dp'), may hold values from 0 to 3, never falling along the last dimension, each value on 1 to 320 neighbouring positions
- cotangent: bfloat16 [15360, 1024], P(('dp', 'tensor')), may hold values from -6 to 6
- query_weight: bfloat16 [1, 4, 1024, 1024], P(None, None, None, 'tensor'), may hold values from -0.1875 to 0.1875
- query_bias: bfloat16 [1, 4, 1024], P(None, None, 'tensor'), may hold values from -3 to 3
- key_weight: bfloat16 [1, 1024, 1024], P(None, None, 'tensor'), may hold values from -0.1875 to 0.1875
- key_bias: bfloat16 [1, 1024], P(None, 'tensor'), may hold values from -3 to 3
- value_weight: bfloat16 [1, 1024, 1024], P(None, None, 'tensor'), may hold values from -0.1875 to 0.1875
- value_bias: bfloat16 [1, 1024], P(None, 'tensor'), may hold values from -3 to 3
- output_weight: bfloat16 [1, 1024, 1024], P(None, 'tensor'), may hold values from -1.5 to 1.5
- output_bias: float32 [1, 1024], replicated, may hold values from -2 to 2
- inner_gain: float32 [1, 1024], replicated, may hold values from 0.5 to 1.5
- inner_shift: float32 [1, 1024], replicated, may hold values from -2 to 2
- expand_weight: bfloat16 [1, 1024, 4096], P(None, None, 'tensor'), may hold values from -0.1875 to 0.1875
- expand_bias: bfloat16 [1, 4096], P(None, 'tensor'), may hold values from -3 to 3
- contract_weight: bfloat16 [1, 4096, 1024], P(None, 'tensor'), may hold values from -0.09375 to 0.09375
- contract_bias: float32 [1, 1024], replicated, may hold values from -2 to 2
- outer_gain: float32 [1, 1024], replicated, may hold values from 0.5 to 1.5
- outer_shift: float32 [1, 1024], replicated, may hold values from -2 to 2
Outputs:
- result: float32 [15360, 1024], P(('dp', 'tensor'))
- tokens_gradient: float32 [15360, 1024], P(('dp', 'tensor'))
- query_weight_gradient: float32 [1, 4, 1024, 1024], P(None, None, None, 'tensor')
- query_bias_gradient: float32 [1, 4, 1024], P(None, None, 'tensor')
- key_weight_gradient: float32 [1, 1024, 1024], P(None, None, 'tensor')
- key_bias_gradient: float32 [1, 1024], P(None, 'tensor')
- value_weight_gradient: float32 [1, 1024, 1024], P(None, None, 'tensor')
- value_bias_gradient: float32 [1, 1024], P(None, 'tensor')
- output_weight_gradient: float32 [1, 1024, 1024], P(None, 'tensor')
- output_bias_gradient: float32 [1, 1024], replicated
- inner_gain_gradient: float32 [1, 1024], replicated
- inner_shift_gradient: float32 [1, 1024], replicated
- expand_weight_gradient: float32 [1, 1024, 4096], P(None, None, 'tensor')
- expand_bias_gradient: float32 [1, 4096], P(None, 'tensor')
- contract_weight_gradient: float32 [1, 4096, 1024], P(None, 'tensor')
- contract_bias_gradient: float32 [1, 1024], replicated
- outer_gain_gradient: float32 [1, 1024], replicated
- outer_shift_gradient: float32 [1, 1024], replicated
Inputs may be any that keep to these rules, and one draw needn't show every extreme that they name: `segment_ids`: document numbers never fall along a sequence; each sequence holds all 4 documents.
All inputs are finite; a program needn't handle non-finite values. No bound on the sum of `token_kinds` on one device may be relied on, other than what follows from the above.
Results may differ from a plain program's by a relative error of at most 0.02.
Values may be sent and summed in bfloat16 or wider, within the bound.
No kernel may reach another device: no remote copies, remote signals or barrier semaphores. Data moves between devices by JAX's collectives and lax.ppermute only.
A program may use at most 128 MiB of HBM per device.

v0:
```python
import jax
import jax.numpy as jnp
from jax import lax
from jax.sharding import PartitionSpec as P

HD = 64


NORM_EPS = 1e-05
MASKED = -1e30


def product(left_side, right_side):
    return jnp.dot(left_side, right_side, preferred_element_type=jnp.float32)


def product_left_t(left_side, right_side):
    return lax.dot_general(
        left_side, right_side, (((0,), (0,)), ((), ())), preferred_element_type=jnp.float32
    )


def product_right_t(left_side, right_side):
    return lax.dot_general(
        left_side, right_side, (((1,), (1,)), ((), ())), preferred_element_type=jnp.float32
    )


def exact_gelu(values):
    return jax.nn.gelu(values, approximate=False)


def norm_rows(values, norm_gain, norm_shift):
    centre = jnp.mean(values, axis=-1, keepdims=True)
    offset = values - centre
    spread = jnp.mean(offset * offset, axis=-1, keepdims=True)
    rstd_rows = lax.rsqrt(spread + NORM_EPS)
    normed = offset * rstd_rows
    return (normed * norm_gain + norm_shift, normed, rstd_rows)


def norm_back(upstream, normed, rstd_rows, norm_gain):
    scaled = upstream * norm_gain
    inner_mean = jnp.mean(scaled, axis=-1, keepdims=True)
    cross_mean = jnp.mean(scaled * normed, axis=-1, keepdims=True)
    delta = rstd_rows * (scaled - inner_mean - normed * cross_mean)
    return (delta, jnp.sum(upstream * normed, axis=0), jnp.sum(upstream, axis=0))


def score_block(query_word, query_entity, keys_seq, kinds_row, segments_row):
    length = keys_seq.shape[0]
    word_heads = query_word.reshape(length, -1, HD)
    entity_heads = query_entity.reshape(length, -1, HD)
    key_heads = keys_seq.reshape(length, -1, HD)
    to_word = jnp.einsum("qhd,khd->hqk", word_heads, key_heads, preferred_element_type=jnp.float32)
    to_entity = jnp.einsum(
        "qhd,khd->hqk", entity_heads, key_heads, preferred_element_type=jnp.float32
    )
    key_is_word = (kinds_row == 0)[None, None, :]
    raw_scores = jnp.where(key_is_word, to_word, to_entity) * HD ** (-0.5)
    same_doc = (segments_row[:, None] == segments_row[None, :])[None]
    return (raw_scores, same_doc, key_is_word, word_heads, entity_heads, key_heads)


def attend_forward(inputs):
    query_word, query_entity, keys_seq, values_seq, kinds_row, segments_row = inputs
    length = keys_seq.shape[0]
    raw_scores, same_doc, key_is_word, word_heads, entity_heads, key_heads = score_block(
        query_word, query_entity, keys_seq, kinds_row, segments_row
    )
    masked = jnp.where(same_doc, raw_scores, MASKED)
    row_top = jnp.max(masked, axis=-1, keepdims=True)
    exponent = jnp.exp(masked - row_top)
    row_total = jnp.sum(exponent, axis=-1, keepdims=True)
    soft_weights = (exponent / row_total).astype(jnp.bfloat16)
    value_heads = values_seq.reshape(length, -1, HD)
    mixed_heads = jnp.einsum(
        "hqk,khd->qhd", soft_weights, value_heads, preferred_element_type=jnp.float32
    )
    return (mixed_heads.reshape(length, -1).astype(jnp.bfloat16), row_top + jnp.log(row_total))


def attend_backward(inputs):
    (
        query_word,
        query_entity,
        keys_seq,
        values_seq,
        kinds_row,
        segments_row,
        log_totals,
        context_delta,
    ) = inputs
    length = keys_seq.shape[0]
    raw_scores, same_doc, key_is_word, word_heads, entity_heads, key_heads = score_block(
        query_word, query_entity, keys_seq, kinds_row, segments_row
    )
    soft_full = jnp.where(same_doc, jnp.exp(raw_scores - log_totals), 0.0)
    value_heads = values_seq.reshape(length, -1, HD)
    delta_heads = context_delta.reshape(length, -1, HD)
    soft_delta = jnp.einsum(
        "qhd,khd->hqk", delta_heads, value_heads, preferred_element_type=jnp.float32
    )
    row_inner = jnp.sum(soft_full * soft_delta, axis=-1, keepdims=True)
    score_delta = (soft_full * (soft_delta - row_inner)).astype(jnp.bfloat16)
    value_delta = jnp.einsum(
        "hqk,qhd->khd",
        soft_full.astype(jnp.bfloat16),
        delta_heads,
        preferred_element_type=jnp.float32,
    )
    zero_scores = jnp.zeros_like(score_delta)
    word_delta = jnp.where(key_is_word, score_delta, zero_scores)
    entity_delta = jnp.where(key_is_word, zero_scores, score_delta)
    score_scale = HD ** (-0.5)
    word_query_delta = jnp.einsum(
        "hqk,khd->qhd", word_delta, key_heads, preferred_element_type=jnp.float32
    )
    entity_query_delta = jnp.einsum(
        "hqk,khd->qhd", entity_delta, key_heads, preferred_element_type=jnp.float32
    )
    key_delta = jnp.einsum(
        "hqk,qhd->khd", word_delta, word_heads, preferred_element_type=jnp.float32
    )
    key_delta = key_delta + jnp.einsum(
        "hqk,qhd->khd", entity_delta, entity_heads, preferred_element_type=jnp.float32
    )
    return (
        (word_query_delta * score_scale).reshape(length, -1).astype(jnp.bfloat16),
        (entity_query_delta * score_scale).reshape(length, -1).astype(jnp.bfloat16),
        (key_delta * score_scale).reshape(length, -1).astype(jnp.bfloat16),
        value_delta.reshape(length, -1).astype(jnp.bfloat16),
    )


def body(
    tokens,
    token_kinds,
    segment_ids,
    cotangent,
    query_weight,
    query_bias,
    key_weight,
    key_bias,
    value_weight,
    value_bias,
    output_weight,
    output_bias,
    inner_gain,
    inner_shift,
    expand_weight,
    expand_bias,
    contract_weight,
    contract_bias,
    outer_gain,
    outer_shift,
):
    seq_count, seq_length = token_kinds.shape
    word_rows = (token_kinds.reshape(-1) == 0)[:, None]
    layer_count = query_weight.shape[0]
    hidden = tokens.astype(jnp.float32)
    layer_index = 0
    rounded_in = hidden.astype(jnp.bfloat16)
    gathered_in = lax.all_gather(rounded_in, "tensor", axis=0, tiled=True)
    query_all = jnp.einsum(
        "td,sde->ste", gathered_in, query_weight[layer_index], preferred_element_type=jnp.float32
    )
    query_all = query_all + query_bias[layer_index].astype(jnp.float32)[:, None, :]
    query_word = jnp.where(word_rows, query_all[0], query_all[2]).astype(jnp.bfloat16)
    query_entity = jnp.where(word_rows, query_all[1], query_all[3]).astype(jnp.bfloat16)
    keys_all = (
        product(gathered_in, key_weight[layer_index]) + key_bias[layer_index].astype(jnp.float32)
    ).astype(jnp.bfloat16)
    values_all = (
        product(gathered_in, value_weight[layer_index])
        + value_bias[layer_index].astype(jnp.float32)
    ).astype(jnp.bfloat16)
    local_width = keys_all.shape[1]
    context, log_totals = lax.map(
        attend_forward,
        (
            query_word.reshape(seq_count, seq_length, local_width),
            query_entity.reshape(seq_count, seq_length, local_width),
            keys_all.reshape(seq_count, seq_length, local_width),
            values_all.reshape(seq_count, seq_length, local_width),
            token_kinds,
            segment_ids,
        ),
    )
    context = context.reshape(-1, local_width)
    out_proj = output_weight[layer_index]
    attention_rows = lax.psum_scatter(
        product(context, out_proj), "tensor", scatter_dimension=0, tiled=True
    )
    inner_sum = attention_rows + output_bias[layer_index] + hidden
    inner_out, inner_normed, inner_rstd = norm_rows(
        inner_sum, inner_gain[layer_index], inner_shift[layer_index]
    )
    rounded_mid = inner_out.astype(jnp.bfloat16)
    gathered_mid = lax.all_gather(rounded_mid, "tensor", axis=0, tiled=True)
    expanded = product(gathered_mid, expand_weight[layer_index]) + expand_bias[layer_index].astype(
        jnp.float32
    )
    activated = exact_gelu(expanded).astype(jnp.bfloat16)
    contract_proj = contract_weight[layer_index]
    ffn_rows = lax.psum_scatter(
        product(activated, contract_proj), "tensor", scatter_dimension=0, tiled=True
    )
    outer_sum = ffn_rows + contract_bias[layer_index] + inner_out
    hidden, outer_normed, outer_rstd = norm_rows(
        outer_sum, outer_gain[layer_index], outer_shift[layer_index]
    )
    kept_in = gathered_in
    kept_mid = gathered_mid
    saved = [
        (
            kept_in,
            query_word,
            query_entity,
            keys_all,
            values_all,
            context,
            log_totals,
            inner_normed,
            inner_rstd,
            kept_mid,
            expanded,
            activated,
            outer_normed,
            outer_rstd,
        )
    ]
    upstream = cotangent.astype(jnp.float32)
    weight_parts = [None] * layer_count
    norm_parts = [None] * layer_count
    for layer_index in reversed(range(layer_count)):
        (
            kept_in,
            query_word,
            query_entity,
            keys_all,
            values_all,
            context,
            log_totals,
            inner_normed,
            inner_rstd,
            kept_mid,
            expanded,
            activated,
            outer_normed,
            outer_rstd,
        ) = saved[layer_index]
        gathered_in, gathered_mid = (kept_in, kept_mid)
        local_width = keys_all.shape[1]
        outer_delta, outer_gain_grad, outer_shift_grad = norm_back(
            upstream, outer_normed, outer_rstd, outer_gain[layer_index]
        )
        contract_bias_grad = jnp.sum(outer_delta, axis=0)
        ffn_delta = lax.all_gather(outer_delta.astype(jnp.bfloat16), "tensor", axis=0, tiled=True)
        act_delta = product_right_t(ffn_delta, contract_weight[layer_index])
        contract_weight_grad = product_left_t(activated, ffn_delta)
        gelu_value, gelu_pull = jax.vjp(exact_gelu, expanded)
        expand_delta = gelu_pull(act_delta)[0].astype(jnp.bfloat16)
        expand_bias_grad = jnp.sum(expand_delta.astype(jnp.float32), axis=0)
        expand_weight_grad = product_left_t(gathered_mid, expand_delta)
        ffn_summed = (expand_weight_grad, expand_bias_grad, contract_weight_grad)
        expand_proj = expand_weight[layer_index]
        mid_rows = lax.psum_scatter(
            product_right_t(expand_delta, expand_proj), "tensor", scatter_dimension=0, tiled=True
        )
        inner_delta, inner_gain_grad, inner_shift_grad = norm_back(
            outer_delta + mid_rows, inner_normed, inner_rstd, inner_gain[layer_index]
        )
        output_bias_grad = jnp.sum(inner_delta, axis=0)
        attention_delta = lax.all_gather(
            inner_delta.astype(jnp.bfloat16), "tensor", axis=0, tiled=True
        )
        context_delta = product_right_t(attention_delta, output_weight[layer_index]).astype(
            jnp.bfloat16
        )
        output_weight_grad = product_left_t(context, attention_delta)
        word_query_delta, entity_query_delta, key_delta, value_delta = lax.map(
            attend_backward,
            (
                query_word.reshape(seq_count, seq_length, local_width),
                query_entity.reshape(seq_count, seq_length, local_width),
                keys_all.reshape(seq_count, seq_length, local_width),
                values_all.reshape(seq_count, seq_length, local_width),
                token_kinds,
                segment_ids,
                log_totals,
                context_delta.reshape(seq_count, seq_length, local_width),
            ),
        )
        word_query_delta = word_query_delta.reshape(-1, local_width)
        entity_query_delta = entity_query_delta.reshape(-1, local_width)
        key_delta = key_delta.reshape(-1, local_width)
        value_delta = value_delta.reshape(-1, local_width)
        zero_rows = jnp.zeros_like(word_query_delta)
        query_delta = jnp.stack(
            [
                jnp.where(word_rows, word_query_delta, zero_rows),
                jnp.where(word_rows, entity_query_delta, zero_rows),
                jnp.where(word_rows, zero_rows, word_query_delta),
                jnp.where(word_rows, zero_rows, entity_query_delta),
            ]
        )
        query_weight_grad = jnp.einsum(
            "td,ste->sde", gathered_in, query_delta, preferred_element_type=jnp.float32
        )
        query_bias_grad = jnp.sum(query_delta.astype(jnp.float32), axis=1)
        key_weight_grad = product_left_t(gathered_in, key_delta)
        key_bias_grad = jnp.sum(key_delta.astype(jnp.float32), axis=0)
        value_weight_grad = product_left_t(gathered_in, value_delta)
        value_bias_grad = jnp.sum(value_delta.astype(jnp.float32), axis=0)
        query_proj = query_weight[layer_index]
        key_proj = key_weight[layer_index]
        value_proj = value_weight[layer_index]
        partial_sum = jnp.einsum(
            "ste,sde->td", query_delta, query_proj, preferred_element_type=jnp.float32
        )
        partial_sum = partial_sum + product_right_t(key_delta, key_proj)
        input_rows = lax.psum_scatter(
            partial_sum + product_right_t(value_delta, value_proj),
            "tensor",
            scatter_dimension=0,
            tiled=True,
        )
        upstream = inner_delta + input_rows
        attention_parts = (
            query_weight_grad,
            query_bias_grad,
            key_weight_grad,
            key_bias_grad,
            value_weight_grad,
            value_bias_grad,
            output_weight_grad,
        )
        weight_parts[layer_index] = tuple(attention_parts) + tuple(ffn_summed)
        norm_parts[layer_index] = (
            output_bias_grad,
            inner_gain_grad,
            inner_shift_grad,
            contract_bias_grad,
            outer_gain_grad,
            outer_shift_grad,
        )
    stacked_weights = [jnp.stack([weight_parts[0][member]]) for member in range(10)]
    stacked_norms = [jnp.stack([norm_parts[0][member]]) for member in range(6)]
    stacked_weights = lax.psum(
        (
            stacked_weights[0],
            stacked_weights[1],
            stacked_weights[2],
            stacked_weights[3],
            stacked_weights[4],
            stacked_weights[5],
            stacked_weights[6],
            stacked_weights[7],
            stacked_weights[8],
            stacked_weights[9],
        ),
        "dp",
    )
    stacked_norms = lax.psum(
        (
            stacked_norms[0],
            stacked_norms[1],
            stacked_norms[2],
            stacked_norms[3],
            stacked_norms[4],
            stacked_norms[5],
        ),
        ("dp", "tensor"),
    )
    return (
        hidden,
        upstream,
        stacked_weights[0],
        stacked_weights[1],
        stacked_weights[2],
        stacked_weights[3],
        stacked_weights[4],
        stacked_weights[5],
        stacked_weights[6],
        stacked_norms[0],
        stacked_norms[1],
        stacked_norms[2],
        stacked_weights[7],
        stacked_weights[8],
        stacked_weights[9],
        stacked_norms[3],
        stacked_norms[4],
        stacked_norms[5],
    )


def solution(mesh):
    return jax.shard_map(
        body,
        mesh=mesh,
        in_specs=(
            P(("dp", "tensor"), None),
            P("dp", None),
            P("dp", None),
            P(("dp", "tensor"), None),
            P(None, None, None, "tensor"),
            P(None, None, "tensor"),
            P(None, None, "tensor"),
            P(None, "tensor"),
            P(None, None, "tensor"),
            P(None, "tensor"),
            P(None, "tensor", None),
            P(),
            P(),
            P(),
            P(None, None, "tensor"),
            P(None, "tensor"),
            P(None, "tensor", None),
            P(),
            P(),
            P(),
        ),
        out_specs=(
            P(("dp", "tensor"), None),
            P(("dp", "tensor"), None),
            P(None, None, None, "tensor"),
            P(None, None, "tensor"),
            P(None, None, "tensor"),
            P(None, "tensor"),
            P(None, None, "tensor"),
            P(None, "tensor"),
            P(None, "tensor", None),
            P(),
            P(),
            P(),
            P(None, None, "tensor"),
            P(None, "tensor"),
            P(None, "tensor", None),
            P(),
            P(),
            P(),
        ),
        check_vma=False,
    )
```

profile of v0, /device:TPU:0, one launch (start us, length us, event | category | flops | bytes accessed | tf_op | source)
XLA Modules:
  0.0 1287.3 jit_solution(11952776301855996014)
XLA Ops:
  10.8 34.6 %all-gather.5.cloned.1.call-done = bf16[1920,1024]{1,0:T(8,128)(2,1)} async-done(((bf16[480,1024]{1,0:T(8,128)(2,1)}), bf16[1920,1024]{1,0:T(8,128)(2,1)}) %all-gather.5.cloned.1.call-update) | async-done | bytes 3932176 | tf_op jit(solution)/shard_map/all_gather | solution.py:164
  45.3 4.4 fusion.78
  51.2 4.4 fusion.79
  57.8 7.6 add_bitcast_fusion
  76.4 3.3 select_convert_fusion
  85.2 32.5 %while.28 = (s32[]{:T(128)}, bf16[3,640,256]{2,1,0:T(8,128)(2,1)}, f32[3,4,640,1]{2,1,3,0:T(4,128)S(1)}, bf16[3,640,256]{1,2,0:T(8,128)(2,1)S(1)}, s32[3,640]{1,...) while((s32[]{:T(128)}, bf16[3,640,256]{2,1,0:T(8,128)(2,1)}, ...), condition=%wide.region_3.4_spmd, body=%wide.region_0.3_spmd.sunk | while | flops 644462720 | bytes 39579012 | solution.py:179
  117.8 5.6 fusion.102
  123.5 69.1 %reduce-scatter.5.cloned.1.call-done = f32[480,1024]{1,0:T(8,128)} async-done(((f32[1920,1024]{1,0:T(8,128)}), f32[480,1024]{1,0:T(8,128)}) %reduce-scatter.5.cloned.1.call-update) | async-done | bytes 1966096 | tf_op jit(solution)/shard_map/reduce_scatter | solution.py:192
  197.4 33.1 %all-gather.7.cloned.1.call-done = bf16[1920,1024]{1,0:T(8,128)(2,1)} async-done(((bf16[480,1024]{1,0:T(8,128)(2,1)}), bf16[1920,1024]{1,0:T(8,128)(2,1)}) %all-gather.7.cloned.1.call-update) | async-done | bytes 3932176 | tf_op jit(solution)/shard_map/all_gather | solution.py:200
  230.5 23.7 %multiply_convert_fusion.1 = (bf16[1920,1024]{1,0:T(8,128)(2,1)S(1)}, f32[1920,1024]{1,0:T(8,128)}, f32[1920,1024]{1,0:T(8,128)}) fusion(f32[1024]{0:T(1024)S(1)} %bitcast.290, bf16[1920,1024]{1,0:T(8,128)(2,1)} %all-gather.7.cloned.1.call-done, bf16[1,1024,1024]{2,1,0:T(8,128)(2,1)S(1)} %copy-done), kind=kOutput, calls=%fused_computation.66 | convolution fusion | flops 4156293120 | bytes 25694208 | tf_op jit(solution)/shard_map/dot_general | solution.py:14
  256.2 6.3 fusion.85
  262.6 69.1 %reduce-scatter.7.cloned.1.call-done = f32[480,1024]{1,0:T(8,128)} async-done(((f32[1920,1024]{1,0:T(8,128)}), f32[480,1024]{1,0:T(8,128)}) %reduce-scatter.7.cloned.1.call-update) | async-done | bytes 1966096 | tf_op jit(solution)/shard_map/reduce_scatter | solution.py:206
  331.7 2.9 fusion.112
  341.6 33.1 %all-gather.9.cloned.1.call-done = bf16[1920,1024]{1,0:T(8,128)(2,1)} async-done(((bf16[480,1024]{1,0:T(8,128)(2,1)}), bf16[1920,1024]{1,0:T(8,128)(2,1)}) %all-gather.9.cloned.1.call-update) | async-done | bytes 3932176 | tf_op jit(solution)/shard_map/all_gather | solution.py:259
  374.7 13.4 %convert_reduce_fusion = (f32[1024]{0:T(1024)}, bf16[1920,1024]{1,0:T(8,128)(2,1)S(1)}) fusion(f32[1920,1024]{1,0:T(8,128)} %get-tuple-element.298, bf16[1920,1024]{1,0:T(8,128)(2,1)} %all-gather.9.cloned.1.call-done, bf16[1,1024,1024]{2,1,0:T(8,128)(2,1)} %param.40, f32[1920,1024]{1,0:T(8,128)} %get-tuple-element.324, f32[1024]{0:T(1024)S(1)} %bitcast.291), kind=kOutput, calls=%fused_computation.63 | convolution fusion | flops 4059954176 | bytes 25698304 | tf_op jit(solution)/shard_map/dot_general | solution.py:24
  390.0 6.7 fusion.89
  396.8 69.1 %reduce-scatter.9.cloned.1.call-done = f32[480,1024]{1,0:T(8,128)} async-done(((f32[1920,1024]{1,0:T(8,128)}), f32[480,1024]{1,0:T(8,128)}) %reduce-scatter.9.cloned.1.call-update) | async-done | bytes 1966096 | tf_op jit(solution)/shard_map/reduce_scatter | solution.py:268
  465.9 3.7 multiply_reduce_fusion.1
  473.4 10.0 convolution_bitcast_fusion
  483.4 6.1 convolution_bitcast_fusion.1
  489.5 16.9 %all-gather.11.cloned.1.call-done = bf16[1920,1024]{1,0:T(8,128)(2,1)} async-done(((bf16[480,1024]{1,0:T(8,128)(2,1)}), bf16[1920,1024]{1,0:T(8,128)(2,1)}) %all-gather.11.cloned.1.call-update) | async-done | bytes 3932176 | tf_op jit(solution)/shard_map/all_gather | solution.py:275
  506.4 4.3 convolution_convert_fusion
  512.7 178.2 %while.29 = (s32[]{:T(128)}, bf16[3,640,256]{2,1,0:T(8,128)(2,1)}, bf16[3,640,256]{2,1,0:T(8,128)(2,1)}, bf16[3,640,256]{1,2,0:T(8,128)(2,1)}, bf16[3,640,256]{1...) while((s32[]{:T(128)}, bf16[3,640,256]{2,1,0:T(8,128)(2,1)}, ...), condition=%wide.region_17.18_spmd, body=%wide.region_15.17_spmd.sunk | while | flops 1720415360 | bytes 126365640 | solution.py:282
  517.8 3.8 fusion.216
  528.8 11.0 fusion.220
  539.7 10.5 fusion.221
  550.2 10.0 fusion.218
  560.2 10.0 fusion.217
  577.1 3.8 fusion.216
  588.0 11.0 fusion.220
  599.0 10.5 fusion.221
  609.5 10.0 fusion.218
  619.5 10.0 fusion.217
  636.4 3.8 fusion.216
  647.3 11.0 fusion.220
  658.3 10.5 fusion.221
  668.7 10.0 fusion.218
  678.8 10.0 fusion.217
  705.9 6.1 fusion.80
  714.6 4.4 fusion.93
  719.0 4.4 fusion.63
  724.2 46.1 %all-reduce = (f32[1,1024]{1,0:T(1,128)}, f32[1,1024]{1,0:T(1,128)}, f32[1,1024]{1,0:T(1,128)}, f32[1,1024]{1,0:T(1,128)}, f32[1,1024]{1,0:T(1,128)}, /*index=5*/f32[1,1024]{1,0:T(1,128)}) all-reduce(f32[1,1024]{1,0:T(1,128)S(1)} %bitcast.285, f32[1,1024]{1,0:T(1,128)S(1)} %bitcast.275, ...), channel_id=1, replica_groups=mesh['dp'=8,'tensor'=4] {'dp','tensor'}, use_global_device_ids=true, to_apply=%region_30.31 | all-reduce | flops 6144 | bytes 49152 | tf_op jit(solution)/shard_map/psum | solution.py:365
  774.8 38.2 %all-reduce.1 = (f32[1,4,256]{2,1,0:T(4,128)}, f32[1,256]{1,0:T(1,128)}, f32[1,256]{1,0:T(1,128)}, f32[1,1024]{1,0:T(1,128)}) all-reduce(f32[1,4,256]{2,1,0:T(4,128)S(1)} %bitcast.279, f32[1,256]{1,0:T(1,128)S(1)} %bitcast.288, f32[1,256]{1,0:T(1,128)S(1)} %bitcast.287, ...), channel_id=1, replica_groups=mesh['dp'=8,'tensor'=4] {'dp'}, use_global_device_ids=true, to_apply=%region_21.22 | all-reduce | flops 2560 | bytes 20480 | tf_op jit(solution)/shard_map/psum | solution.py:350
  813.0 386.8 %all-reduce.5.cloned.1.call-done = (f32[1,4,1024,256]{2,3,1,0:T(8,128)}, f32[1,1024,256]{1,2,0:T(8,128)}, f32[1,1024,256]{1,2,0:T(8,128)}, f32[1,256,1024]{2,1,0...) async-done(((f32[1,4,1024,256]{2,3,1,0:T(8,128)}, f32[1,1024,256]{1,2,0:T(8,128)}, f32[1,1024,256]{1,2,0:T(8,128)}, f32[1,256,1024]{2,1,0:T(8,128)}, ...) | async-done | bytes 15728656 | tf_op jit(solution)/shard_map/psum | solution.py:350
  1199.8 5.5 copy.86
  1206.6 2.9 copy.88
  1209.5 60.8 %reduce-scatter.11.cloned.1.call-done = f32[480,1024]{1,0:T(8,128)} async-done(((f32[1920,1024]{1,0:T(8,128)}), f32[480,1024]{1,0:T(8,128)}) %reduce-scatter.11.cloned.1.call-update) | async-done | bytes 1966096 | tf_op jit(solution)/shard_map/reduce_scatter | solution.py:323
  1270.3 3.5 add.223
  (262 shorter events, 149.6 us)
Async XLA Ops:
  7.2 223.3 %copy-start = (bf16[1,1024,1024]{2,1,0:T(8,128)(2,1)S(1)}, bf16[1,1024,1024]{2,1,0:T(8,128)(2,1)}, u32[]{:S(2)}) copy-start(bf16[1,1024,1024]{2,1,0:T(8,128)(2,1)} %param.38) | copy-start | bytes 6291460
  7.2 38.1 %all-gather.5.cloned.1.call-start = ((), (), s32[]{:S(2)}) async-start(), calls=%async_computation.4 | async-start | bytes 4915200 | tf_op jit(solution)/shard_map/all_gather | solution.py:164
  7.9 184.6 %reduce-scatter.5.cloned.1.call-start = ((), (), s32[]{:S(2)}) async-start(), calls=%async_computation.5 | async-start | bytes 9830400 | tf_op jit(solution)/shard_map/reduce_scatter | solution.py:192
  10.8 65.6 %copy-start.28 = (pred[3,640]{1,0:T(4,128)(4,1)}, pred[3,640]{1,0:T(4,128)(4,1)S(1)}, u32[]{:S(2)}) copy-start(pred[3,640]{1,0:T(4,128)(4,1)S(1)} %broadcast_compare_fusion.2) | copy-start | bytes 5764
  79.7 5.5 copy-start.25
  79.7 5.5 copy-start.27
  123.4 69.2 %copy-start.41 = (f32[1,1024]{1,0:T(1,128)S(1)}, f32[1,1024]{1,0:T(1,128)}, u32[]{:S(2)}) copy-start(f32[1,1024]{1,0:T(1,128)} %param.35) | copy-start | bytes 12292
  123.4 72.6 %copy-start.26 = (f32[1,1024]{1,0:T(1,128)S(1)}, f32[1,1024]{1,0:T(1,128)}, u32[]{:S(2)}) copy-start(f32[1,1024]{1,0:T(1,128)} %param.36) | copy-start | bytes 12292
  123.4 72.6 %copy-start.36 = (f32[1,1024]{1,0:T(1,128)S(1)}, f32[1,1024]{1,0:T(1,128)}, u32[]{:S(2)}) copy-start(f32[1,1024]{1,0:T(1,128)} %param.37) | copy-start | bytes 12292
  123.4 107.1 %all-gather.7.cloned.1.call-start = ((), (), s32[]{:S(2)}) async-start(), calls=%async_computation.6 | async-start | bytes 4915200 | tf_op jit(solution)/shard_map/all_gather | solution.py:200
  194.7 2.7 copy-start.39
  197.4 134.3 %reduce-scatter.7.cloned.1.call-start = ((), (), s32[]{:S(2)}) async-start(), calls=%async_computation.7 | async-start | bytes 9830400 | tf_op jit(solution)/shard_map/reduce_scatter | solution.py:206
  230.5 25.7 %copy-start.46 = (bf16[1,1024,1024]{2,1,0:T(8,128)(2,1)S(1)}, bf16[1,1024,1024]{2,1,0:T(8,128)(2,1)}, u32[]{:S(2)}) copy-start(bf16[1,1024,1024]{2,1,0:T(8,128)(2,1)} %param.40) | copy-start | bytes 6291460
  262.5 69.2 %copy-start.42 = (f32[1,1024]{1,0:T(1,128)S(1)}, f32[1,1024]{1,0:T(1,128)}, u32[]{:S(2)}) copy-start(f32[1,1024]{1,0:T(1,128)} %param.41) | copy-start | bytes 12292
  262.5 112.2 %all-gather.9.cloned.1.call-start = ((), (), s32[]{:S(2)}) async-start(), calls=%async_computation.8 | async-start | bytes 4915200 | tf_op jit(solution)/shard_map/all_gather | solution.py:259
  331.7 3.3 copy-start.11
  331.7 3.3 copy-start.32
  341.5 124.4 %reduce-scatter.9.cloned.1.call-start = ((), (), s32[]{:S(2)}) async-start(), calls=%async_computation.9 | async-start | bytes 9830400 | tf_op jit(solution)/shard_map/reduce_scatter | solution.py:268
  396.7 69.2 %copy-start.4 = (f32[480,1024]{1,0:T(8,128)S(1)}, f32[480,1024]{1,0:T(8,128)}, u32[]{:S(2)}) copy-start(f32[480,1024]{1,0:T(8,128)} %copy-done.3) | copy-start | bytes 5898244
  396.8 109.6 %all-gather.11.cloned.1.call-start = ((), (), s32[]{:S(2)}) async-start(), calls=%async_computation.10 | async-start | bytes 4915200 | tf_op jit(solution)/shard_map/all_gather | solution.py:275
  469.7 3.7 copy-start.29
  473.3 726.5 %all-reduce.5.cloned.1.call-start = ((), (), s32[]{:S(2)}) async-start(), calls=%async_computation.12 | async-start | bytes 31457280 | tf_op jit(solution)/shard_map/psum | solution.py:350
  473.4 10.1 copy-start.45
  473.4 10.0 copy-start.50
  483.4 23.0 %copy-start.23 = (bf16[1,256,1024]{2,1,0:T(8,128)(2,1)S(1)}, bf16[1,256,1024]{2,1,0:T(8,128)(2,1)}, u32[]{:S(2)}) copy-start(bf16[1,256,1024]{2,1,0:T(8,128)(2,1)} %param.34) | copy-start | bytes 1572868
  524.9 2.7 copy-start.2
  584.1 2.7 copy-start.2
  643.4 2.7 copy-start.2
  693.3 4.3 copy-start.8
  695.1 2.7 copy-start.44
  697.8 8.1 copy-start.12
  697.8 8.1 copy-start.14
  697.8 8.1 copy-start.17
  697.8 3.6 copy-start.43
  700.1 3.5 copy-start.19
  712.0 2.5 copy-start.13
  712.0 558.4 %reduce-scatter.11.cloned.1.call-start = ((), (), s32[]{:S(2)}) async-start(), calls=%async_computation.11 | async-start | bytes 9830400 | tf_op jit(solution)/shard_map/reduce_scatter | solution.py:323
  712.1 2.6 copy-start.47
  714.6 4.4 copy-start.20
  714.6 4.4 copy-start.24
  723.5 49.7 %copy-start.16 = (bf16[1,1920,256]{2,1,0:T(8,128)(2,1)S(1)}, bf16[1,1920,256]{2,1,0:T(8,128)(2,1)}, u32[]{:S(2)}) copy-start(bf16[1,1920,256]{2,1,0:T(8,128)(2,1)} %copy-done.14) | copy-start | bytes 2949124
  723.5 51.3 %copy-start.40 = (f32[1024]{0:T(1024)S(1)}, f32[1024]{0:T(1024)}, u32[]{:S(2)}) copy-start(f32[1024]{0:T(1024)} %get-tuple-element.325) | copy-start | bytes 12292
  1199.8 5.5 copy-start.22
  1205.2 65.1 %copy-start.6 = (f32[480,1024]{1,0:T(8,128)S(1)}, f32[480,1024]{1,0:T(8,128)}, u32[]{:S(2)}) copy-start(f32[480,1024]{1,0:T(8,128)} %copy-done.5) | copy-start | bytes 5898244
  1206.6 67.3 %copy-start.21 = (f32[1,256,1024]{2,1,0:T(8,128)S(1)}, f32[1,256,1024]{2,1,0:T(8,128)}, u32[]{:S(2)}) copy-start(f32[1,256,1024]{2,1,0:T(8,128)} %get-tuple-element.563) | copy-start | bytes 3145732
  1270.3 4.5 copy-start.10
  1274.8 3.7 copy-start.9
  1274.8 5.7 copy-start.1
  (14 other events, 18.8 us)
Sparse Core Ops, SparseCore 0:
  9.6 35.6 all-gather.4
  123.5 68.9 reduce-scatter.4
  197.5 32.9 all-gather.6
  262.6 68.9 reduce-scatter.6
  341.7 32.9 all-gather.8
  396.9 68.9 reduce-scatter.8
  473.4 32.9 all-gather.10
  712.1 487.6 all-reduce.4
  1202.5 67.8 reduce-scatter.10
where the time goes:
time: 1300 us; the launch traced here: 1290 us
  waiting for transfers between devices  773 us (59%)
  matrix products  282 us (22%)
  local copies, waits for them, and re-layouts  92.3 us (7%)
  blocking collectives  84.2 us (6%)
  other arithmetic  39.5 us (3%)
  between operations  14.5 us (1%)
    psum x1, waiting for transfers between devices, body(): lax.psum((stacked_weights[0], stacked_weights[1], stacked_weights[2], sta...  387 us
    reduce_scatter x1, waiting for transfers between devices, body(): lax.psum_scatter(product_right_t(expand_delta, expand_proj), 'tensor', sc...  69.1 us
    reduce_scatter x1, waiting for transfers between devices, body(): lax.psum_scatter(product(activated, contract_proj), 'tensor', scatter_dim...  69.1 us
    reduce_scatter x1, waiting for transfers between devices, body(): lax.psum_scatter(product(context, out_proj), 'tensor', scatter_dimension=...  69.1 us
    reduce_scatter x1, waiting for transfers between devices, body(): lax.psum_scatter(partial_sum + product_right_t(value_delta, value_proj),...  60.8 us
    psum x1, blocking collectives, body(): lax.psum((stacked_norms[0], stacked_norms[1], stacked_norms[2], stacked_n...  46.1 us
    dot_general x5, matrix products, product(): return jnp.dot(left_side, right_side, preferred_element_type=jnp.float32)  44.4 us
    psum x1, blocking collectives, body(): lax.psum((stacked_weights[0], stacked_weights[1], stacked_weights[2], sta...  38.2 us
  transfers between devices with their start and end apart: 9, of which 9 were waited for; matrix products, arithmetic and copies ran while one was open for 3% of the time, Pallas kernels for 0%

commit v1 on v0

v1 whole, which is shorter than its diff:
```python
import functools

import jax
import jax.numpy as jnp
import numpy as np
from jax import lax
from jax.experimental import pallas as pl
from jax.experimental.pallas import tpu as pltpu
from jax.sharding import PartitionSpec as P

HD = 64
NORM_EPS = 1e-05
MASKED = -1e30
F32 = jnp.float32
BF16 = jnp.bfloat16
VMEM_LIMIT = 48 * 1024 * 1024


def nn(a, b):
    return lax.dot_general(a, b, (((1,), (0,)), ((), ())), preferred_element_type=F32)


def nt(a, b):
    return lax.dot_general(a, b, (((1,), (1,)), ((), ())), preferred_element_type=F32)


def tn(a, b):
    return lax.dot_general(a, b, (((0,), (0,)), ((), ())), preferred_element_type=F32)


def call(body, name, *, grid=(1,), prefetch=(), ins, outs, aliases=None, scratch=(), flops=0, moved=0):
    def spec(block, index_map):
        if block is None:
            return pl.BlockSpec(memory_space=pl.ANY)
        return pl.BlockSpec(block, index_map)

    in_specs = [spec(block, index_map) for _, block, index_map in ins]
    out_specs = [spec(block, index_map) for _, _, block, index_map in outs]
    shift = len(prefetch)
    return pl.pallas_call(
        body,
        grid_spec=pltpu.PrefetchScalarGridSpec(
            num_scalar_prefetch=shift,
            grid=grid,
            in_specs=in_specs,
            out_specs=out_specs,
            scratch_shapes=list(scratch),
        ),
        out_shape=[jax.ShapeDtypeStruct(shape, dtype) for shape, dtype, _, _ in outs],
        input_output_aliases={shift + k: v for k, v in (aliases or {}).items()},
        compiler_params=pltpu.CompilerParams(vmem_limit_bytes=VMEM_LIMIT),
        cost_estimate=pl.CostEstimate(flops=flops, bytes_accessed=moved, transcendentals=0),
        name=name,
    )(*prefetch, *[array for array, _, _ in ins])


def whole(array):
    zeros = (0,) * array.ndim
    return (array, array.shape, lambda *_: zeros)


def out_whole(shape, dtype):
    zeros = (0,) * len(shape)
    return (shape, dtype, shape, lambda *_: zeros)


def swap(array, axis, size, bit):
    return lax.ppermute(array, axis, [(r, r ^ bit) for r in range(size)])


def gather_blocks(own, size):
    blocks = {0: own}
    bit = 2
    while bit < size:
        for j in sorted(blocks):
            blocks[j | bit] = swap(blocks[j], "tensor", size, bit)
        bit *= 2
    for j in sorted(blocks):
        blocks[j | 1] = swap(blocks[j], "tensor", size, 1)
    return [blocks[j] for j in range(size)]


def scatter_sum(send, keeps, size):
    received = swap(send, "tensor", size, 1)
    addends = [keeps[0][None], received]
    held = {
        2 * m: (keeps[m].astype(F32) + received[m].astype(F32)).astype(BF16)
        for m in range(1, len(keeps))
    }
    bit = size // 2
    while bit >= 2:
        leaving = sorted(j for j in held if j & bit)
        arrived = swap(jnp.stack([held[j] for j in leaving]), "tensor", size, bit)
        addends.append(arrived)
        for m, j in enumerate(leaving):
            if j ^ bit:
                rest = j ^ bit
                held[rest] = (held[rest].astype(F32) + arrived[m].astype(F32)).astype(BF16)
            del held[j]
        bit //= 2
    return addends


def addend_specs(addends):
    return [(a, (1,) + a.shape[1:], lambda *_: (0, 0, 0)) for a in addends]


def place(state, shapes, piece, layout, name):
    array, places = piece
    count = places.shape[0]
    rows = array.shape[0] // count

    def body(places_ref, in_ref, *refs):
        out_refs = refs[-len(layout) :]
        for (_, _, leads, start, wide), out_ref in zip(layout, out_refs, strict=True):
            for lead in range(leads):
                at = start + lead * wide
                out_ref[lead] = in_ref[:, at : at + wide].astype(F32)

    ins = [(array, (rows, array.shape[1]), lambda m, spots: (m, 0))]
    outs, aliases = [], {}
    for number, (out, first, leads, _, wide) in enumerate(layout):
        index_map = functools.partial(lambda lead, m, spots: (lead, spots[m], 0), first // leads)
        outs.append((shapes[out], F32, (leads, rows, wide), index_map))
        if out in state:
            aliases[len(ins)] = number
            ins.append((state[out], None, None))
    got = call(
        body, name, grid=(count,), prefetch=(places,), ins=ins, outs=outs, aliases=aliases, moved=array.size * 6
    )
    return {**state, **{entry[0]: value for entry, value in zip(layout, got, strict=True)}}


def sum_over_dp(array, order, size):
    if array.shape[0] % (16 * size):
        return [(lax.psum(array, "dp"), jnp.zeros((1,), jnp.int32))]
    here = lax.axis_index("dp")
    bits = len(order)
    mine = [(here >> bit) & 1 for bit in order]
    current = array
    for bit, own in zip(order, mine, strict=True):
        half = current.shape[0] // 2
        leaving = lax.dynamic_slice_in_dim(current, (1 - own) * half, half, 0)
        staying = lax.dynamic_slice_in_dim(current, own * half, half, 0)
        arrived = swap(leaving, "dp", size, 1 << bit)
        current = (staying.astype(F32) + arrived.astype(F32)).astype(BF16)

    def where(differs):
        spot = 0
        for level in range(bits):
            spot = spot * 2 + (mine[level] ^ ((differs >> level) & 1))
        return spot

    held = [0]
    pieces = [(current, jnp.stack([where(0)]).astype(jnp.int32))]
    for level in reversed(range(bits)):
        arrived = swap(current, "dp", size, 1 << order[level])
        came = [differs | (1 << level) for differs in held]
        pieces.append((arrived, jnp.stack([where(d) for d in came]).astype(jnp.int32)))
        held = held + came
        if level:
            current = jnp.concatenate([current, arrived], axis=0)
    return pieces


def doubling_sum(array, axis, size):
    bit = 1
    while bit < size:
        array = array + swap(array, axis, size, bit)
        bit *= 2
    return array


def piece_rounds(count, size):
    left = {}
    for g in range(count * size):
        left.setdefault((g // count, g % size), []).append(g)
    rounds = []
    for _ in range(count):
        match = {}

        def augment(u, seen):
            for v in range(size):
                if left.get((u, v)) and v not in seen:
                    seen.add(v)
                    if v not in match or augment(match[v], seen):
                        match[v] = u
                        return True
            return False

        for bit in range(size):
            if all(left.get((u, u ^ bit)) for u in range(size)):
                match.update({u ^ bit: u for u in range(size)})
                break
        else:
            for u in range(size):
                augment(u, set())
        chosen = {u: (v, left[(u, v)].pop(0)) for v, u in match.items()}
        rounds.append([chosen[u] for u in range(size)])
    return rounds


def erf_parts(u):
    size = jnp.abs(u) * np.float32(0.7071067811865476)
    bell = jnp.exp(-(size * size))
    t = pl.reciprocal(1.0 + np.float32(0.3275911) * size)
    poly = np.float32(1.061405429 * 0.5)
    for c in (-1.453152027, 1.421413741, -0.284496736, 0.254829592):
        poly = poly * t + np.float32(c * 0.5)
    tail = poly * t * bell
    return jnp.where(u < 0, tail, 1.0 - tail), bell * np.float32(0.3989422804014327)


def write_rows(values, send_ref, keep_refs, size, rows):
    for j in range(size):
        block = values[j * rows : (j + 1) * rows].astype(BF16)
        if j & 1:
            send_ref[j // 2] = block
        else:
            keep_refs[j // 2][...] = block


def partial_outs(size, rows, width):
    outs = [out_whole((size // 2, rows, width), BF16)]
    return outs + [out_whole((rows, width), BF16) for _ in range(size // 2)]


def project_rows(blocks, kinds_col, weights, biases, buffers, k, count):
    size = len(blocks)
    rows, d = blocks[0].shape
    width = weights[1].shape[1]

    def body(*refs):
        x_refs = refs[:size]
        kind_ref, qw_ref, kw_ref, vw_ref, b_ref = refs[size : size + 5]
        out_ref, x_out = refs[-2:]
        x = jnp.concatenate([r[...] for r in x_refs], axis=0)
        for j in range(size):
            x_out[j] = x_refs[j][...]
        word = jnp.broadcast_to(kind_ref[0], (size * rows, width)) == 0
        bias = [b_ref[m : m + 1, :] for m in range(6)]
        for part, (first, second) in enumerate(((0, 2), (1, 3))):
            one = nn(x, qw_ref[first]) + bias[first]
            two = nn(x, qw_ref[second]) + bias[second]
            both = jnp.where(word, one, two).astype(BF16)
            for j in range(size):
                out_ref[j, :, part * width : (part + 1) * width] = both[j * rows : (j + 1) * rows]
        for part, ref, m in ((2, kw_ref, 4), (3, vw_ref, 5)):
            both = (nn(x, ref[...]) + bias[m]).astype(BF16)
            for j in range(size):
                out_ref[j, :, part * width : (part + 1) * width] = both[j * rows : (j + 1) * rows]

    ins = [whole(b) for b in blocks]
    ins.append((kinds_col, (1,) + kinds_col.shape[1:], lambda *_: (k, 0, 0)))
    ins += [whole(w) for w in weights] + [whole(biases)]
    aliases = {}
    if buffers is not None:
        for number, b in enumerate(buffers):
            aliases[len(ins)] = number
            ins.append((b, None, None))
    outs = [
        ((count * size, rows, 4 * width), BF16, (size, rows, 4 * width), lambda *_: (k, 0, 0)),
        ((count * size, rows, d), BF16, (size, rows, d), lambda *_: (k, 0, 0)),
    ]
    return call(
        body, "project_rows", ins=ins, outs=outs, aliases=aliases,
        flops=2 * size * rows * d * 6 * width, moved=size * rows * d * 6 + 12 * d * width,
    )


def head_views(piece_refs, part, pair, width):
    start = part * width + pair * 128
    return jnp.concatenate([r[0, :, start : start + 128] for r in piece_refs], axis=0)


def swap_lanes(values):
    return pltpu.roll(values.astype(F32), 64, 1)


def extended(piece_refs, pair, width, kind, left):
    qw = head_views(piece_refs, 0, pair, width)
    qe = head_views(piece_refs, 1, pair, width)
    k = head_views(piece_refs, 2, pair, width)
    v = head_views(piece_refs, 3, pair, width)
    qw32, qe32, k32 = qw.astype(F32), qe.astype(F32), k.astype(F32) * 0.125
    qw_s, qe_s, k_s = swap_lanes(qw32), swap_lanes(qe32), swap_lanes(k32)
    q_ext = (
        jnp.where(left, qw32, qe_s).astype(BF16),
        jnp.where(left, qw_s, qe32).astype(BF16),
    )
    takes = (kind + left.astype(jnp.int32)) == 1
    k_ext = (
        jnp.where(takes, jnp.where(left, k32, k_s), 0.0).astype(BF16),
        jnp.where(takes, jnp.where(left, k_s, k32), 0.0).astype(BF16),
    )
    return q_ext, k_ext, v


def query_blocks(length):
    spans, at = [], 0
    while at < length:
        step = 256 if length - at >= 256 else length - at
        spans.append((at, step))
        at += step
    return spans


def attend(pieces, table, s, seg_col, seg_row, kind_col, out_proj, size, rows):
    length = size * rows
    width, d = out_proj.shape
    pairs = width // 128

    def body(table_ref, *refs):
        piece_refs = refs[:size]
        segc_ref, segr_ref, kind_ref, wo_ref, c_ref, lse_ref, send_ref = refs[size : size + 7]
        keep_refs = refs[size + 7 :]
        left = lax.broadcasted_iota(jnp.int32, (length, 128), 1) < 64
        kind = jnp.broadcast_to(kind_ref[0], (length, 128))
        segc, segr = segc_ref[0], segr_ref[0]
        for pair in range(pairs):
            q_ext, k_ext, v = extended(piece_refs, pair, width, kind, left)
            v_t = v.astype(F32).T.astype(BF16)
            for at, step in query_blocks(length):
                same = segc == segr[:, at : at + step]
                tops = []
                for h in range(2):
                    s_t = nt(k_ext[h], q_ext[h][at : at + step])
                    s_t = jnp.where(same, s_t, MASKED)
                    top = jnp.max(s_t, axis=0, keepdims=True)
                    e = jnp.exp(s_t - top)
                    total = jnp.sum(e, axis=0, keepdims=True)
                    o_t = nn(v_t[h * 64 : h * 64 + 64], e.astype(BF16))
                    tops.append(o_t * (1.0 / total))
                    lse_ref[2 * pair + h : 2 * pair + h + 1, at : at + step] = top + jnp.log(total)
                c = jnp.concatenate(tops, axis=0).T.astype(BF16)
                c_ref[at : at + step, pair * 128 : pair * 128 + 128] = c
        write_rows(nn(c_ref[...], wo_ref[...]), send_ref, keep_refs, size, rows)

    ins = [
        (pieces, (1, rows, 4 * width), functools.partial(lambda j, _, t: (t[s * size + j], 0, 0), j))
        for j in range(size)
    ]
    ins += [
        (seg_col, (1, length, 1), lambda *_: (s, 0, 0)),
        (seg_row, (1, 1, length), lambda *_: (s, 0, 0)),
        (kind_col, (1, length, 1), lambda *_: (s, 0, 0)),
        whole(out_proj),
    ]
    outs = [out_whole((length, width), BF16), out_whole((8, length), F32)]
    outs += partial_outs(size, rows, d)
    return call(
        body, "attend", prefetch=(table,), ins=ins, outs=outs,
        flops=pairs * 2 * length * length * 1024 + 2 * length * width * d, moved=length * (5 * width + d) * 2,
    )


def attend_back(pieces, table, s, seg_col, seg_row, kind_col, out_proj, context, lse, delta_blocks, buffers, sums, count):
    size = len(delta_blocks)
    rows, d = delta_blocks[0].shape
    length = size * rows
    width = out_proj.shape[0]
    pairs = width // 128

    def body(table_ref, *refs):
        piece_refs = refs[:size]
        delta_refs = refs[size : 2 * size]
        segc_ref, segr_ref, kind_ref, wo_ref, c_ref, lse_ref = refs[2 * size : 2 * size + 6]
        n_out = 5
        tail = refs[2 * size + 6 :]
        sum_in = tail[0] if sums is not None else None
        first_out, second_out, delta_out, wo_grad, bias_out, first_all, second_all = tail[-(n_out + 2) :]
        step_at = pl.program_id(0)

        @pl.when(step_at == 0)
        def _():
            left = lax.broadcasted_iota(jnp.int32, (length, 128), 1) < 64
            kind = jnp.broadcast_to(kind_ref[0], (length, 128))
            word = kind == 0
            straight = (kind + left.astype(jnp.int32)) == 1
            segc, segr = segc_ref[0], segr_ref[0]
            delta = jnp.concatenate([r[...] for r in delta_refs], axis=0)
            c_all = c_ref[...]
            grad = nn(c_all.astype(F32).T.astype(BF16), delta)
            wo_grad[...] = grad if sum_in is None else grad + sum_in[...]
            for pair in range(pairs):
                dc = nt(delta, wo_ref[pair * 128 : pair * 128 + 128, :]).astype(BF16)
                q_ext, k_ext, v = extended(piece_refs, pair, width, kind, left)
                k_ext_t = [k.astype(F32).T.astype(BF16) for k in k_ext]
                dc32 = dc.astype(F32)
                inner = (dc32 * c_all[:, pair * 128 : pair * 128 + 128].astype(F32)).T
                dc_h = (jnp.where(left, dc32, 0.0).astype(BF16), jnp.where(left, 0.0, dc32).astype(BF16))
                dv = jnp.zeros((length, 128), F32)
                dk = [jnp.zeros((length, 128), F32)] * 2
                dq = [[], []]
                for at, step in query_blocks(length):
                    same = segc == segr[:, at : at + step]
                    for h in range(2):
                        q_b, dc_b = q_ext[h][at : at + step], dc_h[h][at : at + step]
                        row = 2 * pair + h
                        s_t = nt(k_ext[h], q_b)
                        p = jnp.where(same, jnp.exp(s_t - lse_ref[row : row + 1, at : at + step]), 0.0)
                        dp = nt(v, dc_b)
                        row_inner = jnp.sum(inner[h * 64 : h * 64 + 64, at : at + step], axis=0, keepdims=True)
                        ds = (p * (dp - row_inner)).astype(BF16)
                        dv = dv + nn(p.astype(BF16), dc_b)
                        dk[h] = dk[h] + nn(ds, q_b)
                        dq[h].append(nn(k_ext_t[h], ds).T)
                dq0, dq1 = (jnp.concatenate(parts, axis=0) for parts in dq)
                dqw = jnp.where(left, dq0, swap_lanes(dq1))
                dqe = jnp.where(left, swap_lanes(dq0), dq1)
                dk0, dk1 = dk[0] * 0.125, dk[1] * 0.125
                dk_pair = jnp.where(straight, jnp.where(left, dk0, dk1), jnp.where(left, swap_lanes(dk0), swap_lanes(dk1)))
                outs = (
                    jnp.where(word, dqw, 0.0), jnp.where(word, dqe, 0.0), jnp.where(word, 0.0, dqw),
                    jnp.where(word, 0.0, dqe), dk_pair, dv,
                )
                for number, values in enumerate(outs):
                    rounded = values.astype(BF16)
                    target = (first_all, second_all)[number // 3]
                    start = (number % 3) * width + pair * 128
                    target[:, start : start + 128] = rounded
                    bias_out[number : number + 1, pair * 128 : pair * 128 + 128] = jnp.sum(
                        rounded.astype(F32), axis=0, keepdims=True
                    )

        at_rows = pl.ds(pl.multiple_of(step_at * rows, 16), rows)
        first_out[0] = first_all[at_rows, :]
        second_out[0] = second_all[at_rows, :]
        for j in range(size):

            @pl.when(step_at == j)
            def _():
                delta_out[0] = delta_refs[j][...]

    ins = [
        (pieces, (1, rows, 4 * width), functools.partial(lambda j, _, t: (t[s * size + j], 0, 0), j))
        for j in range(size)
    ]
    ins += [whole(b) for b in delta_blocks]
    ins += [
        (seg_col, (1, length, 1), lambda *_: (s, 0, 0)),
        (seg_row, (1, 1, length), lambda *_: (s, 0, 0)),
        (kind_col, (1, length, 1), lambda *_: (s, 0, 0)),
        whole(out_proj),
        whole(context),
        whole(lse),
    ]
    if sums is not None:
        ins.append(whole(sums))
    aliases = {}
    if buffers is not None:
        for number, b in enumerate(buffers):
            aliases[len(ins)] = number
            ins.append((b, None, None))
    spot = lambda m, t: (t[s * size + m], 0, 0)
    outs = [
        ((count * size, rows, 3 * width), BF16, (1, rows, 3 * width), spot),
        ((count * size, rows, 3 * width), BF16, (1, rows, 3 * width), spot),
        ((count * size, rows, d), BF16, (1, rows, d), spot),
        out_whole((width, d), F32),
        out_whole((8, width), F32),
    ]
    return call(
        body, "attend_back", grid=(size,), prefetch=(table,), ins=ins, outs=outs, aliases=aliases,
        scratch=[pltpu.VMEM((length, 3 * width), BF16)] * 2,
        flops=pairs * 2 * length * length * 128 * 10 + 4 * length * width * d, moved=length * (11 * width + 2 * d) * 2,
    )


def add_up(refs):
    total = refs[0][0].astype(F32)
    for r in refs[1:]:
        total = total + r[0].astype(F32)
    return total


def normed(values):
    centre = jnp.mean(values, axis=-1, keepdims=True)
    offset = values - centre
    spread = jnp.mean(offset * offset, axis=-1, keepdims=True)
    rstd = lax.rsqrt(spread + NORM_EPS)
    return offset * rstd, rstd


def norm_pull(upstream, n, rstd, gain):
    scaled = upstream * gain
    inner = jnp.mean(scaled, axis=-1, keepdims=True)
    cross = jnp.mean(scaled * n, axis=-1, keepdims=True)
    return rstd * (scaled - inner - n * cross)


def column_sum(values):
    return jnp.sum(values, axis=0, keepdims=True)


def inner_norm(addends, x_pieces, table, s, bias, gain, shift, size):
    rows, d = addends[0].shape[1:]
    n_add = len(addends)

    def body(table_ref, *refs):
        x_ref, b_ref, g_ref, h_ref, y_ref, n_ref, rstd_ref = refs[n_add:]
        r = add_up(refs[:n_add]) + b_ref[...] + x_ref[0].astype(F32)
        n, rstd = normed(r)
        n_ref[...] = n
        rstd_ref[...] = jnp.broadcast_to(rstd, (rows, 128))
        y_ref[...] = (n * g_ref[...] + h_ref[...]).astype(BF16)

    ins = addend_specs(addends)
    ins.append((x_pieces, (1, rows, d), lambda _, t: (t[s * size], 0, 0)))
    ins += [whole(bias), whole(gain), whole(shift)]
    outs = [out_whole((rows, d), BF16), out_whole((rows, d), F32), out_whole((rows, 128), F32)]
    return call(body, "inner_norm", prefetch=(table,), ins=ins, outs=outs, flops=rows * d * 10, moved=rows * d * 14)


def outer_norm(addends, n1, inner_gain, inner_shift, bias, gain, shift, cotangents, spots, buffer, s, count):
    rows, d = addends[0].shape[1:]
    n_add = len(addends)

    def body(spots_ref, *refs):
        n1_ref, g1_ref, h1_ref, b_ref, g_ref, h_ref, e_ref = refs[n_add : n_add + 7]
        res_ref, dz_ref, dzb_ref, sums_ref = refs[-4:]
        z = add_up(refs[:n_add]) + b_ref[...] + (n1_ref[...] * g1_ref[...] + h1_ref[...])
        n, rstd = normed(z)
        res_ref[0] = n * g_ref[...] + h_ref[...]
        e = e_ref[0].astype(F32)
        dz = norm_pull(e, n, rstd, g_ref[...])
        dz_ref[...] = dz
        dzb_ref[...] = dz.astype(BF16)
        sums_ref[0:1] = column_sum(dz)
        sums_ref[1:2] = column_sum(e * n)
        sums_ref[2:3] = column_sum(e)

    ins = addend_specs(addends)
    ins += [whole(a) for a in (n1, inner_gain, inner_shift, bias, gain, shift)]
    ins.append((cotangents, (1, rows, d), lambda _, t: (t[s], 0, 0)))
    aliases = {}
    if buffer is not None:
        aliases[len(ins)] = 0
        ins.append((buffer, None, None))
    outs = [
        ((count, rows, d), F32, (1, rows, d), lambda *_: (s, 0, 0)),
        out_whole((rows, d), F32),
        out_whole((rows, d), BF16),
        out_whole((8, d), F32),
    ]
    return call(
        body, "outer_norm", prefetch=(spots,), ins=ins, outs=outs, aliases=aliases,
        flops=rows * d * 20, moved=rows * d * 22,
    )


def inner_norm_back(addends, dz, n1, rstd1, gain):
    rows, d = addends[0].shape[1:]
    n_add = len(addends)

    def body(*refs):
        dz_ref, n_ref, rstd_ref, g_ref, dr_ref, sums_ref = refs[n_add:]
        da = add_up(refs[:n_add]) + dz_ref[...]
        n = n_ref[...]
        dr = norm_pull(da, n, rstd_ref[:, 0:1], g_ref[...])
        dr_ref[...] = dr.astype(BF16)
        sums_ref[0:1] = column_sum(dr)
        sums_ref[1:2] = column_sum(da * n)
        sums_ref[2:3] = column_sum(da)

    ins = addend_specs(addends) + [whole(a) for a in (dz, n1, rstd1, gain)]
    outs = [out_whole((rows, d), BF16), out_whole((8, d), F32)]
    return call(body, "inner_norm_back", ins=ins, outs=outs, flops=rows * d * 20, moved=rows * d * 18)


def feed_forward(blocks, expand, expand_bias, contract, buffers, s, count):
    size = len(blocks)
    rows, d = blocks[0].shape
    hidden = expand.shape[1]
    length = size * rows
    tile = min(256, hidden)

    def body(*refs):
        y_refs = refs[:size]
        we_ref, be_ref, wc_ref = refs[size : size + 3]
        y_out, g_out, slope_out, send_ref = refs[-4 - size // 2 : -(size // 2)]
        keep_refs = refs[-(size // 2) :]
        y = jnp.concatenate([r[...] for r in y_refs], axis=0)
        y_out[0] = y
        for at in range(0, hidden, tile):
            cols = slice(at, at + tile)
            u = nn(y, we_ref[:, cols]) + be_ref[:, cols]
            phi_sum, phi = erf_parts(u)
            g_out[0, :, cols] = (u * phi_sum).astype(BF16)
            slope_out[0, :, cols] = (phi_sum + u * phi).astype(BF16)
        write_rows(nn(g_out[0], wc_ref[...]), send_ref, keep_refs, size, rows)

    ins = [whole(b) for b in blocks] + [whole(a) for a in (expand, expand_bias, contract)]
    aliases = {}
    if buffers is not None:
        for number, b in enumerate(buffers):
            aliases[len(ins)] = number
            ins.append((b, None, None))
    outs = [
        ((count, length, w), BF16, (1, length, w), lambda *_: (s, 0, 0)) for w in (d, hidden, hidden)
    ] + partial_outs(size, rows, d)
    return call(
        body, "feed_forward", ins=ins, outs=outs, aliases=aliases,
        flops=4 * length * d * hidden, moved=4 * d * hidden + length * (3 * d + 2 * hidden) * 2,
    )


def feed_back(blocks, expand, contract, slopes, buffers, s, count):
    size = len(blocks)
    rows, d = blocks[0].shape
    hidden = expand.shape[1]
    length = size * rows
    tile = min(256, hidden)

    def body(*refs):
        dz_refs = refs[:size]
        we_ref, wc_ref, slope_ref = refs[size : size + 3]
        sums_ref, dz_out, du_out, send_ref = refs[-4 - size // 2 : -(size // 2)]
        keep_refs = refs[-(size // 2) :]
        dz = jnp.concatenate([r[...] for r in dz_refs], axis=0)
        dz_out[0] = dz
        for at in range(0, hidden, tile):
            cols = slice(at, at + tile)
            du = (nt(dz, wc_ref[cols, :]) * slope_ref[0, :, cols].astype(F32)).astype(BF16)
            du_out[0, :, cols] = du
            sums_ref[:, cols] = column_sum(du.astype(F32))
        write_rows(nt(du_out[0], we_ref[...]), send_ref, keep_refs, size, rows)

    ins = [whole(b) for b in blocks] + [whole(expand), whole(contract)]
    ins.append((slopes, (1, length, hidden), lambda *_: (s, 0, 0)))
    aliases = {}
    if buffers is not None:
        for number, b in enumerate(buffers):
            aliases[len(ins)] = 1 + number
            ins.append((b, None, None))
    outs = [out_whole((1, hidden), F32)]
    outs += [((count, length, w), BF16, (1, length, w), lambda *_: (s, 0, 0)) for w in (d, hidden)]
    outs += partial_outs(size, rows, d)
    return call(
        body, "feed_back", ins=ins, outs=outs, aliases=aliases,
        flops=4 * length * d * hidden, moved=4 * d * hidden + length * (3 * d + 2 * hidden) * 2,
    )


def input_back(first, second, weights, k, size):
    rows = first.shape[1]
    d = weights[1].shape[0]
    width = weights[1].shape[1]

    def body(*refs):
        a_ref, b_ref, qw_ref, kw_ref, vw_ref, send_ref = refs[:6]
        keep_refs = refs[6:]
        a = jnp.concatenate([a_ref[j] for j in range(size)], axis=0)
        b = jnp.concatenate([b_ref[j] for j in range(size)], axis=0)
        total = nt(a[:, :width], qw_ref[0])
        for m in (1, 2):
            total = total + nt(a[:, m * width : (m + 1) * width], qw_ref[m])
        total = total + nt(b[:, :width], qw_ref[3])
        total = total + nt(b[:, width : 2 * width], kw_ref[...])
        total = total + nt(b[:, 2 * width :], vw_ref[...])
        write_rows(total, send_ref, keep_refs, size, rows)

    block = (size, rows, 3 * width)
    ins = [(first, block, lambda *_: (k, 0, 0)), (second, block, lambda *_: (k, 0, 0))]
    ins += [whole(w) for w in weights]
    return call(
        body, "input_back", ins=ins, outs=partial_outs(size, rows, d),
        flops=12 * size * rows * d * width, moved=size * rows * (6 * width + d) * 2 + 12 * d * width,
    )


def final_sum(addends, dr_pieces, buffer, k, count, size):
    rows, d = addends[0].shape[1:]
    n_add = len(addends)

    def body(*refs):
        refs[-1][0] = add_up(refs[: n_add + 1])

    ins = addend_specs(addends)
    ins.append((dr_pieces, (1, rows, d), lambda *_: (k * size, 0, 0)))
    aliases = {}
    if buffer is not None:
        aliases[len(ins)] = 0
        ins.append((buffer, None, None))
    outs = [((count, rows, d), F32, (1, rows, d), lambda *_: (k, 0, 0))]
    return call(body, "final_sum", ins=ins, outs=outs, aliases=aliases, flops=rows * d * 4, moved=rows * d * 12)[0]


def body(
    dp, tensor, tokens, token_kinds, segment_ids, cotangent, query_weight, query_bias, key_weight, key_bias,
    value_weight, value_bias, output_weight, output_bias, inner_gain, inner_shift, expand_weight, expand_bias,
    contract_weight, contract_bias, outer_gain, outer_shift,
):
    count, length = token_kinds.shape
    d = tokens.shape[1]
    rows = length // tensor
    me = lax.axis_index("tensor")
    width = key_weight.shape[2]
    hidden = expand_weight.shape[2]

    devices = np.arange(tensor)
    piece_at = np.array(
        [[[o * count + k for o in devices ^ r] for k in range(count)] for r in range(tensor)], np.int32
    )
    seq_piece = np.array(
        [[[s * tensor + b for b in devices ^ r] for s in range(count)] for r in range(tensor)], np.int32
    )
    table_of = np.array(
        [[(g % count) * tensor + ((g // count) ^ r) for g in seq_piece[r].reshape(-1)] for r in range(tensor)], np.int32
    )
    pick = lambda values: lax.dynamic_index_in_dim(jnp.asarray(values), me, 0, keepdims=False)
    table = pick(table_of)
    kinds = token_kinds.reshape(count * tensor, rows)
    segments = segment_ids.reshape(count * tensor, rows)
    kinds_by_piece = kinds[pick(piece_at).reshape(-1)].reshape(count, length, 1)
    seq_spots = pick(seq_piece).reshape(-1)
    kind_col = kinds[seq_spots].reshape(count, length, 1)
    seg_seq = segments[seq_spots]
    seg_col = seg_seq.reshape(count, length, 1)
    seg_row = seg_seq.reshape(count, 1, length)

    weights = (query_weight[0], key_weight[0], value_weight[0])
    biases = jnp.concatenate([query_bias[0], key_bias, value_bias], axis=0).astype(F32)

    pieces = None
    for k in range(count):
        blocks = gather_blocks(tokens[k * rows : (k + 1) * rows], tensor)
        pieces = project_rows(blocks, kinds_by_piece, weights, biases, pieces, k, count)
    qkv, x_pieces = pieces

    rounds = piece_rounds(count, tensor)
    arrived = []
    spots_of = np.zeros((tensor, count), np.int32)
    for number, chosen in enumerate(rounds):
        sends = pick(np.array([g % count for _, g in chosen], np.int32))
        block = lax.dynamic_slice_in_dim(cotangent, sends * rows, rows, 0)
        perm = [(u, v) for u, (v, _) in enumerate(chosen)]
        if any(u != v for u, v in perm):
            block = lax.ppermute(block, "tensor", perm)
        arrived.append(block)
        for v, g in chosen:
            spots_of[v, g // tensor] = number
    cotangents = jnp.stack(arrived)
    spots = pick(spots_of)

    contexts, totals, n1s, rstds, ys = [], [], [], [], []
    for s in range(count):
        context, lse, send, *keeps = attend(
            qkv, table, s, seg_col, seg_row, kind_col, output_weight[0], tensor, rows
        )
        addends = scatter_sum(send, keeps, tensor)
        y, n1, rstd1 = inner_norm(addends, x_pieces, table, s, output_bias, inner_gain, inner_shift, tensor)
        contexts.append(context)
        totals.append(lse)
        n1s.append(n1)
        rstds.append(rstd1)
        ys.append(y)

    expand, contract = expand_weight[0], contract_weight[0]
    expand_bias32 = expand_bias.astype(F32)
    kept, results, dzs, dzbs, outer_sums = None, None, [], [], []
    for s in range(count):
        blocks = gather_blocks(ys[s], tensor)
        *kept, send = (out := feed_forward(blocks, expand, expand_bias32, contract, kept, s, count))[:4]
        addends = scatter_sum(send, out[4:], tensor)
        results, dz, dzb, sums = outer_norm(
            addends, n1s[s], inner_gain, inner_shift, contract_bias, outer_gain, outer_shift, cotangents, spots,
            results, s, count,
        )
        dzs.append(dz)
        dzbs.append(dzb)
        outer_sums.append(sums)
    y_all, g_all, slopes = kept

    result = {}
    for number, chosen in enumerate(rounds):
        sends, lands = np.zeros(tensor, np.int32), np.zeros(tensor, np.int32)
        for u, (v, g) in enumerate(chosen):
            sends[v], lands[u] = g // tensor, g % count
        block = lax.dynamic_index_in_dim(results, pick(sends), 0, keepdims=False)
        perm = [(v, u) for u, (v, _) in enumerate(chosen)]
        if any(u != v for u, v in perm):
            block = lax.ppermute(block.astype(BF16), "tensor", perm)
        result = place(
            result, [(1, count * rows, d)], (block, pick(lands).reshape(1)), [(0, 0, 1, 0, d)], "place_result"
        )

    kept, drbs, inner_sums, expand_bias_sums = None, [], [], 0.0
    for s in range(count):
        blocks = gather_blocks(dzbs[s], tensor)
        sums, *kept, send = (out := feed_back(blocks, expand, contract, slopes, kept, s, count))[:4]
        expand_bias_sums = expand_bias_sums + sums
        addends = scatter_sum(send, out[4:], tensor)
        drb, sums = inner_norm_back(addends, dzs[s], n1s[s], rstds[s], inner_gain)
        drbs.append(drb)
        inner_sums.append(sums)
    dz_all, du_all = kept
    flat = lambda a: a.reshape(-1, a.shape[-1])
    bits = list(range(dp.bit_length() - 1))
    swapped = bits[1::-1] + bits[2:]
    contract_pieces = sum_over_dp(tn(flat(g_all), flat(dz_all)).astype(BF16), bits, dp)
    expand_pieces = sum_over_dp(tn(flat(y_all), flat(du_all)).astype(BF16), swapped, dp)

    kept, output_sum, bias_sums = None, None, 0.0
    for s in range(count):
        blocks = gather_blocks(drbs[s], tensor)
        *kept, output_sum, sums = attend_back(
            qkv, table, s, seg_col, seg_row, kind_col, output_weight[0], contexts[s], totals[s], blocks, kept,
            output_sum, count,
        )
        bias_sums = bias_sums + sums[:6]
    first, second, dr_pieces = kept
    output_pieces = sum_over_dp(output_sum.astype(BF16), bits, dp)

    x_flat = flat(x_pieces)
    first_pieces = sum_over_dp(tn(x_flat, flat(first)).astype(BF16), bits, dp)
    second_pieces = sum_over_dp(tn(x_flat, flat(second)).astype(BF16), swapped, dp)

    upstream = None
    for k in range(count):
        send, *keeps = input_back(first, second, weights, k, tensor)
        addends = scatter_sum(send, keeps, tensor)
        upstream = final_sum(addends, dr_pieces, upstream, k, count, tensor)

    norms = jnp.concatenate([sum(outer_sums)[:3], sum(inner_sums)[:3]], axis=0)
    norms = doubling_sum(norms, "tensor", tensor)
    top = jnp.concatenate([norms, jnp.pad(expand_bias_sums, ((0, 0), (0, d - hidden)))], axis=0)
    packed = jnp.concatenate([top, jnp.pad(bias_sums, ((0, 1), (0, 0)))], axis=1)
    packed = doubling_sum(packed, "dp", dp)

    shapes = [(4, d, width), (1, d, width), (1, d, width), (1, width, d), (1, d, hidden), (1, hidden, d)]
    grads = {}
    for piece in contract_pieces:
        grads = place(grads, shapes, piece, [(5, 0, 1, 0, d)], "place_contract")
    for piece in expand_pieces:
        grads = place(grads, shapes, piece, [(4, 0, 1, 0, hidden)], "place_expand")
    for piece in output_pieces:
        grads = place(grads, shapes, piece, [(3, 0, 1, 0, d)], "place_output")
    for one, two in zip(first_pieces, second_pieces, strict=True):
        grads = place(grads, shapes, one, [(0, 0, 3, 0, width)], "place_first")
        layout = [(0, 3, 1, 0, width), (1, 0, 1, width, width), (2, 0, 1, 2 * width, width)]
        grads = place(grads, shapes, two, layout, "place_second")

    return (
        result[0].reshape(-1, d),
        upstream.reshape(-1, d),
        grads[0][None],
        packed[None, 0:4, d:],
        grads[1],
        packed[4:5, d:],
        grads[2],
        packed[5:6, d:],
        grads[3],
        packed[3:4, :d],
        packed[4:5, :d],
        packed[5:6, :d],
        grads[4],
        packed[6:7, :hidden],
        grads[5],
        packed[0:1, :d],
        packed[1:2, :d],
        packed[2:3, :d],
    )


def solution(mesh):
    rows, both = P("dp", None), P(("dp", "tensor"), None)
    columns = lambda dims: P(*[None] * (dims - 1), "tensor")
    down = P(None, "tensor", None)
    weight_specs = [columns(4), columns(3), columns(3), columns(2), columns(3), columns(2), down]
    ffn_specs = [columns(3), columns(2), down]
    return jax.shard_map(
        functools.partial(body, mesh.shape["dp"], mesh.shape["tensor"]),
        mesh=mesh,
        in_specs=(both, rows, rows, both, *weight_specs, P(), P(), P(), *ffn_specs, P(), P(), P()),
        out_specs=(both, both, *weight_specs, P(), P(), P(), *ffn_specs, P(), P(), P()),
        check_vma=False,
    )
```

time: 1300 us -> 581 us (0.45)
  waiting for transfers between devices: 773 us -> 209 us
  matrix products: 282 us -> 22 us
  Pallas kernels: 0 us -> 175 us
  starting transfers between devices: 0.37 us -> 90.9 us
  blocking collectives: 84.2 us -> 0 us
  local copies, waits for them, and re-layouts: 92.3 us -> 46.6 us
  other arithmetic: 39.5 us -> 18.5 us
    psum x1 -> x0, waiting for transfers between devices: 387 us -> none  [body(): lax.psum((stacked_weights[0], stacked_weights[1], stacked_weights[2], sta...]
    reduce_scatter x4 -> x0, waiting for transfers between devices: 268 us -> none  [the longest x1 69.1 us: body(): lax.psum_scatter(product_right_t(expand_delta, expand_proj), 'tensor', sc...]
    dot_general x51 -> x4, matrix products: 282 us -> 22 us  [tn(): lax.dot_general(a, b, (((0,), (0,)), ((), ())), preferred_element_type=F32)]
    ppermute x0 -> x99, waiting for transfers between devices: none -> 209 us  [the longest x95 206 us: swap(): return lax.ppermute(array, axis, [(r, r ^ bit) for r in range(size)])]
    pallas_call x0 -> x53, Pallas kernels: none -> 175 us  [call(): pl.pallas_call(body, grid_spec=pltpu.PrefetchScalarGridSpec(num_scalar_pr...]
    all_gather x4 -> x0, waiting for transfers between devices: 118 us -> none  [the longest x1 34.6 us: body(): gathered_in = lax.all_gather(rounded_in, 'tensor', axis=0, tiled=True)]
    ppermute x0 -> x99, starting transfers between devices: none -> 90.9 us  [the longest x95 86.8 us: swap(): return lax.ppermute(array, axis, [(r, r ^ bit) for r in range(size)])]
    psum x2 -> x0, blocking collectives: 84.2 us -> none  [the longest x1 46.1 us: body(): lax.psum((stacked_norms[0], stacked_norms[1], stacked_norms[2], stacked_n...]
  transfers between devices with their start and end apart: 9 -> 99, of which waited for: 9 -> 38; matrix products, arithmetic and copies ran while one was open for 3% -> 11% of each run, Pallas kernels for 0% -> 28%
where the time goes in v1:
time: 581 us; the launch traced here: 571 us
  waiting for transfers between devices  209 us (36%)
  Pallas kernels  175 us (30%)
  starting transfers between devices  90.9 us (16%)
  local copies, waits for them, and re-layouts  46.6 us (8%)
  matrix products  22 us (4%)
  other arithmetic  18.5 us (3%)
  between operations  9.47 us (2%)
    ppermute x95, waiting for transfers between devices, swap(): return lax.ppermute(array, axis, [(r, r ^ bit) for r in range(size)])  206 us
    pallas_call x53, Pallas kernels, call(): pl.pallas_call(body, grid_spec=pltpu.PrefetchScalarGridSpec(num_scalar_pr...  175 us
    ppermute x95, starting transfers between devices, swap(): return lax.ppermute(array, axis, [(r, r ^ bit) for r in range(size)])  86.8 us
    unnamed x186, local copies, waits for them, and re-layouts  23.4 us
    dot_general x4, matrix products, tn(): lax.dot_general(a, b, (((0,), (0,)), ((), ())), preferred_element_type=F32)  22 us
  transfers between devices with their start and end apart: 99, of which 38 were waited for; matrix products, arithmetic and copies ran while one was open for 11% of the time, Pallas kernels for 28%

profile of v1, /device:TPU:0, one launch (start us, length us, event | category | flops | bytes accessed | tf_op | source)
XLA Modules:
  0.0 571.3 jit_solution(712884061293382606)
XLA Ops:
  9.7 5.0 collective-permute-done.7.refs_2_
  14.8 7.0 %collective-permute-done.4.refs_2_ = bf16[160,1024]{1,0:T(8,128)(2,1)} collective-permute-done((bf16[160,1024]{1,0:T(8,128)(2,1)}, bf16[160,1024]{1,0:T(8,128)(2,1)}, u32[]{:S(2)}, u32[]{:S(2)}) %collective-permute-start.4) | collective-permute-done | bytes 327712 | tf_op jit(solution)/shard_map/ppermute | solution.py:68
  33.4 5.0 project_rows.3
  38.4 5.0 project_rows.4
  43.5 4.8 project_rows.5
  48.3 7.8 %attend.5 = (bf16[640,256]{1,0:T(8,128)(2,1)S(1)}, f32[8,640]{1,0:T(8,128)S(1)}, bf16[2,160,1024]{2,1,0:T(8,128)(2,1)S(1)}, bf16[160,1024]{1,0:T(8,128)(2,1)S(1)}, bf16[160,1024]{1,0:T(8,128)(2,1)S(1)}) custom-call(s32[12]{0:T(128)S(1)} %fusion.29.table_ref, bf16[12,160,1024]{2,1,0:T(8,128)(2,1)} %get-tuple-element.142.refs_0_.refs_1_.refs_2_.refs_3_, ...), custom_call_target="tpu_custom_call" | custom-call | flops 2013265920 | bytes 2949120 | tf_op jit(solution)/shard_map/attend/pallas_call | solution.py:40
  57.3 7.6 %attend.4 = (bf16[640,256]{1,0:T(8,128)(2,1)S(1)}, f32[8,640]{1,0:T(8,128)S(1)}, bf16[2,160,1024]{2,1,0:T(8,128)(2,1)S(1)}, bf16[160,1024]{1,0:T(8,128)(2,1)S(1)}, bf16[160,1024]{1,0:T(8,128)(2,1)S(1)}) custom-call(s32[12]{0:T(128)S(1)} %fusion.29.table_ref, bf16[12,160,1024]{2,1,0:T(8,128)(2,1)} %get-tuple-element.142.refs_0_.refs_1_.refs_2_.refs_3_, ...), custom_call_target="tpu_custom_call" | custom-call | flops 2013265920 | bytes 2949120 | tf_op jit(solution)/shard_map/attend/pallas_call | solution.py:40
  66.3 7.6 %attend.3 = (bf16[640,256]{1,0:T(8,128)(2,1)S(1)}, f32[8,640]{1,0:T(8,128)S(1)}, bf16[2,160,1024]{2,1,0:T(8,128)(2,1)S(1)}, bf16[160,1024]{1,0:T(8,128)(2,1)S(1)}, bf16[160,1024]{1,0:T(8,128)(2,1)S(1)}) custom-call(s32[12]{0:T(128)S(1)} %fusion.29.table_ref, bf16[12,160,1024]{2,1,0:T(8,128)(2,1)} %get-tuple-element.142.refs_0_.refs_1_.refs_2_.refs_3_, ...), custom_call_target="tpu_custom_call" | custom-call | flops 2013265920 | bytes 2949120 | tf_op jit(solution)/shard_map/attend/pallas_call | solution.py:40
  80.6 5.4 collective-permute-done.20.refs_2_
  108.6 5.5 collective-permute-done.17.refs_2_
  116.9 4.2 collective-permute-done.12.refs_2_
  121.6 7.6 %feed_forward.3 = (bf16[3,640,1024]{2,1,0:T(8,128)(2,1)}, bf16[3,640,1024]{2,1,0:T(8,128)(2,1)}, bf16[3,640,1024]{2,1,0:T(8,128)(2,1)}, bf16[2,160,1024]{2,1,0:T...) custom-call(bf16[160,1024]{1,0:T(8,128)(2,1)} %get-tuple-element.155.refs_0_, ...), custom_call_target="tpu_custom_call" | custom-call | flops 2684354560 | bytes 10747904 | tf_op jit(solution)/shard_map/feed_forward/pallas_call | solution.py:40
  130.4 7.6 %feed_forward.4 = (bf16[3,640,1024]{2,1,0:T(8,128)(2,1)}, bf16[3,640,1024]{2,1,0:T(8,128)(2,1)}, bf16[3,640,1024]{2,1,0:T(8,128)(2,1)}, bf16[2,160,1024]{2,1,0:T...) custom-call(bf16[160,1024]{1,0:T(8,128)(2,1)} %get-tuple-element.151, ...), custom_call_target="tpu_custom_call", output_to_operand_aliasing={{0}: (7, {}), {1}: (8, {}), {2}: (9, {})} | custom-call | flops 2684354560 | bytes 10747904 | tf_op jit(solution)/shard_map/feed_forward/pallas_call | solution.py:40
  139.6 7.8 %feed_forward.5 = (bf16[3,640,1024]{2,1,0:T(8,128)(2,1)}, bf16[3,640,1024]{2,1,0:T(8,128)(2,1)}, bf16[3,640,1024]{2,1,0:T(8,128)(2,1)}, bf16[2,160,1024]{2,1,0:T...) custom-call(bf16[160,1024]{1,0:T(8,128)(2,1)S(1)} %get-tuple-element, ...), custom_call_target="tpu_custom_call", output_to_operand_aliasing={{0}: (7, {}), {1}: (8, {}), {2}: (9, {})} | custom-call | flops 2684354560 | bytes 10747904 | tf_op jit(solution)/shard_map/feed_forward/pallas_call | solution.py:40
  167.4 4.2 collective-permute-done.31.refs_2_
  192.6 7.0 %collective-permute-done.38.refs_2_ = bf16[160,1024]{1,0:T(8,128)(2,1)S(1)} collective-permute-done((bf16[160,1024]{1,0:T(8,128)(2,1)S(1)}, bf16[160,1024]{1,0:T(8,128)(2,1)S(1)}, u32[]{:S(2)}, u32[]{:S(2)}) %collective-permute-start.38) | collective-permute-done | bytes 327712 | tf_op jit(solution)/shard_map/ppermute | solution.py:68
  200.6 5.5 collective-permute-done.35.refs_2_
  209.4 4.9 feed_back.3
  215.1 4.9 feed_back.4
  220.9 6.0 %feed_back.5 = (f32[1,1024]{1,0:T(1,128)S(1)}, bf16[3,640,1024]{2,1,0:T(8,128)(2,1)}, bf16[3,640,1024]{2,1,0:T(8,128)(2,1)}, bf16[2,160,1024]{2,1,0:T(8,128)(2,1...) custom-call(bf16[160,1024]{1,0:T(8,128)(2,1)S(1)} %get-tuple-element, ...), custom_call_target="tpu_custom_call", output_to_operand_aliasing={{1}: (7, {}), {2}: (8, {})} | custom-call | flops 2684354560 | bytes 10747904 | tf_op jit(solution)/shard_map/feed_back/pallas_call | solution.py:40
  227.9 8.0 %bitcast_convert_fusion = bf16[1024,1024]{1,0:T(8,128)(2,1)S(1)} fusion(bf16[3,640,1024]{2,1,0:T(8,128)(2,1)} %get-tuple-element.256, bf16[3,640,1024]{2,1,0:T(8,128)(2,1)} %get-tuple-element.257), kind=kOutput, calls=%fused_computation.3 | convolution fusion | flops 4027580416 | bytes 9961472 | tf_op jit(solution)/shard_map/dot_general | solution.py:28
  242.7 5.0 bitcast_convert_fusion.1
  251.5 5.0 collective-permute-done.49.refs_2_
  258.6 4.9 collective-permute-done.54.refs_2_
  275.8 6.9 %collective-permute-done.87 = bf16[512,1024]{1,0:T(8,128)(2,1)} collective-permute-done((bf16[512,1024]{1,0:T(8,128)(2,1)S(1)}, bf16[512,1024]{1,0:T(8,128)(2,1)}, u32[]{:S(2)}, u32[]{:S(2)}) %collective-permute-start.87) | collective-permute-done | bytes 1048608 | tf_op jit(solution)/shard_map/ppermute | solution.py:68
  287.1 3.4 collective-permute-done.94
  291.6 3.1 collective-permute-done.51.refs_6_
  297.2 4.5 collective-permute-done.56.refs_6_
  309.4 12.1 %attend_back.3 = (bf16[12,160,768]{2,1,0:T(8,128)(2,1)}, bf16[12,160,768]{2,1,0:T(8,128)(2,1)}, bf16[12,160,1024]{2,1,0:T(8,128)(2,1)}, f32[256,1024]{1,0:T(8,128)S(1)}, f32[8,256]{1,0:T(8,128)S(1)}) custom-call(s32[12]{0:T(128)S(1)} %fusion.29.table_ref, bf16[12,160,1024]{2,1,0:T(8,128)(2,1)} %get-tuple-element.142.refs_0_.refs_1_.refs_2_.refs_3_, ...), custom_call_target="tpu_custom_call" | custom-call | flops 2768240640 | bytes 6225920 | tf_op jit(solution)/shard_map/attend_back/pallas_call | solution.py:40
  322.8 12.5 %attend_back.4 = (bf16[12,160,768]{2,1,0:T(8,128)(2,1)}, bf16[12,160,768]{2,1,0:T(8,128)(2,1)}, bf16[12,160,1024]{2,1,0:T(8,128)(2,1)}, f32[256,1024]{1,0:T(8,128)S(1)}, f32[8,256]{1,0:T(8,128)S(1)}) custom-call(s32[12]{0:T(128)S(1)} %fusion.29.table_ref, ...), custom_call_target="tpu_custom_call", output_to_operand_aliasing={{0}: (16, {}), {1}: (17, {}), {2}: (18, {})} | custom-call | flops 2768240640 | bytes 6225920 | tf_op jit(solution)/shard_map/attend_back/pallas_call | solution.py:40
  336.4 12.9 %attend_back.5 = (bf16[12,160,768]{2,1,0:T(8,128)(2,1)}, bf16[12,160,768]{2,1,0:T(8,128)(2,1)}, bf16[12,160,1024]{2,1,0:T(8,128)(2,1)}, f32[256,1024]{1,0:T(8,128)S(1)}, f32[8,256]{1,0:T(8,128)S(1)}) custom-call(s32[12]{0:T(128)S(1)} %fusion.29.table_ref, ...), custom_call_target="tpu_custom_call", output_to_operand_aliasing={{0}: (16, {}), {1}: (17, {}), {2}: (18, {})} | custom-call | flops 2768240640 | bytes 6225920 | tf_op jit(solution)/shard_map/attend_back/pallas_call | solution.py:40
  349.3 3.7 input_back.5
  353.1 3.7 input_back.4
  356.8 3.9 input_back.3
  360.7 5.5 bitcast_convert_fusion.3
  366.2 3.5 bitcast_convert_fusion.2
  386.2 3.1 collective-permute-start.96
  390.7 21.2 %collective-permute-done.82 = bf16[64,1024]{1,0:T(8,128)(2,1)S(1)} collective-permute-done((bf16[64,1024]{1,0:T(8,128)(2,1)S(1)}, bf16[64,1024]{1,0:T(8,128)(2,1)S(1)}, u32[]{:S(2)}, u32[]{:S(2)}) %collective-permute-start.82) | collective-permute-done | bytes 131104 | tf_op jit(solution)/shard_map/ppermute | solution.py:68
  415.0 14.4 %collective-permute-done.83 = bf16[32,1024]{1,0:T(8,128)(2,1)S(1)} collective-permute-done((bf16[32,1024]{1,0:T(8,128)(2,1)S(1)}, bf16[32,1024]{1,0:T(8,128)(2,1)S(1)}, u32[]{:S(2)}, u32[]{:S(2)}) %collective-permute-start.83) | collective-permute-done | bytes 65568 | tf_op jit(solution)/shard_map/ppermute | solution.py:68
  431.1 6.2 %collective-permute-done.84.in_ref = bf16[32,1024]{1,0:T(8,128)(2,1)S(1)} collective-permute-done((bf16[32,1024]{1,0:T(8,128)(2,1)S(1)}, bf16[32,1024]{1,0:T(8,128)(2,1)S(1)}, u32[]{:S(2)}, u32[]{:S(2)}) %collective-permute-start.84) | collective-permute-done | bytes 65568 | tf_op jit(solution)/shard_map/ppermute | solution.py:68
  438.4 11.5 %collective-permute-done.70 = bf16[512,768]{1,0:T(8,128)(2,1)S(1)} collective-permute-done((bf16[512,768]{1,0:T(8,128)(2,1)S(1)}, bf16[512,768]{1,0:T(8,128)(2,1)S(1)}, u32[]{:S(2)}, u32[]{:S(2)}) %collective-permute-start.70) | collective-permute-done | bytes 786464 | tf_op jit(solution)/shard_map/ppermute | solution.py:68
  452.5 15.1 %collective-permute-done.65 = bf16[256,768]{1,0:T(8,128)(2,1)S(1)} collective-permute-done((bf16[256,768]{1,0:T(8,128)(2,1)S(1)}, bf16[256,768]{1,0:T(8,128)(2,1)S(1)}, u32[]{:S(2)}, u32[]{:S(2)}) %collective-permute-start.65) | collective-permute-done | bytes 393248 | tf_op jit(solution)/shard_map/ppermute | solution.py:68
  469.4 3.4 collective-permute-start.66
  473.0 8.0 %collective-permute-done.66 = bf16[128,768]{1,0:T(8,128)(2,1)S(1)} collective-permute-done((bf16[128,768]{1,0:T(8,128)(2,1)S(1)}, bf16[128,768]{1,0:T(8,128)(2,1)S(1)}, u32[]{:S(2)}, u32[]{:S(2)}) %collective-permute-start.66) | collective-permute-done | bytes 196640 | tf_op jit(solution)/shard_map/ppermute | solution.py:68
  481.1 10.4 %collective-permute-done.72 = bf16[128,768]{1,0:T(8,128)(2,1)S(1)} collective-permute-done((bf16[128,768]{1,0:T(8,128)(2,1)S(1)}, bf16[128,768]{1,0:T(8,128)(2,1)S(1)}, u32[]{:S(2)}, u32[]{:S(2)}) %collective-permute-start.72) | collective-permute-done | bytes 196640 | tf_op jit(solution)/shard_map/ppermute | solution.py:68
  494.6 11.9 %collective-permute-done.67.in_ref = bf16[128,768]{1,0:T(8,128)(2,1)S(1)} collective-permute-done((bf16[128,768]{1,0:T(8,128)(2,1)S(1)}, bf16[128,768]{1,0:T(8,128)(2,1)S(1)}, u32[]{:S(2)}, u32[]{:S(2)}) %collective-permute-start.67) | collective-permute-done | bytes 196640 | tf_op jit(solution)/shard_map/ppermute | solution.py:68
  514.0 8.6 %collective-permute-done.68.in_ref = bf16[256,768]{1,0:T(8,128)(2,1)S(1)} collective-permute-done((bf16[256,768]{1,0:T(8,128)(2,1)S(1)}, bf16[256,768]{1,0:T(8,128)(2,1)S(1)}, u32[]{:S(2)}, u32[]{:S(2)}) %collective-permute-start.68) | collective-permute-done | bytes 393248 | tf_op jit(solution)/shard_map/ppermute | solution.py:68
  562.1 4.5 collective-permute-done.75.in_ref
  (494 shorter events, 224.2 us)
Async XLA Ops:
  5.9 23.6 %collective-permute-start.6 = (bf16[160,1024]{1,0:T(8,128)(2,1)}, bf16[160,1024]{1,0:T(8,128)(2,1)}, u32[]{:S(2)}, u32[]{:S(2)}) collective-permute-start(bf16[160,1024]{1,0:T(8,128)(2,1)} %get-tuple-element.263.refs_0_), channel_id=1, source_target_pairs={{0,1},{1,0},{2,3},{3,2},{4,5},{5,4},{6,7},{7,6},{8,9},{9,8},{10,11... | collective-permute-start | bytes 983048 | tf_op jit(solution)/shard_map/ppermute | solution.py:68
  6.0 32.4 %collective-permute-start.3 = (bf16[160,1024]{1,0:T(8,128)(2,1)}, bf16[160,1024]{1,0:T(8,128)(2,1)}, u32[]{:S(2)}, u32[]{:S(2)}) collective-permute-start(bf16[160,1024]{1,0:T(8,128)(2,1)} %get-tuple-element.265.refs_0_), channel_id=1, source_target_pairs={{0,1},{1,0},{2,3},{3,2},{4,5},{5,4},{6,7},{7,6},{8,9},{9,8},{10,11... | collective-permute-start | bytes 983048 | tf_op jit(solution)/shard_map/ppermute | solution.py:68
  6.4 23.6 %collective-permute-start.1 = (bf16[160,1024]{1,0:T(8,128)(2,1)S(1)}, bf16[160,1024]{1,0:T(8,128)(2,1)}, u32[]{:S(2)}, u32[]{:S(2)}) collective-permute-start(bf16[160,1024]{1,0:T(8,128)(2,1)S(1)} %get-tuple-element.264.refs_0_), channel_id=1, source_target_pairs={{0,2},{1,3},{2,0},{3,1},{4,6},{5,7},{6,4},{7,5},{8,10},{9,11},{10,... | collective-permute-start | bytes 983048 | tf_op jit(solution)/shard_map/ppermute | solution.py:68
  56.8 18.3 %collective-permute-start.19 = (bf16[2,160,1024]{2,1,0:T(8,128)(2,1)S(1)}, bf16[2,160,1024]{2,1,0:T(8,128)(2,1)S(1)}, u32[]{:S(2)}, u32[]{:S(2)}) collective-permute-start(bf16[2,160,1024]{2,1,0:T(8,128)(2,1)S(1)} %get-tuple-element.153), channel_id=1, source_target_pairs={{0,1},{1,0},{2,3},{3,2},{4,5},{5,4},{6,7},{7,6},{8,9},{9,8},{10,11... | collective-permute-start | bytes 1966088 | tf_op jit(solution)/shard_map/ppermute | solution.py:68
  78.6 23.2 %collective-permute-start.10 = (bf16[1,160,1024]{2,1,0:T(8,128)(2,1)}, bf16[1,160,1024]{2,1,0:T(8,128)(2,1)}, u32[]{:S(2)}, u32[]{:S(2)}) collective-permute-start(bf16[1,160,1024]{2,1,0:T(8,128)(2,1)} %fusion.14), channel_id=1, source_target_pairs={{0,2},{1,3},{2,0},{3,1},{4,6},{5,7},{6,4},{7,5},{8,10},{9,11},{10,... | collective-permute-start | bytes 983048 | tf_op jit(solution)/shard_map/ppermute | solution.py:68
  108.1 21.8 %collective-permute-start.16 = (bf16[160,1024]{1,0:T(8,128)(2,1)}, bf16[160,1024]{1,0:T(8,128)(2,1)S(1)}, u32[]{:S(2)}, u32[]{:S(2)}) collective-permute-start(bf16[160,1024]{1,0:T(8,128)(2,1)} %get-tuple-element.151.refs_0_), channel_id=1, source_target_pairs={{0,1},{1,0},{2,3},{3,2},{4,5},{5,4},{6,7},{7,6},{8,9},{9,8},{10,11... | collective-permute-start | bytes 983048 | tf_op jit(solution)/shard_map/ppermute | solution.py:68
  114.8 43.5 %collective-permute-start.27 = (bf16[160,1024]{1,0:T(8,128)(2,1)}, bf16[160,1024]{1,0:T(8,128)(2,1)}, u32[]{:S(2)}, u32[]{:S(2)}) collective-permute-start(bf16[160,1024]{1,0:T(8,128)(2,1)} %get-tuple-element.261), channel_id=1, source_target_pairs={{0,2},{1,3},{2,0},{3,1},{4,6},{5,7},{6,4},{7,5},{8,10},{9,11},{10,... | collective-permute-start | bytes 983048 | tf_op jit(solution)/shard_map/ppermute | solution.py:739
  121.0 18.5 %collective-permute-start.11 = (bf16[160,1024]{1,0:T(8,128)(2,1)S(1)}, bf16[160,1024]{1,0:T(8,128)(2,1)S(1)}, u32[]{:S(2)}, u32[]{:S(2)}) collective-permute-start(bf16[160,1024]{1,0:T(8,128)(2,1)S(1)} %get-tuple-element.147.refs_0_), channel_id=1, source_target_pairs={{0,1},{1,0},{2,3},{3,2},{4,5},{5,4},{6,7},{7,6},{8,9},{9,8},{10,11... | collective-permute-start | bytes 983048 | tf_op jit(solution)/shard_map/ppermute | solution.py:68
  121.0 18.5 %collective-permute-start.13 = (bf16[160,1024]{1,0:T(8,128)(2,1)S(1)}, bf16[160,1024]{1,0:T(8,128)(2,1)S(1)}, u32[]{:S(2)}, u32[]{:S(2)}) collective-permute-start(bf16[160,1024]{1,0:T(8,128)(2,1)S(1)} %collective-permute-done.12.refs_2_), channel_id=1, source_target_pairs={{0,1},{1,0},{2,3},{3,2},{4,5},{5,4},{6,7},{7,6},{8,9},{9,8},{10,11... | collective-permute-start | bytes 983048 | tf_op jit(solution)/shard_map/ppermute | solution.py:68
  129.9 28.4 %collective-permute-start.26 = (bf16[160,1024]{1,0:T(8,128)(2,1)}, bf16[160,1024]{1,0:T(8,128)(2,1)}, u32[]{:S(2)}, u32[]{:S(2)}) collective-permute-start(bf16[160,1024]{1,0:T(8,128)(2,1)} %get-tuple-element.262), channel_id=1, source_target_pairs={{0,1},{1,0},{2,3},{3,2},{4,5},{5,4},{6,7},{7,6},{8,9},{9,8},{10,11... | collective-permute-start | bytes 983048 | tf_op jit(solution)/shard_map/ppermute | solution.py:739
  129.9 29.8 %collective-permute-start.30 = (bf16[2,160,1024]{2,1,0:T(8,128)(2,1)}, bf16[2,160,1024]{2,1,0:T(8,128)(2,1)}, u32[]{:S(2)}, u32[]{:S(2)}) collective-permute-start(bf16[2,160,1024]{2,1,0:T(8,128)(2,1)} %get-tuple-element.171), channel_id=1, source_target_pairs={{0,1},{1,0},{2,3},{3,2},{4,5},{5,4},{6,7},{7,6},{8,9},{9,8},{10,11... | collective-permute-start | bytes 1966088 | tf_op jit(solution)/shard_map/ppermute | solution.py:68
  139.5 23.6 %collective-permute-start.28 = (bf16[2,160,1024]{2,1,0:T(8,128)(2,1)}, bf16[2,160,1024]{2,1,0:T(8,128)(2,1)}, u32[]{:S(2)}, u32[]{:S(2)}) collective-permute-start(bf16[2,160,1024]{2,1,0:T(8,128)(2,1)} %get-tuple-element.167), channel_id=1, source_target_pairs={{0,1},{1,0},{2,3},{3,2},{4,5},{5,4},{6,7},{7,6},{8,9},{9,8},{10,11... | collective-permute-start | bytes 1966088 | tf_op jit(solution)/shard_map/ppermute | solution.py:68
  165.3 20.3 %collective-permute-start.25 = (bf16[1,160,1024]{2,1,0:T(8,128)(2,1)S(1)}, bf16[1,160,1024]{2,1,0:T(8,128)(2,1)S(1)}, u32[]{:S(2)}, u32[]{:S(2)}) collective-permute-start(bf16[1,160,1024]{2,1,0:T(8,128)(2,1)S(1)} %fusion.17), channel_id=1, source_target_pairs={{0,2},{1,3},{2,0},{3,1},{4,6},{5,7},{6,4},{7,5},{8,10},{9,11},{10,... | collective-permute-start | bytes 983048 | tf_op jit(solution)/shard_map/ppermute | solution.py:68
  174.8 17.8 %collective-permute-start.41 = (bf16[160,1024]{1,0:T(8,128)(2,1)S(1)}, bf16[160,1024]{1,0:T(8,128)(2,1)S(1)}, u32[]{:S(2)}, u32[]{:S(2)}) collective-permute-start(bf16[160,1024]{1,0:T(8,128)(2,1)S(1)} %get-tuple-element.180.refs_0_), channel_id=1, source_target_pairs={{0,2},{1,3},{2,0},{3,1},{4,6},{5,7},{6,4},{7,5},{8,10},{9,11},{10,... | collective-permute-start | bytes 983048 | tf_op jit(solution)/shard_map/ppermute | solution.py:68
  181.7 18.0 %collective-permute-start.38 = (bf16[160,1024]{1,0:T(8,128)(2,1)S(1)}, bf16[160,1024]{1,0:T(8,128)(2,1)S(1)}, u32[]{:S(2)}, u32[]{:S(2)}) collective-permute-start(bf16[160,1024]{1,0:T(8,128)(2,1)S(1)} %get-tuple-element.179.refs_0_), channel_id=1, source_target_pairs={{0,2},{1,3},{2,0},{3,1},{4,6},{5,7},{6,4},{7,5},{8,10},{9,11},{10,... | collective-permute-start | bytes 983048 | tf_op jit(solution)/shard_map/ppermute | solution.py:68
  184.3 30.8 %collective-permute-start.37 = (bf16[160,1024]{1,0:T(8,128)(2,1)S(1)}, bf16[160,1024]{1,0:T(8,128)(2,1)S(1)}, u32[]{:S(2)}, u32[]{:S(2)}) collective-permute-start(bf16[160,1024]{1,0:T(8,128)(2,1)S(1)} %get-tuple-element.179.refs_0_), channel_id=1, source_target_pairs={{0,1},{1,0},{2,3},{3,2},{4,5},{5,4},{6,7},{7,6},{8,9},{9,8},{10,11... | collective-permute-start | bytes 983048 | tf_op jit(solution)/shard_map/ppermute | solution.py:68
  184.3 21.8 %collective-permute-start.40 = (bf16[160,1024]{1,0:T(8,128)(2,1)S(1)}, bf16[160,1024]{1,0:T(8,128)(2,1)S(1)}, u32[]{:S(2)}, u32[]{:S(2)}) collective-permute-start(bf16[160,1024]{1,0:T(8,128)(2,1)S(1)} %get-tuple-element.180.refs_0_), channel_id=1, source_target_pairs={{0,1},{1,0},{2,3},{3,2},{4,5},{5,4},{6,7},{7,6},{8,9},{9,8},{10,11... | collective-permute-start | bytes 983048 | tf_op jit(solution)/shard_map/ppermute | solution.py:68
  188.0 18.2 %collective-permute-start.35 = (bf16[160,1024]{1,0:T(8,128)(2,1)S(1)}, bf16[160,1024]{1,0:T(8,128)(2,1)S(1)}, u32[]{:S(2)}, u32[]{:S(2)}) collective-permute-start(bf16[160,1024]{1,0:T(8,128)(2,1)S(1)} %get-tuple-element.177.refs_0_), channel_id=1, source_target_pairs={{0,2},{1,3},{2,0},{3,1},{4,6},{5,7},{6,4},{7,5},{8,10},{9,11},{10,... | collective-permute-start | bytes 983048 | tf_op jit(solution)/shard_map/ppermute | solution.py:68
  206.8 58.8 %collective-permute-start.33 = (bf16[160,1024]{1,0:T(8,128)(2,1)}, bf16[160,1024]{1,0:T(8,128)(2,1)S(1)}, u32[]{:S(2)}, u32[]{:S(2)}) collective-permute-start(bf16[160,1024]{1,0:T(8,128)(2,1)} %get-tuple-element.258), channel_id=1, source_target_pairs={{1,0},{0,1},{3,2},{2,3},{5,4},{4,5},{7,6},{6,7},{9,8},{8,9},{11,10... | collective-permute-start | bytes 983048 | tf_op jit(solution)/shard_map/ppermute | solution.py:783
  237.0 35.5 %collective-permute-start.93 = (bf16[512,1024]{1,0:T(8,128)(2,1)}, bf16[512,1024]{1,0:T(8,128)(2,1)}, u32[]{:S(2)}, u32[]{:S(2)}) collective-permute-start(bf16[512,1024]{1,0:T(8,128)(2,1)} %constant_dynamic-slice_fusion.1), channel_id=1, source_target_pairs={{0,4},{4,0},{8,12},{12,8},{16,20},{20,16},{24,28},{28,24},{1,5},{5... | collective-permute-start | bytes 3145736 | tf_op jit(solution)/shard_map/ppermute | solution.py:68
  241.1 22.3 %collective-permute-start.54 = (bf16[1,160,1024]{2,1,0:T(8,128)(2,1)S(1)}, bf16[1,160,1024]{2,1,0:T(8,128)(2,1)S(1)}, u32[]{:S(2)}, u32[]{:S(2)}) collective-permute-start(bf16[1,160,1024]{2,1,0:T(8,128)(2,1)S(1)} %fusion.22), channel_id=1, source_target_pairs={{0,2},{1,3},{2,0},{3,1},{4,6},{5,7},{6,4},{7,5},{8,10},{9,11},{10,... | collective-permute-start | bytes 983048 | tf_op jit(solution)/shard_map/ppermute | solution.py:68
  249.4 19.9 %collective-permute-start.32 = (bf16[160,1024]{1,0:T(8,128)(2,1)S(1)}, bf16[160,1024]{1,0:T(8,128)(2,1)S(1)}, u32[]{:S(2)}, u32[]{:S(2)}) collective-permute-start(bf16[160,1024]{1,0:T(8,128)(2,1)S(1)} %copy-done.84), channel_id=1, source_target_pairs={{2,0},{3,1},{0,2},{1,3},{6,4},{7,5},{4,6},{5,7},{10,8},{11,9},{8,1... | collective-permute-start | bytes 983048 | tf_op jit(solution)/shard_map/ppermute | solution.py:783
  256.5 26.2 %collective-permute-start.87 = (bf16[512,1024]{1,0:T(8,128)(2,1)S(1)}, bf16[512,1024]{1,0:T(8,128)(2,1)}, u32[]{:S(2)}, u32[]{:S(2)}) collective-permute-start(bf16[512,1024]{1,0:T(8,128)(2,1)S(1)} %constant_dynamic-slice_fusion.4), channel_id=1, source_target_pairs={{0,8},{4,12},{8,0},{12,4},{16,24},{20,28},{24,16},{28,20},{1,9},{5... | collective-permute-start | bytes 3145736 | tf_op jit(solution)/shard_map/ppermute | solution.py:68
  286.6 35.9 %collective-permute-start.50 = (bf16[160,1024]{1,0:T(8,128)(2,1)S(1)}, bf16[160,1024]{1,0:T(8,128)(2,1)S(1)}, u32[]{:S(2)}, u32[]{:S(2)}) collective-permute-start(bf16[160,1024]{1,0:T(8,128)(2,1)S(1)} %get-tuple-element.198.refs_4_), channel_id=1, source_target_pairs={{0,1},{1,0},{2,3},{3,2},{4,5},{5,4},{6,7},{7,6},{8,9},{9,8},{10,11... | collective-permute-start | bytes 983048 | tf_op jit(solution)/shard_map/ppermute | solution.py:68
  301.7 21.1 %collective-permute-start.52 = (bf16[160,1024]{1,0:T(8,128)(2,1)S(1)}, bf16[160,1024]{1,0:T(8,128)(2,1)S(1)}, u32[]{:S(2)}, u32[]{:S(2)}) collective-permute-start(bf16[160,1024]{1,0:T(8,128)(2,1)S(1)} %collective-permute-done.51.refs_6_), channel_id=1, source_target_pairs={{0,1},{1,0},{2,3},{3,2},{4,5},{5,4},{6,7},{7,6},{8,9},{9,8},{10,11... | collective-permute-start | bytes 983048 | tf_op jit(solution)/shard_map/ppermute | solution.py:68
  306.2 30.1 %collective-permute-start.45 = (bf16[160,1024]{1,0:T(8,128)(2,1)S(1)}, bf16[160,1024]{1,0:T(8,128)(2,1)S(1)}, u32[]{:S(2)}, u32[]{:S(2)}) collective-permute-start(bf16[160,1024]{1,0:T(8,128)(2,1)S(1)} %get-tuple-element.190.refs_4_), channel_id=1, source_target_pairs={{0,1},{1,0},{2,3},{3,2},{4,5},{5,4},{6,7},{7,6},{8,9},{9,8},{10,11... | collective-permute-start | bytes 983048 | tf_op jit(solution)/shard_map/ppermute | solution.py:68
  306.2 30.1 %collective-permute-start.47 = (bf16[160,1024]{1,0:T(8,128)(2,1)S(1)}, bf16[160,1024]{1,0:T(8,128)(2,1)S(1)}, u32[]{:S(2)}, u32[]{:S(2)}) collective-permute-start(bf16[160,1024]{1,0:T(8,128)(2,1)S(1)} %collective-permute-done.46.refs_6_), channel_id=1, source_target_pairs={{0,1},{1,0},{2,3},{3,2},{4,5},{5,4},{6,7},{7,6},{8,9},{9,8},{10,11... | collective-permute-start | bytes 983048 | tf_op jit(solution)/shard_map/ppermute | solution.py:68
  306.7 76.8 %collective-permute-start.95 = (bf16[128,1024]{1,0:T(8,128)(2,1)}, bf16[128,1024]{1,0:T(8,128)(2,1)}, u32[]{:S(2)}, u32[]{:S(2)}) collective-permute-start(bf16[128,1024]{1,0:T(8,128)(2,1)} %constant_dynamic-slice_fusion.15), channel_id=1, source_target_pairs={{0,16},{4,20},{8,24},{12,28},{16,0},{20,4},{24,8},{28,12},{1,17},{... | collective-permute-start | bytes 786440 | tf_op jit(solution)/shard_map/ppermute | solution.py:68
  322.5 66.9 %collective-permute-start.89 = (bf16[128,1024]{1,0:T(8,128)(2,1)}, bf16[128,1024]{1,0:T(8,128)(2,1)}, u32[]{:S(2)}, u32[]{:S(2)}) collective-permute-start(bf16[128,1024]{1,0:T(8,128)(2,1)} %constant_dynamic-slice_fusion.2), channel_id=1, source_target_pairs={{0,16},{4,20},{8,24},{12,28},{16,0},{20,4},{24,8},{28,12},{1,17},{... | collective-permute-start | bytes 786440 | tf_op jit(solution)/shard_map/ppermute | solution.py:68
  372.1 65.2 %collective-permute-start.62 = (bf16[2,160,1024]{2,1,0:T(8,128)(2,1)S(1)}, bf16[2,160,1024]{2,1,0:T(8,128)(2,1)S(1)}, u32[]{:S(2)}, u32[]{:S(2)}) collective-permute-start(bf16[2,160,1024]{2,1,0:T(8,128)(2,1)S(1)} %get-tuple-element.227), channel_id=1, source_target_pairs={{0,1},{1,0},{2,3},{3,2},{4,5},{5,4},{6,7},{7,6},{8,9},{9,8},{10,11... | collective-permute-start | bytes 1966088 | tf_op jit(solution)/shard_map/ppermute | solution.py:68
  383.5 68.2 %collective-permute-start.60 = (bf16[2,160,1024]{2,1,0:T(8,128)(2,1)S(1)}, bf16[2,160,1024]{2,1,0:T(8,128)(2,1)S(1)}, u32[]{:S(2)}, u32[]{:S(2)}) collective-permute-start(bf16[2,160,1024]{2,1,0:T(8,128)(2,1)S(1)} %get-tuple-element.224), channel_id=1, source_target_pairs={{0,1},{1,0},{2,3},{3,2},{4,5},{5,4},{6,7},{7,6},{8,9},{9,8},{10,11... | collective-permute-start | bytes 1966088 | tf_op jit(solution)/shard_map/ppermute | solution.py:68
  383.5 54.1 %collective-permute-start.64 = (bf16[512,768]{1,0:T(8,128)(2,1)S(1)}, bf16[512,768]{1,0:T(8,128)(2,1)S(1)}, u32[]{:S(2)}, u32[]{:S(2)}) collective-permute-start(bf16[512,768]{1,0:T(8,128)(2,1)S(1)} %constant_dynamic-slice_fusion.13), channel_id=1, source_target_pairs={{0,8},{4,12},{8,0},{12,4},{16,24},{20,28},{24,16},{28,20},{1,9},{5... | collective-permute-start | bytes 2359304 | tf_op jit(solution)/shard_map/ppermute | solution.py:68
  386.2 28.7 %collective-permute-start.96 = (bf16[128,1024]{1,0:T(8,128)(2,1)S(1)}, bf16[128,1024]{1,0:T(8,128)(2,1)S(1)}, u32[]{:S(2)}, u32[]{:S(2)}) collective-permute-start(bf16[128,1024]{1,0:T(8,128)(2,1)S(1)} %add_convert_fusion.8.in_ref), channel_id=1, source_target_pairs={{0,16},{4,20},{8,24},{12,28},{16,0},{20,4},{24,8},{28,12},{1,17},{... | collective-permute-start | bytes 786440 | tf_op jit(solution)/shard_map/ppermute | solution.py:68
  389.4 22.6 %collective-permute-start.82 = (bf16[64,1024]{1,0:T(8,128)(2,1)S(1)}, bf16[64,1024]{1,0:T(8,128)(2,1)S(1)}, u32[]{:S(2)}, u32[]{:S(2)}) collective-permute-start(bf16[64,1024]{1,0:T(8,128)(2,1)S(1)} %constant_dynamic-slice_fusion.6), channel_id=1, source_target_pairs={{0,8},{4,12},{8,0},{12,4},{16,24},{20,28},{24,16},{28,20},{1,9},{5... | collective-permute-start | bytes 393224 | tf_op jit(solution)/shard_map/ppermute | solution.py:68
  411.9 19.0 %collective-permute-start.90 = (bf16[128,1024]{1,0:T(8,128)(2,1)S(1)}, bf16[128,1024]{1,0:T(8,128)(2,1)S(1)}, u32[]{:S(2)}, u32[]{:S(2)}) collective-permute-start(bf16[128,1024]{1,0:T(8,128)(2,1)S(1)} %add_convert_fusion.9.in_ref), channel_id=1, source_target_pairs={{0,16},{4,20},{8,24},{12,28},{16,0},{20,4},{24,8},{28,12},{1,17},{... | collective-permute-start | bytes 786440 | tf_op jit(solution)/shard_map/ppermute | solution.py:68
  429.4 20.5 %collective-permute-start.70 = (bf16[512,768]{1,0:T(8,128)(2,1)S(1)}, bf16[512,768]{1,0:T(8,128)(2,1)S(1)}, u32[]{:S(2)}, u32[]{:S(2)}) collective-permute-start(bf16[512,768]{1,0:T(8,128)(2,1)S(1)} %constant_dynamic-slice_fusion.10), channel_id=1, source_target_pairs={{0,4},{4,0},{8,12},{12,8},{16,20},{20,16},{24,28},{28,24},{1,5},{5... | collective-permute-start | bytes 2359304 | tf_op jit(solution)/shard_map/ppermute | solution.py:68
  437.3 88.8 %collective-permute-start.58 = (bf16[2,160,1024]{2,1,0:T(8,128)(2,1)S(1)}, bf16[2,160,1024]{2,1,0:T(8,128)(2,1)S(1)}, u32[]{:S(2)}, u32[]{:S(2)}) collective-permute-start(bf16[2,160,1024]{2,1,0:T(8,128)(2,1)S(1)} %get-tuple-element.220), channel_id=1, source_target_pairs={{0,1},{1,0},{2,3},{3,2},{4,5},{5,4},{6,7},{7,6},{8,9},{9,8},{10,11... | collective-permute-start | bytes 1966088 | tf_op jit(solution)/shard_map/ppermute | solution.py:68
  437.3 74.9 %collective-permute-start.97 = (bf16[256,1024]{1,0:T(8,128)(2,1)S(1)}, bf16[256,1024]{1,0:T(8,128)(2,1)S(1)}, u32[]{:S(2)}, u32[]{:S(2)}) collective-permute-start(bf16[256,1024]{1,0:T(8,128)(2,1)S(1)} %pad_maximum_fusion.6), channel_id=1, source_target_pairs={{0,8},{4,12},{8,0},{12,4},{16,24},{20,28},{24,16},{28,20},{1,9},{5... | collective-permute-start | bytes 1572872 | tf_op jit(solution)/shard_map/ppermute | solution.py:68
  437.6 74.8 %collective-permute-start.91 = (bf16[256,1024]{1,0:T(8,128)(2,1)S(1)}, bf16[256,1024]{1,0:T(8,128)(2,1)S(1)}, u32[]{:S(2)}, u32[]{:S(2)}) collective-permute-start(bf16[256,1024]{1,0:T(8,128)(2,1)S(1)} %pad_maximum_fusion.5), channel_id=1, source_target_pairs={{0,4},{4,0},{8,12},{12,8},{16,20},{20,16},{24,28},{28,24},{1,5},{5... | collective-permute-start | bytes 1572872 | tf_op jit(solution)/shard_map/ppermute | solution.py:68
  449.9 17.7 %collective-permute-start.65 = (bf16[256,768]{1,0:T(8,128)(2,1)S(1)}, bf16[256,768]{1,0:T(8,128)(2,1)S(1)}, u32[]{:S(2)}, u32[]{:S(2)}) collective-permute-start(bf16[256,768]{1,0:T(8,128)(2,1)S(1)} %constant_dynamic-slice_fusion.12), channel_id=1, source_target_pairs={{0,4},{4,0},{8,12},{12,8},{16,20},{20,16},{24,28},{28,24},{1,5},{5... | collective-permute-start | bytes 1179656 | tf_op jit(solution)/shard_map/ppermute | solution.py:68
  451.7 17.7 %collective-permute-start.71 = (bf16[256,768]{1,0:T(8,128)(2,1)S(1)}, bf16[256,768]{1,0:T(8,128)(2,1)S(1)}, u32[]{:S(2)}, u32[]{:S(2)}) collective-permute-start(bf16[256,768]{1,0:T(8,128)(2,1)S(1)} %constant_dynamic-slice_fusion.9), channel_id=1, source_target_pairs={{0,8},{4,12},{8,0},{12,4},{16,24},{20,28},{24,16},{28,20},{1,9},{5... | collective-permute-start | bytes 1179656 | tf_op jit(solution)/shard_map/ppermute | solution.py:68
  467.6 24.0 %collective-permute-start.85 = (bf16[64,1024]{1,0:T(8,128)(2,1)S(1)}, bf16[64,1024]{1,0:T(8,128)(2,1)S(1)}, u32[]{:S(2)}, u32[]{:S(2)}) collective-permute-start(bf16[64,1024]{1,0:T(8,128)(2,1)S(1)} %pad_maximum_fusion.10), channel_id=1, source_target_pairs={{0,8},{4,12},{8,0},{12,4},{16,24},{20,28},{24,16},{28,20},{1,9},{5... | collective-permute-start | bytes 393224 | tf_op jit(solution)/shard_map/ppermute | solution.py:68
  491.6 19.0 %collective-permute-start.73 = (bf16[128,768]{1,0:T(8,128)(2,1)S(1)}, bf16[128,768]{1,0:T(8,128)(2,1)S(1)}, u32[]{:S(2)}, u32[]{:S(2)}) collective-permute-start(bf16[128,768]{1,0:T(8,128)(2,1)S(1)} %add_convert_fusion.11.in_ref), channel_id=1, source_target_pairs={{0,16},{4,20},{8,24},{12,28},{16,0},{20,4},{24,8},{28,12},{1,17},{... | collective-permute-start | bytes 589832 | tf_op jit(solution)/shard_map/ppermute | solution.py:68
  506.5 23.1 %collective-permute-start.63 = (bf16[1,160,1024]{2,1,0:T(8,128)(2,1)S(1)}, bf16[1,160,1024]{2,1,0:T(8,128)(2,1)S(1)}, u32[]{:S(2)}, u32[]{:S(2)}) collective-permute-start(bf16[1,160,1024]{2,1,0:T(8,128)(2,1)S(1)} %fusion.25), channel_id=1, source_target_pairs={{0,2},{1,3},{2,0},{3,1},{4,6},{5,7},{6,4},{7,5},{8,10},{9,11},{10,... | collective-permute-start | bytes 983048 | tf_op jit(solution)/shard_map/ppermute | solution.py:68
  522.6 34.7 %collective-permute-start.98 = (bf16[512,1024]{1,0:T(8,128)(2,1)S(1)}, bf16[512,1024]{1,0:T(8,128)(2,1)S(1)}, u32[]{:S(2)}, u32[]{:S(2)}) collective-permute-start(bf16[512,1024]{1,0:T(8,128)(2,1)S(1)} %pad_maximum_fusion.1), channel_id=1, source_target_pairs={{0,4},{4,0},{8,12},{12,8},{16,20},{20,16},{24,28},{28,24},{1,5},{5... | collective-permute-start | bytes 3145736 | tf_op jit(solution)/shard_map/ppermute | solution.py:68
  525.1 34.7 %collective-permute-start.92 = (bf16[512,1024]{1,0:T(8,128)(2,1)}, bf16[512,1024]{1,0:T(8,128)(2,1)S(1)}, u32[]{:S(2)}, u32[]{:S(2)}) collective-permute-start(bf16[512,1024]{1,0:T(8,128)(2,1)} %pad_maximum_fusion), channel_id=1, source_target_pairs={{0,8},{4,12},{8,0},{12,4},{16,24},{20,28},{24,16},{28,20},{1,9},{5... | collective-permute-start | bytes 3145736 | tf_op jit(solution)/shard_map/ppermute | solution.py:68
  528.2 40.6 %collective-permute-start.69 = (bf16[512,768]{1,0:T(8,128)(2,1)}, bf16[512,768]{1,0:T(8,128)(2,1)S(1)}, u32[]{:S(2)}, u32[]{:S(2)}) collective-permute-start(bf16[512,768]{1,0:T(8,128)(2,1)} %pad_maximum_fusion.3), channel_id=1, source_target_pairs={{0,8},{4,12},{8,0},{12,4},{16,24},{20,28},{24,16},{28,20},{1,9},{5... | collective-permute-start | bytes 2359304 | tf_op jit(solution)/shard_map/ppermute | solution.py:68
  529.6 37.0 %collective-permute-start.75 = (bf16[512,768]{1,0:T(8,128)(2,1)}, bf16[512,768]{1,0:T(8,128)(2,1)S(1)}, u32[]{:S(2)}, u32[]{:S(2)}) collective-permute-start(bf16[512,768]{1,0:T(8,128)(2,1)} %pad_maximum_fusion.4), channel_id=1, source_target_pairs={{0,4},{4,0},{8,12},{12,8},{16,20},{20,16},{24,28},{28,24},{1,5},{5... | collective-permute-start | bytes 2359304 | tf_op jit(solution)/shard_map/ppermute | solution.py:68
  (144 other events, 1580.4 us)

commit v2 on v1

v2 whole, which is shorter than its diff:
```python
import functools

import jax
import jax.numpy as jnp
import numpy as np
from jax import lax
from jax.experimental import pallas as pl
from jax.experimental.pallas import tpu as pltpu
from jax.sharding import PartitionSpec as P

HD = 64
NORM_EPS = 1e-05
MASKED = -1e30
F32 = jnp.float32
BF16 = jnp.bfloat16
VMEM_LIMIT = 48 * 1024 * 1024
COST = 5e8


def nn(a, b):
    return lax.dot_general(a, b, (((1,), (0,)), ((), ())), preferred_element_type=F32)


def nt(a, b):
    return lax.dot_general(a, b, (((1,), (1,)), ((), ())), preferred_element_type=F32)


def tn(a, b):
    return lax.dot_general(a, b, (((0,), (0,)), ((), ())), preferred_element_type=F32)


class Order:
    mark = None


def call(body, name, *, grid=(1,), prefetch=(), ins, outs, aliases=None, scratch=(), weight=1.0):
    def spec(block, index_map):
        if block is None:
            return pl.BlockSpec(memory_space=pl.ANY)
        return pl.BlockSpec(block, index_map)

    shift = len(prefetch)
    marks = [] if Order.mark is None else [Order.mark]
    n_in, n_out = shift + len(ins), len(outs)

    def inner(*refs):
        given, rest = refs[:n_in], refs[n_in + len(marks) :]
        body(*given, *rest[:n_out], *rest[n_out + 1 :])

    in_specs = [spec(block, index_map) for _, block, index_map in ins]
    in_specs += [pl.BlockSpec(memory_space=pl.ANY) for _ in marks]
    out_specs = [spec(block, index_map) for _, _, block, index_map in outs]
    out_specs.append(pl.BlockSpec(memory_space=pl.ANY))
    shapes = [jax.ShapeDtypeStruct(shape, dtype) for shape, dtype, _, _ in outs]
    *results, Order.mark = pl.pallas_call(
        inner,
        grid_spec=pltpu.PrefetchScalarGridSpec(
            num_scalar_prefetch=shift,
            grid=grid,
            in_specs=in_specs,
            out_specs=out_specs,
            scratch_shapes=list(scratch),
        ),
        out_shape=[*shapes, jax.ShapeDtypeStruct((8, 128), F32)],
        input_output_aliases={shift + k: v for k, v in (aliases or {}).items()},
        compiler_params=pltpu.CompilerParams(vmem_limit_bytes=VMEM_LIMIT),
        cost_estimate=pl.CostEstimate(flops=int(weight * COST), bytes_accessed=1, transcendentals=0),
        name=name,
    )(*prefetch, *[array for array, _, _ in ins], *marks)
    return results


def whole(array):
    zeros = (0,) * array.ndim
    return (array, array.shape, lambda *_: zeros)


def out_whole(shape, dtype):
    zeros = (0,) * len(shape)
    return (shape, dtype, shape, lambda *_: zeros)


def swap(array, axis, size, bit):
    return lax.ppermute(array, axis, [(r, r ^ bit) for r in range(size)])


def gather_blocks(own, size):
    blocks = {0: own}
    bit = 2
    while bit < size:
        for j in sorted(blocks):
            blocks[j | bit] = swap(blocks[j], "tensor", size, bit)
        bit *= 2
    for j in sorted(blocks):
        blocks[j | 1] = swap(blocks[j], "tensor", size, 1)
    return [blocks[j] for j in range(size)]


def combine(keep, received):
    def body(k_ref, r_ref, o_ref):
        o_ref[...] = (k_ref[...].astype(F32) + r_ref[...].astype(F32)).astype(BF16)

    return call(body, "combine", ins=[whole(keep), whole(received)], outs=[out_whole(keep.shape, BF16)])[0]


def scatter_start(sends, size):
    return [swap(block, "tensor", size, 1) for block in sends]


def scatter_rest(keeps, received, size):
    addends = [keeps[0][None], received[0][None]]
    held = {2 * m: combine(keeps[m], received[m]) for m in range(1, len(keeps))}
    bit = size // 2
    while bit >= 2:
        leaving = sorted(j for j in held if j & bit)
        arrived = [swap(held.pop(j), "tensor", size, bit) for j in leaving]
        addends.append(arrived[0][None])
        for j, block in zip(leaving[1:], arrived[1:], strict=True):
            held[j ^ bit] = combine(held[j ^ bit], block)
        bit //= 2
    return addends


def addend_specs(addends):
    return [(a, (1,) + a.shape[1:], lambda *_: (0, 0, 0)) for a in addends]


def place_outs(state, shapes, layout, rows, spot_of, ins):
    outs, aliases = [], {}
    for number, (out, first, leads, _, wide) in enumerate(layout):
        index_map = functools.partial(lambda lead, m, spots: (lead, spot_of(m, spots), 0), first // leads)
        outs.append((shapes[out], F32, (leads, rows, wide), index_map))
        if out in state:
            aliases[len(ins)] = number
            ins.append((state[out], None, None))
    return outs, aliases


def place_values(values, layout, out_refs):
    for (_, _, leads, start, wide), out_ref in zip(layout, out_refs, strict=True):
        for lead in range(leads):
            at = start + lead * wide
            out_ref[lead] = values[:, at : at + wide].astype(F32)


def place(state, shapes, array, places, layout, name):
    count = places.shape[0]
    rows = array.shape[0] // count
    n_out = len(layout)

    def body(places_ref, in_ref, *refs):
        place_values(in_ref[...], layout, refs[-n_out:])

    ins = [(array, (rows, array.shape[1]), lambda m, spots: (m, 0))]
    outs, aliases = place_outs(state, shapes, layout, rows, lambda m, spots: spots[m], ins)
    got = call(body, name, grid=(count,), prefetch=(places,), ins=ins, outs=outs, aliases=aliases)
    state.update({entry[0]: value for entry, value in zip(layout, got, strict=True)})


class DpSum:
    def __init__(self, array, order, size, state, shapes, layout, name):
        self.order, self.size, self.name = order, size, name
        self.state, self.shapes, self.layout = state, shapes, layout
        self.at = 0
        self.whole = array.shape[0] % (16 * size) != 0
        if self.whole:
            self.staying = lax.psum(array, "dp")
            return
        here = lax.axis_index("dp")
        self.mine = [(here >> bit) & 1 for bit in order]
        half = array.shape[0] // 2
        leaving = lax.dynamic_slice_in_dim(array, (1 - self.mine[0]) * half, half, 0)
        self.staying = array
        self.arrived = swap(leaving, "dp", size, 1 << order[0])
        self.held = [0]

    def where(self, differs):
        spot = 0
        for level, mine in enumerate(self.mine):
            spot = spot * 2 + (mine ^ ((differs >> level) & 1))
        return spot

    def step(self):
        if self.whole:
            if self.at == 0:
                place(self.state, self.shapes, self.staying, jnp.zeros((1,), jnp.int32), self.layout, self.name)
        elif self.at < len(self.order):
            self.halve()
        else:
            self.join()
        self.at += 1

    def halve(self):
        level, bits = self.at, len(self.order)
        rows, columns = self.arrived.shape
        last = level == bits - 1
        half = rows // 2
        scalars = [self.mine[0] if level == 0 else 0, self.where(0) if last else self.mine[level + 1]]
        n_out = len(self.layout)

        def body(scalars_ref, stay_ref, came_ref, *refs):
            if last:
                total = (stay_ref[...].astype(F32) + came_ref[...].astype(F32)).astype(BF16)
                refs[-1][...] = total
                place_values(total, self.layout, refs[-1 - n_out : -1])
                return
            for out_ref, part in ((refs[-2], 1 - scalars_ref[1]), (refs[-1], scalars_ref[1])):
                at = pl.ds(pl.multiple_of(part * half, 16), half)
                out_ref[...] = (stay_ref[at, :].astype(F32) + came_ref[at, :].astype(F32)).astype(BF16)

        ins = [(self.staying, (rows, columns), lambda m, spots: (spots[0], 0)), whole(self.arrived)]
        prefetch = (jnp.stack([jnp.asarray(v, jnp.int32) for v in scalars]),)
        if last:
            outs, aliases = place_outs(self.state, self.shapes, self.layout, rows, lambda m, spots: spots[1], ins)
            outs.append(out_whole((rows, columns), BF16))
        else:
            outs, aliases = [out_whole((half, columns), BF16)] * 2, {}
        *got, self.staying = call(
            body, self.name + "_halve", prefetch=prefetch, ins=ins, outs=outs, aliases=aliases
        )
        if last:
            self.state.update({entry[0]: value for entry, value in zip(self.layout, got, strict=True)})
            self.arrived = swap(self.staying, "dp", self.size, 1 << self.order[level])
        else:
            self.arrived = swap(got[0], "dp", self.size, 1 << self.order[level + 1])

    def join(self):
        level = 2 * len(self.order) - 1 - self.at
        count = len(self.held)
        came = [differs | (1 << level) for differs in self.held]
        spots = jnp.stack([self.where(d) for d in came]).astype(jnp.int32)
        self.held = self.held + came
        total, columns = self.arrived.shape
        rows = total // count
        n_out = len(self.layout)
        block = lambda m, spots: (m, 0)
        ins = [(self.arrived, (rows, columns), block)]
        if level:
            ins.append((self.staying, (rows, columns), block))

        def body(spots_ref, came_ref, *refs):
            values = came_ref[...]
            if level:
                refs[-1][0] = refs[0][...]
                refs[-1][1] = values
                place_values(values, self.layout, refs[-1 - n_out : -1])
            else:
                place_values(values, self.layout, refs[-n_out:])

        outs, aliases = place_outs(self.state, self.shapes, self.layout, rows, lambda m, spots: spots[m], ins)
        if level:
            outs.append(((2, total, columns), BF16, (2, rows, columns), lambda m, spots: (0, m, 0)))
        got = call(
            body, self.name + "_join", grid=(count,), prefetch=(spots,), ins=ins, outs=outs, aliases=aliases
        )
        if level:
            self.staying = got.pop().reshape(2 * total, columns)
            self.arrived = swap(self.staying, "dp", self.size, 1 << self.order[level - 1])
        self.state.update({entry[0]: value for entry, value in zip(self.layout, got, strict=True)})


def doubling_sum(array, axis, size):
    bit = 1
    while bit < size:
        array = array + swap(array, axis, size, bit)
        bit *= 2
    return array


def piece_rounds(count, size):
    left = {}
    for g in range(count * size):
        left.setdefault((g // count, g % size), []).append(g)
    rounds = []
    for _ in range(count):
        match = {}

        def augment(u, seen):
            for v in range(size):
                if left.get((u, v)) and v not in seen:
                    seen.add(v)
                    if v not in match or augment(match[v], seen):
                        match[v] = u
                        return True
            return False

        for bit in range(size):
            if all(left.get((u, u ^ bit)) for u in range(size)):
                match.update({u ^ bit: u for u in range(size)})
                break
        else:
            for u in range(size):
                augment(u, set())
        chosen = {u: (v, left[(u, v)].pop(0)) for v, u in match.items()}
        rounds.append([chosen[u] for u in range(size)])
    return rounds


def erf_parts(u):
    size = jnp.abs(u) * np.float32(0.7071067811865476)
    bell = jnp.exp(-(size * size))
    t = pl.reciprocal(1.0 + np.float32(0.3275911) * size)
    poly = np.float32(1.061405429 * 0.5)
    for c in (-1.453152027, 1.421413741, -0.284496736, 0.254829592):
        poly = poly * t + np.float32(c * 0.5)
    tail = poly * t * bell
    return jnp.where(u < 0, tail, 1.0 - tail), bell * np.float32(0.3989422804014327)


def write_rows(values, out_refs, size, rows):
    for j in range(size):
        out_refs[j][...] = values[j * rows : (j + 1) * rows].astype(BF16)


def partial_outs(size, rows, width):
    return [out_whole((rows, width), BF16) for _ in range(size)]


def column(row, wide):
    one = jnp.broadcast_to(row.astype(F32), (128, row.shape[1])).T
    return one if wide == 128 else jnp.concatenate([one] * (wide // 128), axis=1)


def project_rows(blocks, codes, weights, biases, buffers, k, count):
    size = len(blocks)
    rows, d = blocks[0].shape
    width = weights[1].shape[1]

    def body(*refs):
        x_refs = refs[:size]
        kind_ref, qw_ref, kw_ref, vw_ref, b_ref = refs[size : size + 5]
        out_ref, x_out = refs[-2:]
        x = jnp.concatenate([r[...] for r in x_refs], axis=0)
        for j in range(size):
            x_out[j] = x_refs[j][...]
        word = column(kind_ref[0] & 1, width) == 0.0
        bias = [b_ref[m : m + 1, :] for m in range(6)]
        for part, (first, second) in enumerate(((0, 2), (1, 3))):
            one = nn(x, qw_ref[first]) + bias[first]
            two = nn(x, qw_ref[second]) + bias[second]
            both = jnp.where(word, one, two).astype(BF16)
            for j in range(size):
                out_ref[j, :, part * width : (part + 1) * width] = both[j * rows : (j + 1) * rows]
        for part, ref, m in ((2, kw_ref, 4), (3, vw_ref, 5)):
            both = (nn(x, ref[...]) + bias[m]).astype(BF16)
            for j in range(size):
                out_ref[j, :, part * width : (part + 1) * width] = both[j * rows : (j + 1) * rows]

    ins = [whole(b) for b in blocks]
    ins.append((codes, (1,) + codes.shape[1:], lambda *_: (k, 0, 0)))
    ins += [whole(w) for w in weights] + [whole(biases)]
    aliases = {}
    if buffers is not None:
        for number, b in enumerate(buffers):
            aliases[len(ins)] = number
            ins.append((b, None, None))
    outs = [
        ((count * size, rows, 4 * width), BF16, (size, rows, 4 * width), lambda *_: (k, 0, 0)),
        ((count * size, rows, d), BF16, (size, rows, d), lambda *_: (k, 0, 0)),
    ]
    return call(
        body, "project_rows", weight=5, ins=ins, outs=outs, aliases=aliases,
    )


def head_views(piece_refs, part, pair, width):
    start = part * width + pair * 128
    return jnp.concatenate([r[0, :, start : start + 128] for r in piece_refs], axis=0)


def swap_lanes(values):
    return pltpu.roll(values.astype(F32), 64, 1)


def extended(piece_refs, pair, width, takes, left):
    qw = head_views(piece_refs, 0, pair, width)
    qe = head_views(piece_refs, 1, pair, width)
    k = head_views(piece_refs, 2, pair, width)
    v = head_views(piece_refs, 3, pair, width)
    qw32, qe32, k32 = qw.astype(F32), qe.astype(F32), k.astype(F32) * 0.125
    qw_s, qe_s, k_s = swap_lanes(qw32), swap_lanes(qe32), swap_lanes(k32)
    q_ext = (
        jnp.where(left, qw32, qe_s).astype(BF16),
        jnp.where(left, qw_s, qe32).astype(BF16),
    )
    k_ext = (
        jnp.where(takes, jnp.where(left, k32, k_s), 0.0).astype(BF16),
        jnp.where(takes, jnp.where(left, k_s, k32), 0.0).astype(BF16),
    )
    return q_ext, k_ext, v


def query_blocks(length):
    spans, at = [], 0
    while at < length:
        step = 256 if length - at >= 256 else length - at
        spans.append((at, step))
        at += step
    return spans


def attend(pieces, table, s, codes, out_proj, size, rows):
    length = size * rows
    width, d = out_proj.shape
    pairs = width // 128

    def body(table_ref, *refs):
        piece_refs = refs[:size]
        code_ref, wo_ref, c_ref, lse_ref = refs[size : size + 4]
        left = lax.broadcasted_iota(jnp.int32, (length, 128), 1) < 64
        code = code_ref[0]
        word = column(code & 1, 128) == 0.0
        takes = word == left
        segr = (code >> 1).astype(F32)
        segc = column(code >> 1, 256)
        for pair in range(pairs):
            q_ext, k_ext, v = extended(piece_refs, pair, width, takes, left)
            v_t = v.astype(F32).T.astype(BF16)
            for at, step in query_blocks(length):
                same = segc[:, :step] == segr[:, at : at + step]
                tops = []
                for h in range(2):
                    s_t = nt(k_ext[h], q_ext[h][at : at + step])
                    s_t = jnp.where(same, s_t, MASKED)
                    top = jnp.max(s_t, axis=0, keepdims=True)
                    e = jnp.exp(s_t - top)
                    total = jnp.sum(e, axis=0, keepdims=True)
                    o_t = nn(v_t[h * 64 : h * 64 + 64], e.astype(BF16))
                    tops.append(o_t * (1.0 / total))
                    lse_ref[2 * pair + h : 2 * pair + h + 1, at : at + step] = top + jnp.log(total)
                c = jnp.concatenate(tops, axis=0).T.astype(BF16)
                c_ref[at : at + step, pair * 128 : pair * 128 + 128] = c
        write_rows(nn(c_ref[...], wo_ref[...]), refs[-size:], size, rows)

    ins = [
        (pieces, (1, rows, 4 * width), functools.partial(lambda j, _, t: (t[s * size + j], 0, 0), j))
        for j in range(size)
    ]
    ins += [
        (codes, (1, 1, length), lambda *_: (s, 0, 0)),
        whole(out_proj),
    ]
    outs = [out_whole((length, width), BF16), out_whole((8, length), F32)]
    outs += partial_outs(size, rows, d)
    return call(
        body, "attend", weight=7, prefetch=(table,), ins=ins, outs=outs,
    )


def attend_back(pieces, table, s, codes, out_proj, context, lse, delta_blocks, buffers, sums, count):
    size = len(delta_blocks)
    rows, d = delta_blocks[0].shape
    length = size * rows
    width = out_proj.shape[0]
    pairs = width // 128

    def body(table_ref, *refs):
        piece_refs = refs[:size]
        delta_refs = refs[size : 2 * size]
        code_ref, wo_ref, c_ref, lse_ref = refs[2 * size : 2 * size + 4]
        n_out = 5
        tail = refs[2 * size + 4 :]
        sum_in = tail[0] if sums is not None else None
        first_out, second_out, delta_out, wo_grad, bias_out, first_all, second_all = tail[-(n_out + 2) :]
        step_at = pl.program_id(0)

        @pl.when(step_at == 0)
        def _():
            left = lax.broadcasted_iota(jnp.int32, (length, 128), 1) < 64
            code = code_ref[0]
            word = column(code & 1, 128) == 0.0
            takes = word == left
            segr = (code >> 1).astype(F32)
            segc = column(code >> 1, 256)
            delta = jnp.concatenate([r[...] for r in delta_refs], axis=0)
            c_all = c_ref[...]
            grad = nn(c_all.astype(F32).T.astype(BF16), delta)
            wo_grad[...] = grad if sum_in is None else grad + sum_in[...]
            for pair in range(pairs):
                dc = nt(delta, wo_ref[pair * 128 : pair * 128 + 128, :]).astype(BF16)
                q_ext, k_ext, v = extended(piece_refs, pair, width, takes, left)
                k_ext_t = [k.astype(F32).T.astype(BF16) for k in k_ext]
                dc32 = dc.astype(F32)
                dc_h = (jnp.where(left, dc32, 0.0).astype(BF16), jnp.where(left, 0.0, dc32).astype(BF16))
                dv = jnp.zeros((length, 128), F32)
                dk = [jnp.zeros((length, 128), F32)] * 2
                dq = [[], []]
                for at, step in query_blocks(length):
                    same = segc[:, :step] == segr[:, at : at + step]
                    for h in range(2):
                        q_b, dc_b = q_ext[h][at : at + step], dc_h[h][at : at + step]
                        row = 2 * pair + h
                        s_t = nt(k_ext[h], q_b)
                        p = jnp.where(same, jnp.exp(s_t - lse_ref[row : row + 1, at : at + step]), 0.0)
                        dp = nt(v, dc_b)
                        row_inner = jnp.sum(p * dp, axis=0, keepdims=True)
                        ds = (p * (dp - row_inner)).astype(BF16)
                        dv = dv + nn(p.astype(BF16), dc_b)
                        dk[h] = dk[h] + nn(ds, q_b)
                        dq[h].append(nn(k_ext_t[h], ds).T)
                dq0, dq1 = (jnp.concatenate(parts, axis=0) for parts in dq)
                dqw = jnp.where(left, dq0, swap_lanes(dq1))
                dqe = jnp.where(left, swap_lanes(dq0), dq1)
                dk0, dk1 = dk[0] * 0.125, dk[1] * 0.125
                dk_pair = jnp.where(takes, jnp.where(left, dk0, dk1), jnp.where(left, swap_lanes(dk0), swap_lanes(dk1)))
                outs = (
                    jnp.where(word, dqw, 0.0), jnp.where(word, dqe, 0.0), jnp.where(word, 0.0, dqw),
                    jnp.where(word, 0.0, dqe), dk_pair, dv,
                )
                for number, values in enumerate(outs):
                    rounded = values.astype(BF16)
                    target = (first_all, second_all)[number // 3]
                    start = (number % 3) * width + pair * 128
                    target[:, start : start + 128] = rounded
                    bias_out[number : number + 1, pair * 128 : pair * 128 + 128] = jnp.sum(
                        rounded.astype(F32), axis=0, keepdims=True
                    )

        at_rows = pl.ds(pl.multiple_of(step_at * rows, 16), rows)
        first_out[0] = first_all[at_rows, :]
        second_out[0] = second_all[at_rows, :]
        for j in range(size):

            @pl.when(step_at == j)
            def _():
                delta_out[0] = delta_refs[j][...]

    ins = [
        (pieces, (1, rows, 4 * width), functools.partial(lambda j, _, t: (t[s * size + j], 0, 0), j))
        for j in range(size)
    ]
    ins += [whole(b) for b in delta_blocks]
    ins += [
        (codes, (1, 1, length), lambda *_: (s, 0, 0)),
        whole(out_proj),
        whole(context),
        whole(lse),
    ]
    if sums is not None:
        ins.append(whole(sums))
    aliases = {}
    if buffers is not None:
        for number, b in enumerate(buffers):
            aliases[len(ins)] = number
            ins.append((b, None, None))
    spot = lambda m, t: (t[s * size + m], 0, 0)
    outs = [
        ((count * size, rows, 3 * width), BF16, (1, rows, 3 * width), spot),
        ((count * size, rows, 3 * width), BF16, (1, rows, 3 * width), spot),
        ((count * size, rows, d), BF16, (1, rows, d), spot),
        out_whole((width, d), F32),
        out_whole((8, width), F32),
    ]
    return call(
        body, "attend_back", weight=13, grid=(size,), prefetch=(table,), ins=ins, outs=outs, aliases=aliases,
        scratch=[pltpu.VMEM((length, 3 * width), BF16)] * 2,
    )


def add_up(refs):
    total = refs[0][0].astype(F32)
    for r in refs[1:]:
        total = total + r[0].astype(F32)
    return total


def normed(values):
    centre = jnp.mean(values, axis=-1, keepdims=True)
    offset = values - centre
    spread = jnp.mean(offset * offset, axis=-1, keepdims=True)
    rstd = lax.rsqrt(spread + NORM_EPS)
    return offset * rstd, rstd


def norm_pull(upstream, n, rstd, gain):
    scaled = upstream * gain
    inner = jnp.mean(scaled, axis=-1, keepdims=True)
    cross = jnp.mean(scaled * n, axis=-1, keepdims=True)
    return rstd * (scaled - inner - n * cross)


def column_sum(values):
    return jnp.sum(values, axis=0, keepdims=True)


def inner_norm(addends, x_pieces, table, s, bias, gain, shift, size):
    rows, d = addends[0].shape[1:]
    n_add = len(addends)

    def body(table_ref, *refs):
        x_ref, b_ref, g_ref, h_ref, y_ref, n_ref, rstd_ref = refs[n_add:]
        r = add_up(refs[:n_add]) + b_ref[...] + x_ref[0].astype(F32)
        n, rstd = normed(r)
        n_ref[...] = n
        rstd_ref[...] = jnp.broadcast_to(rstd, (rows, 128))
        y_ref[...] = (n * g_ref[...] + h_ref[...]).astype(BF16)

    ins = addend_specs(addends)
    ins.append((x_pieces, (1, rows, d), lambda _, t: (t[s * size], 0, 0)))
    ins += [whole(bias), whole(gain), whole(shift)]
    outs = [out_whole((rows, d), BF16), out_whole((rows, d), F32), out_whole((rows, 128), F32)]
    return call(body, "inner_norm", weight=2, prefetch=(table,), ins=ins, outs=outs)


def outer_norm(addends, n1, inner_gain, inner_shift, bias, gain, shift, cotangents, spots, buffer, s, count):
    rows, d = addends[0].shape[1:]
    n_add = len(addends)

    def body(spots_ref, *refs):
        n1_ref, g1_ref, h1_ref, b_ref, g_ref, h_ref, e_ref = refs[n_add : n_add + 7]
        res_ref, dz_ref, dzb_ref, sums_ref = refs[-4:]
        z = add_up(refs[:n_add]) + b_ref[...] + (n1_ref[...] * g1_ref[...] + h1_ref[...])
        n, rstd = normed(z)
        res_ref[0] = n * g_ref[...] + h_ref[...]
        e = e_ref[0].astype(F32)
        dz = norm_pull(e, n, rstd, g_ref[...])
        dz_ref[...] = dz
        dzb_ref[...] = dz.astype(BF16)
        sums_ref[0:1] = column_sum(dz)
        sums_ref[1:2] = column_sum(e * n)
        sums_ref[2:3] = column_sum(e)

    ins = addend_specs(addends)
    ins += [whole(a) for a in (n1, inner_gain, inner_shift, bias, gain, shift)]
    ins.append((cotangents, (1, rows, d), lambda _, t: (t[s], 0, 0)))
    aliases = {}
    if buffer is not None:
        aliases[len(ins)] = 0
        ins.append((buffer, None, None))
    outs = [
        ((count, rows, d), F32, (1, rows, d), lambda *_: (s, 0, 0)),
        out_whole((rows, d), F32),
        out_whole((rows, d), BF16),
        out_whole((8, d), F32),
    ]
    return call(
        body, "outer_norm", weight=2, prefetch=(spots,), ins=ins, outs=outs, aliases=aliases,
    )


def inner_norm_back(addends, dz, n1, rstd1, gain):
    rows, d = addends[0].shape[1:]
    n_add = len(addends)

    def body(*refs):
        dz_ref, n_ref, rstd_ref, g_ref, dr_ref, sums_ref = refs[n_add:]
        da = add_up(refs[:n_add]) + dz_ref[...]
        n = n_ref[...]
        dr = norm_pull(da, n, rstd_ref[:, 0:1], g_ref[...])
        dr_ref[...] = dr.astype(BF16)
        sums_ref[0:1] = column_sum(dr)
        sums_ref[1:2] = column_sum(da * n)
        sums_ref[2:3] = column_sum(da)

    ins = addend_specs(addends) + [whole(a) for a in (dz, n1, rstd1, gain)]
    outs = [out_whole((rows, d), BF16), out_whole((8, d), F32)]
    return call(body, "inner_norm_back", weight=2, ins=ins, outs=outs)


def feed_forward(blocks, expand, expand_bias, contract, buffers, s, count):
    size = len(blocks)
    rows, d = blocks[0].shape
    hidden = expand.shape[1]
    length = size * rows
    tile = min(256, hidden)

    def body(*refs):
        y_refs = refs[:size]
        we_ref, be_ref, wc_ref = refs[size : size + 3]
        y_out, g_out, slope_out = refs[-3 - size : -size]
        y = jnp.concatenate([r[...] for r in y_refs], axis=0)
        y_out[0] = y
        for at in range(0, hidden, tile):
            cols = slice(at, at + tile)
            u = nn(y, we_ref[:, cols]) + be_ref[:, cols]
            phi_sum, phi = erf_parts(u)
            g_out[0, :, cols] = (u * phi_sum).astype(BF16)
            slope_out[0, :, cols] = (phi_sum + u * phi).astype(BF16)
        write_rows(nn(g_out[0], wc_ref[...]), refs[-size:], size, rows)

    ins = [whole(b) for b in blocks] + [whole(a) for a in (expand, expand_bias, contract)]
    aliases = {}
    if buffers is not None:
        for number, b in enumerate(buffers):
            aliases[len(ins)] = number
            ins.append((b, None, None))
    outs = [
        ((count, length, w), BF16, (1, length, w), lambda *_: (s, 0, 0)) for w in (d, hidden, hidden)
    ] + partial_outs(size, rows, d)
    return call(
        body, "feed_forward", weight=8, ins=ins, outs=outs, aliases=aliases,
    )


def feed_back(blocks, expand, contract, slopes, buffers, s, count):
    size = len(blocks)
    rows, d = blocks[0].shape
    hidden = expand.shape[1]
    length = size * rows
    tile = min(256, hidden)

    def body(*refs):
        dz_refs = refs[:size]
        we_ref, wc_ref, slope_ref = refs[size : size + 3]
        sums_ref, dz_out, du_out = refs[-3 - size : -size]
        dz = jnp.concatenate([r[...] for r in dz_refs], axis=0)
        dz_out[0] = dz
        for at in range(0, hidden, tile):
            cols = slice(at, at + tile)
            du = (nt(dz, wc_ref[cols, :]) * slope_ref[0, :, cols].astype(F32)).astype(BF16)
            du_out[0, :, cols] = du
            sums_ref[:, cols] = column_sum(du.astype(F32))
        write_rows(nt(du_out[0], we_ref[...]), refs[-size:], size, rows)

    ins = [whole(b) for b in blocks] + [whole(expand), whole(contract)]
    ins.append((slopes, (1, length, hidden), lambda *_: (s, 0, 0)))
    aliases = {}
    if buffers is not None:
        for number, b in enumerate(buffers):
            aliases[len(ins)] = 1 + number
            ins.append((b, None, None))
    outs = [out_whole((1, hidden), F32)]
    outs += [((count, length, w), BF16, (1, length, w), lambda *_: (s, 0, 0)) for w in (d, hidden)]
    outs += partial_outs(size, rows, d)
    return call(
        body, "feed_back", weight=5, ins=ins, outs=outs, aliases=aliases,
    )


def input_back(first, second, weights, k, size):
    rows = first.shape[1]
    d = weights[1].shape[0]
    width = weights[1].shape[1]

    def body(*refs):
        a_ref, b_ref, qw_ref, kw_ref, vw_ref = refs[:5]
        a = jnp.concatenate([a_ref[j] for j in range(size)], axis=0)
        b = jnp.concatenate([b_ref[j] for j in range(size)], axis=0)
        total = nt(a[:, :width], qw_ref[0])
        for m in (1, 2):
            total = total + nt(a[:, m * width : (m + 1) * width], qw_ref[m])
        total = total + nt(b[:, :width], qw_ref[3])
        total = total + nt(b[:, width : 2 * width], kw_ref[...])
        total = total + nt(b[:, 2 * width :], vw_ref[...])
        write_rows(total, refs[-size:], size, rows)

    block = (size, rows, 3 * width)
    ins = [(first, block, lambda *_: (k, 0, 0)), (second, block, lambda *_: (k, 0, 0))]
    ins += [whole(w) for w in weights]
    return call(
        body, "input_back", weight=4, ins=ins, outs=partial_outs(size, rows, d),
    )


def collect(blocks):
    rows, d = blocks[0].shape

    def body(*refs):
        for m in range(len(blocks)):
            refs[-1][m] = refs[m][...]

    outs = [out_whole((len(blocks), rows, d), BF16)]
    return call(body, "collect", ins=[whole(b) for b in blocks], outs=outs)[0]


def final_sum(addends, dr_pieces, buffer, k, count, size):
    rows, d = addends[0].shape[1:]
    n_add = len(addends)

    def body(*refs):
        refs[-1][0] = add_up(refs[: n_add + 1])

    ins = addend_specs(addends)
    ins.append((dr_pieces, (1, rows, d), lambda *_: (k * size, 0, 0)))
    aliases = {}
    if buffer is not None:
        aliases[len(ins)] = 0
        ins.append((buffer, None, None))
    outs = [((count, rows, d), F32, (1, rows, d), lambda *_: (k, 0, 0))]
    return call(body, "final_sum", ins=ins, outs=outs, aliases=aliases)[0]


def body(
    dp, tensor, tokens, token_kinds, segment_ids, cotangent, query_weight, query_bias, key_weight, key_bias,
    value_weight, value_bias, output_weight, output_bias, inner_gain, inner_shift, expand_weight, expand_bias,
    contract_weight, contract_bias, outer_gain, outer_shift,
):
    count, length = token_kinds.shape
    d = tokens.shape[1]
    rows = length // tensor
    me = lax.axis_index("tensor")
    width = key_weight.shape[2]
    hidden = expand_weight.shape[2]

    devices = np.arange(tensor)
    piece_at = np.array(
        [[[o * count + k for o in devices ^ r] for k in range(count)] for r in range(tensor)], np.int32
    )
    seq_piece = np.array(
        [[[s * tensor + b for b in devices ^ r] for s in range(count)] for r in range(tensor)], np.int32
    )
    table_of = np.array(
        [[(g % count) * tensor + ((g // count) ^ r) for g in seq_piece[r].reshape(-1)] for r in range(tensor)], np.int32
    )
    pick = lambda values: lax.dynamic_index_in_dim(jnp.asarray(values), me, 0, keepdims=False)
    table = pick(table_of)
    codes = (segment_ids * 2 + token_kinds).reshape(count * tensor, rows)
    order = np.concatenate([piece_at.reshape(tensor, -1), seq_piece.reshape(tensor, -1)], axis=1)
    codes = codes[pick(order)].reshape(2, count, 1, length)
    piece_codes, seq_codes = codes[0], codes[1]

    weights = (query_weight[0], key_weight[0], value_weight[0])
    biases = jnp.concatenate([query_bias[0], key_bias, value_bias], axis=0).astype(F32)
    expand, contract = expand_weight[0], contract_weight[0]
    expand_bias32 = expand_bias.astype(F32)
    out_proj = output_weight[0]
    Order.mark = None

    gathered = [gather_blocks(tokens[k * rows : (k + 1) * rows], tensor) for k in range(count)]
    pieces = None
    for k in range(count):
        pieces = project_rows(gathered[k], piece_codes, weights, biases, pieces, k, count)
    qkv, x_pieces = pieces

    rounds = piece_rounds(count, tensor)
    arrived = []
    spots_of = np.zeros((tensor, count), np.int32)
    for number, chosen in enumerate(rounds):
        sends = pick(np.array([g % count for _, g in chosen], np.int32))
        block = lax.dynamic_slice_in_dim(cotangent, sends * rows, rows, 0)
        perm = [(u, v) for u, (v, _) in enumerate(chosen)]
        if any(u != v for u, v in perm):
            block = lax.ppermute(block, "tensor", perm)
        arrived.append(block)
        for v, g in chosen:
            spots_of[v, g // tensor] = number
    spots = pick(spots_of)
    hold = {"cotangents": collect(arrived)}

    def stage(run, finish, before):
        for s in range(count):
            partial = run(s)
            received = scatter_start(partial[1::2], tensor)
            if s:
                finish(s - 1)
            elif before is not None:
                before(count - 1)
            hold["addends", s] = scatter_rest(partial[0::2], received, tensor)

    def run_attend(s):
        hold["context", s], hold["lse", s], *partial = attend(qkv, table, s, seq_codes, out_proj, tensor, rows)
        return partial

    def finish_attend(s):
        y, hold["n1", s], hold["rstd1", s] = inner_norm(
            hold["addends", s], x_pieces, table, s, output_bias, inner_gain, inner_shift, tensor
        )
        hold["y", s] = gather_blocks(y, tensor)

    def run_forward(s):
        out = feed_forward(hold["y", s], expand, expand_bias32, contract, hold.get("kept"), s, count)
        hold["kept"] = out[:3]
        return out[3:]

    def finish_forward(s):
        hold["results"], hold["dz", s], dzb, hold["outer", s] = outer_norm(
            hold["addends", s], hold["n1", s], inner_gain, inner_shift, contract_bias, outer_gain, outer_shift,
            hold["cotangents"], spots, hold.get("results"), s, count,
        )
        hold["dzb", s] = gather_blocks(dzb, tensor)

    def run_back(s):
        out = feed_back(hold["dzb", s], expand, contract, hold["kept"][2], hold.get("back"), s, count)
        hold["expand_bias", s], hold["back"] = out[0], out[1:3]
        return out[3:]

    def finish_back(s):
        drb, hold["inner", s] = inner_norm_back(
            hold["addends", s], hold["dz", s], hold["n1", s], hold["rstd1", s], inner_gain
        )
        hold["drb", s] = gather_blocks(drb, tensor)

    stage(run_attend, finish_attend, None)
    stage(run_forward, finish_forward, finish_attend)
    stage(run_back, finish_back, finish_forward)
    y_all, g_all, _ = hold["kept"]
    dz_all, du_all = hold["back"]

    shapes = [(4, d, width), (1, d, width), (1, d, width), (1, width, d), (1, d, hidden), (1, hidden, d)]
    grads = {}
    flat = lambda a: a.reshape(-1, a.shape[-1])
    bits = list(range(dp.bit_length() - 1))
    swapped = bits[1::-1] + bits[2:]
    sum_of = lambda array, order, layout, name: DpSum(array, order, dp, grads, shapes, layout, name)
    steps = lambda *sums: [one.step() for one in sums]
    of_contract = sum_of(tn(flat(g_all), flat(dz_all)).astype(BF16), bits, [(5, 0, 1, 0, d)], "contract")
    of_expand = sum_of(tn(flat(y_all), flat(du_all)).astype(BF16), swapped, [(4, 0, 1, 0, hidden)], "expand")

    kept, output_sum = None, None
    for s in range(count):
        *kept, output_sum, hold["bias", s] = attend_back(
            qkv, table, s, seq_codes, out_proj, hold["context", s], hold["lse", s], hold["drb", s], kept, output_sum, count
        )
        if s == 0:
            finish_back(count - 1)
        steps(of_contract, of_expand)
    first, second, dr_pieces = kept

    x_flat = flat(x_pieces)
    of_first = sum_of(tn(x_flat, flat(first)).astype(BF16), bits, [(0, 0, 3, 0, width)], "first")
    layout = [(0, 3, 1, 0, width), (1, 0, 1, width, width), (2, 0, 1, 2 * width, width)]
    of_second = sum_of(tn(x_flat, flat(second)).astype(BF16), swapped, layout, "second")
    of_output = sum_of(output_sum.astype(BF16), bits, [(3, 0, 1, 0, d)], "output")

    for k in range(count):
        partial = input_back(first, second, weights, k, tensor)
        hold["addends", k] = scatter_rest(partial[0::2], scatter_start(partial[1::2], tensor), tensor)
    done = len(bits) * 2
    while of_first.at < done:
        for one in (of_first, of_second, of_output, of_contract, of_expand):
            if one.at < done:
                one.step()

    result = {}
    for number, chosen in enumerate(rounds):
        sends, lands = np.zeros(tensor, np.int32), np.zeros(tensor, np.int32)
        for u, (v, g) in enumerate(chosen):
            sends[v], lands[u] = g // tensor, g % count
        block = lax.dynamic_index_in_dim(hold["results"], pick(sends), 0, keepdims=False)
        perm = [(v, u) for u, (v, _) in enumerate(chosen)]
        if any(u != v for u, v in perm):
            block = lax.ppermute(block.astype(BF16), "tensor", perm)
        place(result, [(1, count * rows, d)], block, pick(lands).reshape(1), [(0, 0, 1, 0, d)], "place_result")

    upstream = None
    for k in range(count):
        upstream = final_sum(hold["addends", k], dr_pieces, upstream, k, count, tensor)

    total = lambda name: sum(hold[name, s] for s in range(count))
    norms = jnp.concatenate([total("outer")[:3], total("inner")[:3]], axis=0)
    norms = doubling_sum(norms, "tensor", tensor)
    top = jnp.concatenate([norms, jnp.pad(total("expand_bias"), ((0, 0), (0, d - hidden)))], axis=0)
    packed = jnp.concatenate([top, jnp.pad(total("bias")[:6], ((0, 1), (0, 0)))], axis=1)
    packed = doubling_sum(packed, "dp", dp)

    return (
        result[0].reshape(-1, d),
        upstream.reshape(-1, d),
        grads[0][None],
        packed[None, 0:4, d:],
        grads[1],
        packed[4:5, d:],
        grads[2],
        packed[5:6, d:],
        grads[3],
        packed[3:4, :d],
        packed[4:5, :d],
        packed[5:6, :d],
        grads[4],
        packed[6:7, :hidden],
        grads[5],
        packed[0:1, :d],
        packed[1:2, :d],
        packed[2:3, :d],
    )


def solution(mesh):
    rows, both = P("dp", None), P(("dp", "tensor"), None)
    columns = lambda dims: P(*[None] * (dims - 1), "tensor")
    down = P(None, "tensor", None)
    weight_specs = [columns(4), columns(3), columns(3), columns(2), columns(3), columns(2), down]
    ffn_specs = [columns(3), columns(2), down]
    return jax.shard_map(
        functools.partial(body, mesh.shape["dp"], mesh.shape["tensor"]),
        mesh=mesh,
        in_specs=(both, rows, rows, both, *weight_specs, P(), P(), P(), *ffn_specs, P(), P(), P()),
        out_specs=(both, both, *weight_specs, P(), P(), P(), *ffn_specs, P(), P(), P()),
        check_vma=False,
    )
```

time: 581 us -> 505 us (0.87)
  waiting for transfers between devices: 209 us -> 138 us
  Pallas kernels: 175 us -> 193 us
  other arithmetic: 18.5 us -> 5.07 us
  starting transfers between devices: 90.9 us -> 81.1 us
    ppermute x95 -> x107, waiting for transfers between devices: 206 us -> 138 us  [swap(): return lax.ppermute(array, axis, [(r, r ^ bit) for r in range(size)])]
    pallas_call x53 -> x76, Pallas kernels: 175 us -> 193 us  [call(): pl.pallas_call(inner, grid_spec=pltpu.PrefetchScalarGridSpec(num_scalar_p...]
    ppermute x95 -> x107, starting transfers between devices: 86.8 us -> 77.3 us  [swap(): return lax.ppermute(array, axis, [(r, r ^ bit) for r in range(size)])]
    unnamed x186 -> x258, local copies, waits for them, and re-layouts: 23.4 us -> 31.6 us
    another operation x17 -> x9, other arithmetic: 8.43 us -> 1.27 us  [the longest x4 0.9 us: join(): spots = jnp.stack([self.where(d) for d in came]).astype(jnp.int32)]
    convert_element_type x16 -> x1, other arithmetic: 6.61 us -> 0.07 us  [body(): output_sum.astype(BF16)]
  transfers between devices with their start and end apart: 99 -> 111, of which waited for: 38 -> 29; matrix products, arithmetic and copies ran while one was open for 11% -> 8% of each run, Pallas kernels for 28% -> 35%
where the time goes in v2:
time: 505 us; the launch traced here: 495 us
  Pallas kernels  193 us (38%)
  waiting for transfers between devices  138 us (27%)
  starting transfers between devices  81.1 us (16%)
  local copies, waits for them, and re-layouts  49.5 us (10%)
  matrix products  19.9 us (4%)
  between operations  9.51 us (2%)
  other arithmetic  5.07 us (1%)
    pallas_call x76, Pallas kernels, call(): pl.pallas_call(inner, grid_spec=pltpu.PrefetchScalarGridSpec(num_scalar_p...  193 us
    ppermute x107, waiting for transfers between devices, swap(): return lax.ppermute(array, axis, [(r, r ^ bit) for r in range(size)])  138 us
    ppermute x107, starting transfers between devices, swap(): return lax.ppermute(array, axis, [(r, r ^ bit) for r in range(size)])  77.3 us
    unnamed x258, local copies, waits for them, and re-layouts  31.6 us
    dot_general x4, matrix products, tn(): lax.dot_general(a, b, (((0,), (0,)), ((), ())), preferred_element_type=F32)  19.9 us
  transfers between devices with their start and end apart: 111, of which 29 were waited for; matrix products, arithmetic and copies ran while one was open for 8% of the time, Pallas kernels for 35%

profile of v2, /device:TPU:0, one launch (start us, length us, event | category | flops | bytes accessed | tf_op | source)
XLA Modules:
  0.0 495.4 jit_solution(12542059240102579808)
XLA Ops:
  2.9 3.0 collective-permute-start.7
  16.3 5.5 %collective-permute-done.4.refs_2_ = bf16[160,1024]{1,0:T(8,128)(2,1)} collective-permute-done((bf16[160,1024]{1,0:T(8,128)(2,1)}, bf16[160,1024]{1,0:T(8,128)(2,1)}, u32[]{:S(2)}, u32[]{:S(2)}) %collective-permute-start.4) | collective-permute-done | bytes 327712 | tf_op jit(solution)/shard_map/ppermute | solution.py:84
  23.0 5.0 %collective-permute-done.1.refs_2_ = bf16[160,1024]{1,0:T(8,128)(2,1)} collective-permute-done((bf16[160,1024]{1,0:T(8,128)(2,1)S(1)}, bf16[160,1024]{1,0:T(8,128)(2,1)}, u32[]{:S(2)}, u32[]{:S(2)}) %collective-permute-start.1) | collective-permute-done | bytes 327712 | tf_op jit(solution)/shard_map/ppermute | solution.py:84
  29.7 4.9 project_rows.3
  35.2 5.0 %project_rows.4 = (bf16[12,160,1024]{2,1,0:T(8,128)(2,1)}, bf16[12,160,1024]{2,1,0:T(8,128)(2,1)}, f32[8,128]{1,0:T(8,128)S(1)}) custom-call(bf16[160,1024]{1,0:T(8,128)(2,1)} %get-tuple-element.579.refs_0_, bf16[160,1024]{1,0:T(8,128)(2,1)} %collective-permute-done.3.refs_1_, ...), custom_call_target="tpu_custom_call", output_to_operand_aliasing={{0}: (9, {}), {1}: (10, {})} | custom-call | flops 2500000000 | bytes 1 | tf_op jit(solution)/shard_map/project_rows/pallas_call | solution.py:55
  40.2 4.7 project_rows.5
  48.1 6.4 %attend.3 = (bf16[640,256]{1,0:T(8,128)(2,1)S(1)}, f32[8,640]{1,0:T(8,128)S(1)}, bf16[160,1024]{1,0:T(8,128)(2,1)S(1)}, bf16[160,1024]{1,0:T(8,128)(2,1)S(1)}, b...) custom-call(s32[12]{0:T(128)S(1)} %fusion.5.refs_0_, ...), custom_call_target="tpu_custom_call" | custom-call | flops 3500000000 | bytes 1 | tf_op jit(solution)/shard_map/attend/pallas_call | solution.py:55
  56.7 6.7 %attend.4 = (bf16[640,256]{1,0:T(8,128)(2,1)S(1)}, f32[8,640]{1,0:T(8,128)S(1)}, bf16[160,1024]{1,0:T(8,128)(2,1)S(1)}, bf16[160,1024]{1,0:T(8,128)(2,1)S(1)}, b...) custom-call(s32[12]{0:T(128)S(1)} %fusion.5.refs_0_, ...), custom_call_target="tpu_custom_call" | custom-call | flops 3500000000 | bytes 1 | tf_op jit(solution)/shard_map/attend/pallas_call | solution.py:55
  69.3 6.4 %attend.5 = (bf16[640,256]{1,0:T(8,128)(2,1)S(1)}, f32[8,640]{1,0:T(8,128)S(1)}, bf16[160,1024]{1,0:T(8,128)(2,1)S(1)}, bf16[160,1024]{1,0:T(8,128)(2,1)S(1)}, b...) custom-call(s32[12]{0:T(128)S(1)} %fusion.5.refs_0_, ...), custom_call_target="tpu_custom_call" | custom-call | flops 3500000000 | bytes 1 | tf_op jit(solution)/shard_map/attend/pallas_call | solution.py:55
  76.9 6.3 %collective-permute-done.21.refs_2_ = bf16[160,1024]{1,0:T(8,128)(2,1)S(1)} collective-permute-done((bf16[160,1024]{1,0:T(8,128)(2,1)S(1)}, bf16[160,1024]{1,0:T(8,128)(2,1)S(1)}, u32[]{:S(2)}, u32[]{:S(2)}) %collective-permute-start.21) | collective-permute-done | bytes 327712 | tf_op jit(solution)/shard_map/ppermute | solution.py:84
  86.9 6.9 %feed_forward.3 = (bf16[3,640,1024]{2,1,0:T(8,128)(2,1)}, bf16[3,640,1024]{2,1,0:T(8,128)(2,1)}, bf16[3,640,1024]{2,1,0:T(8,128)(2,1)}, bf16[160,1024]{1,0:T(8,1...) custom-call(bf16[160,1024]{1,0:T(8,128)(2,1)S(1)} %get-tuple-element, ...), custom_call_target="tpu_custom_call" | custom-call | flops 4000000000 | bytes 1 | tf_op jit(solution)/shard_map/feed_forward/pallas_call | solution.py:55
  94.4 7.2 %collective-permute-done.27.refs_2_ = bf16[160,1024]{1,0:T(8,128)(2,1)S(1)} collective-permute-done((bf16[160,1024]{1,0:T(8,128)(2,1)S(1)}, bf16[160,1024]{1,0:T(8,128)(2,1)S(1)}, u32[]{:S(2)}, u32[]{:S(2)}) %collective-permute-start.27) | collective-permute-done | bytes 327712 | tf_op jit(solution)/shard_map/ppermute | solution.py:84
  105.9 6.8 %feed_forward.4 = (bf16[3,640,1024]{2,1,0:T(8,128)(2,1)}, bf16[3,640,1024]{2,1,0:T(8,128)(2,1)}, bf16[3,640,1024]{2,1,0:T(8,128)(2,1)}, bf16[160,1024]{1,0:T(8,1...) custom-call(bf16[160,1024]{1,0:T(8,128)(2,1)S(1)} %get-tuple-element, ...), custom_call_target="tpu_custom_call", output_to_operand_aliasing={{0}: (7, {}), {1}: (8, {}), {2}: (9, {})} | custom-call | flops 4000000000 | bytes 1 | tf_op jit(solution)/shard_map/feed_forward/pallas_call | solution.py:55
  115.7 4.9 collective-permute-done.32
  124.1 7.2 %feed_forward.5 = (bf16[3,640,1024]{2,1,0:T(8,128)(2,1)}, bf16[3,640,1024]{2,1,0:T(8,128)(2,1)}, bf16[3,640,1024]{2,1,0:T(8,128)(2,1)}, bf16[160,1024]{1,0:T(8,1...) custom-call(bf16[160,1024]{1,0:T(8,128)(2,1)} %get-tuple-element.330, ...), custom_call_target="tpu_custom_call", output_to_operand_aliasing={{0}: (7, {}), {1}: (8, {}), {2}: (9, {})} | custom-call | flops 4000000000 | bytes 1 | tf_op jit(solution)/shard_map/feed_forward/pallas_call | solution.py:55
  131.8 6.1 %collective-permute-done.39.refs_2_ = bf16[160,1024]{1,0:T(8,128)(2,1)S(1)} collective-permute-done((bf16[160,1024]{1,0:T(8,128)(2,1)S(1)}, bf16[160,1024]{1,0:T(8,128)(2,1)S(1)}, u32[]{:S(2)}, u32[]{:S(2)}) %collective-permute-start.39) | collective-permute-done | bytes 327712 | tf_op jit(solution)/shard_map/ppermute | solution.py:84
  141.9 5.5 %feed_back.3 = (f32[1,1024]{1,0:T(1,128)S(1)}, bf16[3,640,1024]{2,1,0:T(8,128)(2,1)}, bf16[3,640,1024]{2,1,0:T(8,128)(2,1)}, bf16[160,1024]{1,0:T(8,128)(2,1)S(1...) custom-call(bf16[160,1024]{1,0:T(8,128)(2,1)S(1)} %get-tuple-element, ...), custom_call_target="tpu_custom_call" | custom-call | flops 2500000000 | bytes 1 | tf_op jit(solution)/shard_map/feed_back/pallas_call | solution.py:55
  150.3 6.1 %collective-permute-done.37 = bf16[160,1024]{1,0:T(8,128)(2,1)S(1)} collective-permute-done((bf16[160,1024]{1,0:T(8,128)(2,1)S(1)}, bf16[160,1024]{1,0:T(8,128)(2,1)S(1)}, u32[]{:S(2)}, u32[]{:S(2)}) %collective-permute-start.37) | collective-permute-done | bytes 327712 | tf_op jit(solution)/shard_map/ppermute | solution.py:84
  160.6 5.6 %feed_back.4 = (f32[1,1024]{1,0:T(1,128)S(1)}, bf16[3,640,1024]{2,1,0:T(8,128)(2,1)}, bf16[3,640,1024]{2,1,0:T(8,128)(2,1)}, bf16[160,1024]{1,0:T(8,128)(2,1)S(1...) custom-call(bf16[160,1024]{1,0:T(8,128)(2,1)S(1)} %get-tuple-element, ...), custom_call_target="tpu_custom_call", output_to_operand_aliasing={{1}: (7, {}), {2}: (8, {})} | custom-call | flops 2500000000 | bytes 1 | tf_op jit(solution)/shard_map/feed_back/pallas_call | solution.py:55
  169.6 4.0 collective-permute-done.52
  183.5 5.1 %feed_back.5 = (f32[1,1024]{1,0:T(1,128)S(1)}, bf16[3,640,1024]{2,1,0:T(8,128)(2,1)}, bf16[3,640,1024]{2,1,0:T(8,128)(2,1)}, bf16[160,1024]{1,0:T(8,128)(2,1)S(1...) custom-call(bf16[160,1024]{1,0:T(8,128)(2,1)S(1)} %get-tuple-element, ...), custom_call_target="tpu_custom_call", output_to_operand_aliasing={{1}: (7, {}), {2}: (8, {})} | custom-call | flops 2500000000 | bytes 1 | tf_op jit(solution)/shard_map/feed_back/pallas_call | solution.py:55
  189.4 8.0 %bitcast_convert_fusion.refs_1_ = bf16[1024,1024]{1,0:T(8,128)(2,1)S(1)} fusion(bf16[3,640,1024]{2,1,0:T(8,128)(2,1)} %get-tuple-element.422, bf16[3,640,1024]{2,1,0:T(8,128)(2,1)} %get-tuple-element.423), kind=kOutput, calls=%fused_computation.1 | convolution fusion | flops 4027580416 | bytes 9961472 | tf_op jit(solution)/shard_map/dot_general | solution.py:29
  197.5 4.8 bitcast_convert_fusion.1.refs_1_
  211.5 13.5 %attend_back.3 = (bf16[12,160,768]{2,1,0:T(8,128)(2,1)S(1)}, bf16[12,160,768]{2,1,0:T(8,128)(2,1)}, bf16[12,160,1024]{2,1,0:T(8,128)(2,1)}, f32[256,1024]{1,0:T(...) custom-call(s32[12]{0:T(128)S(1)} %fusion.5.refs_0_, ...), custom_call_target="tpu_custom_call" | custom-call | flops 6499999744 | bytes 1 | tf_op jit(solution)/shard_map/attend_back/pallas_call | solution.py:55
  231.2 8.6 %collective-permute-done.62.refs_7_ = bf16[160,1024]{1,0:T(8,128)(2,1)S(1)} collective-permute-done((bf16[160,1024]{1,0:T(8,128)(2,1)}, bf16[160,1024]{1,0:T(8,128)(2,1)S(1)}, u32[]{:S(2)}, u32[]{:S(2)}) %collective-permute-start.62) | collective-permute-done | bytes 327712 | tf_op jit(solution)/shard_map/ppermute | solution.py:84
  248.1 13.8 %attend_back.4 = (bf16[12,160,768]{2,1,0:T(8,128)(2,1)}, bf16[12,160,768]{2,1,0:T(8,128)(2,1)}, bf16[12,160,1024]{2,1,0:T(8,128)(2,1)}, f32[256,1024]{1,0:T(8,12...) custom-call(s32[12]{0:T(128)S(1)} %fusion.5.refs_0_, ...), custom_call_target="tpu_custom_call", output_to_operand_aliasing={{0}: (14, {}), {1}: (15, {}), {2}: (16, {})} | custom-call | flops 6499999744 | bytes 1 | tf_op jit(solution)/shard_map/attend_back/pallas_call | solution.py:55
  262.6 2.7 collective-permute-start.75
  266.3 14.0 %attend_back.5 = (bf16[12,160,768]{2,1,0:T(8,128)(2,1)}, bf16[12,160,768]{2,1,0:T(8,128)(2,1)}, bf16[12,160,1024]{2,1,0:T(8,128)(2,1)}, f32[256,1024]{1,0:T(8,12...) custom-call(s32[12]{0:T(128)S(1)} %fusion.5.refs_0_, ...), custom_call_target="tpu_custom_call", output_to_operand_aliasing={{0}: (14, {}), {1}: (15, {}), {2}: (16, {})} | custom-call | flops 6499999744 | bytes 1 | tf_op jit(solution)/shard_map/attend_back/pallas_call | solution.py:55
  289.5 3.9 input_back.3
  294.1 3.5 bitcast_convert_fusion.2.refs_1_
  298.6 4.6 input_back.4
  305.2 3.5 bitcast_convert_fusion.3.refs_1_
  315.6 4.8 input_back.5
  324.8 3.4 collective-permute-start.83
  340.1 6.7 %collective-permute-done.83.refs_1_ = bf16[128,1024]{1,0:T(8,128)(2,1)} collective-permute-done((bf16[128,1024]{1,0:T(8,128)(2,1)}, bf16[128,1024]{1,0:T(8,128)(2,1)}, u32[]{:S(2)}, u32[]{:S(2)}) %collective-permute-start.83) | collective-permute-done | bytes 262176 | tf_op jit(solution)/shard_map/ppermute | solution.py:84
  348.8 3.4 collective-permute-done.82.refs_1_
  356.9 9.2 %collective-permute-done.79.refs_2_ = bf16[64,1024]{1,0:T(8,128)(2,1)S(1)} collective-permute-done((bf16[64,1024]{1,0:T(8,128)(2,1)S(1)}, bf16[64,1024]{1,0:T(8,128)(2,1)S(1)}, u32[]{:S(2)}, u32[]{:S(2)}) %collective-permute-start.79) | collective-permute-done | bytes 131104 | tf_op jit(solution)/shard_map/ppermute | solution.py:84
  374.8 4.3 collective-permute-start.86
  379.2 3.0 collective-permute-start.84
  382.1 17.8 %collective-permute-done.86.refs_2_ = bf16[128,768]{1,0:T(8,128)(2,1)S(1)} collective-permute-done((bf16[128,768]{1,0:T(8,128)(2,1)S(1)}, bf16[128,768]{1,0:T(8,128)(2,1)S(1)}, u32[]{:S(2)}, u32[]{:S(2)}) %collective-permute-start.86) | collective-permute-done | bytes 196640 | tf_op jit(solution)/shard_map/ppermute | solution.py:84
  401.3 3.4 collective-permute-start.91
  406.0 2.9 collective-permute-start.90
  412.7 2.4 expand_join.5
  415.1 4.9 collective-permute-done.91.refs_1_
  420.8 3.4 collective-permute-done.90.refs_1_
  453.1 14.8 %collective-permute-done.94.refs_1_ = bf16[64,1024]{1,0:T(8,128)(2,1)S(1)} collective-permute-done((bf16[64,1024]{1,0:T(8,128)(2,1)S(1)}, bf16[64,1024]{1,0:T(8,128)(2,1)S(1)}, u32[]{:S(2)}, u32[]{:S(2)}) %collective-permute-start.94) | collective-permute-done | bytes 131104 | tf_op jit(solution)/shard_map/ppermute | solution.py:84
  476.5 3.1 collective-permute-done.97.refs_1_
  490.5 3.5 collective-permute-done.101
  (562 shorter events, 194.7 us)
Async XLA Ops:
  5.9 16.6 %collective-permute-start.6 = (bf16[160,1024]{1,0:T(8,128)(2,1)}, bf16[160,1024]{1,0:T(8,128)(2,1)}, u32[]{:S(2)}, u32[]{:S(2)}) collective-permute-start(bf16[160,1024]{1,0:T(8,128)(2,1)} %get-tuple-element.577.refs_0_), channel_id=1, source_target_pairs={{0,1},{1,0},{2,3},{3,2},{4,5},{5,4},{6,7},{7,6},{8,9},{9,8},{10,11... | collective-permute-start | bytes 983048 | tf_op jit(solution)/shard_map/ppermute | solution.py:84
  6.0 28.7 %collective-permute-start.3 = (bf16[160,1024]{1,0:T(8,128)(2,1)}, bf16[160,1024]{1,0:T(8,128)(2,1)}, u32[]{:S(2)}, u32[]{:S(2)}) collective-permute-start(bf16[160,1024]{1,0:T(8,128)(2,1)} %get-tuple-element.579.refs_0_), channel_id=1, source_target_pairs={{0,1},{1,0},{2,3},{3,2},{4,5},{5,4},{6,7},{7,6},{8,9},{9,8},{10,11... | collective-permute-start | bytes 983048 | tf_op jit(solution)/shard_map/ppermute | solution.py:84
  6.4 21.6 %collective-permute-start.1 = (bf16[160,1024]{1,0:T(8,128)(2,1)S(1)}, bf16[160,1024]{1,0:T(8,128)(2,1)}, u32[]{:S(2)}, u32[]{:S(2)}) collective-permute-start(bf16[160,1024]{1,0:T(8,128)(2,1)S(1)} %get-tuple-element.578.refs_0_), channel_id=1, source_target_pairs={{0,2},{1,3},{2,0},{3,1},{4,6},{5,7},{6,4},{7,5},{8,10},{9,11},{10,... | collective-permute-start | bytes 983048 | tf_op jit(solution)/shard_map/ppermute | solution.py:84
  22.4 17.7 %collective-permute-start = (bf16[160,1024]{1,0:T(8,128)(2,1)S(1)}, bf16[160,1024]{1,0:T(8,128)(2,1)S(1)}, u32[]{:S(2)}, u32[]{:S(2)}) collective-permute-start(bf16[160,1024]{1,0:T(8,128)(2,1)S(1)} %get-tuple-element.578.refs_0_), channel_id=1, source_target_pairs={{0,1},{1,0},{2,3},{3,2},{4,5},{5,4},{6,7},{7,6},{8,9},{9,8},{10,11... | collective-permute-start | bytes 983048 | tf_op jit(solution)/shard_map/ppermute | solution.py:84
  27.9 17.0 %collective-permute-start.10 = (bf16[160,1024]{1,0:T(8,128)(2,1)S(1)}, bf16[160,1024]{1,0:T(8,128)(2,1)S(1)}, u32[]{:S(2)}, u32[]{:S(2)}) collective-permute-start(bf16[160,1024]{1,0:T(8,128)(2,1)S(1)} %get-tuple-element.574), channel_id=1, source_target_pairs={{0,2},{1,3},{2,0},{3,1},{4,6},{5,7},{6,4},{7,5},{8,10},{9,11},{10,... | collective-permute-start | bytes 983048 | tf_op jit(solution)/shard_map/ppermute | solution.py:833
  64.1 19.1 %collective-permute-start.17 = (bf16[160,1024]{1,0:T(8,128)(2,1)S(1)}, bf16[160,1024]{1,0:T(8,128)(2,1)S(1)}, u32[]{:S(2)}, u32[]{:S(2)}) collective-permute-start(bf16[160,1024]{1,0:T(8,128)(2,1)S(1)} %get-tuple-element.322), channel_id=1, source_target_pairs={{0,1},{1,0},{2,3},{3,2},{4,5},{5,4},{6,7},{7,6},{8,9},{9,8},{10,11... | collective-permute-start | bytes 983048 | tf_op jit(solution)/shard_map/ppermute | solution.py:84
  67.2 16.6 %collective-permute-start.18 = (bf16[160,1024]{1,0:T(8,128)(2,1)S(1)}, bf16[160,1024]{1,0:T(8,128)(2,1)S(1)}, u32[]{:S(2)}, u32[]{:S(2)}) collective-permute-start(bf16[160,1024]{1,0:T(8,128)(2,1)S(1)} %get-tuple-element.323), channel_id=1, source_target_pairs={{0,2},{1,3},{2,0},{3,1},{4,6},{5,7},{6,4},{7,5},{8,10},{9,11},{10,... | collective-permute-start | bytes 983048 | tf_op jit(solution)/shard_map/ppermute | solution.py:84
  83.2 18.4 %collective-permute-start.15 = (bf16[160,1024]{1,0:T(8,128)(2,1)S(1)}, bf16[160,1024]{1,0:T(8,128)(2,1)S(1)}, u32[]{:S(2)}, u32[]{:S(2)}) collective-permute-start(bf16[160,1024]{1,0:T(8,128)(2,1)S(1)} %get-tuple-element.318), channel_id=1, source_target_pairs={{0,1},{1,0},{2,3},{3,2},{4,5},{5,4},{6,7},{7,6},{8,9},{9,8},{10,11... | collective-permute-start | bytes 983048 | tf_op jit(solution)/shard_map/ppermute | solution.py:84
  84.8 17.2 %collective-permute-start.19 = (bf16[160,1024]{1,0:T(8,128)(2,1)S(1)}, bf16[160,1024]{1,0:T(8,128)(2,1)S(1)}, u32[]{:S(2)}, u32[]{:S(2)}) collective-permute-start(bf16[160,1024]{1,0:T(8,128)(2,1)S(1)} %get-tuple-element.326), channel_id=1, source_target_pairs={{0,2},{1,3},{2,0},{3,1},{4,6},{5,7},{6,4},{7,5},{8,10},{9,11},{10,... | collective-permute-start | bytes 983048 | tf_op jit(solution)/shard_map/ppermute | solution.py:84
  115.2 22.7 %collective-permute-start.35 = (bf16[160,1024]{1,0:T(8,128)(2,1)S(1)}, bf16[160,1024]{1,0:T(8,128)(2,1)S(1)}, u32[]{:S(2)}, u32[]{:S(2)}) collective-permute-start(bf16[160,1024]{1,0:T(8,128)(2,1)S(1)} %get-tuple-element.357), channel_id=1, source_target_pairs={{0,1},{1,0},{2,3},{3,2},{4,5},{5,4},{6,7},{7,6},{8,9},{9,8},{10,11... | collective-permute-start | bytes 983048 | tf_op jit(solution)/shard_map/ppermute | solution.py:84
  169.3 35.5 %collective-permute-start.55 = (bf16[160,1024]{1,0:T(8,128)(2,1)}, bf16[160,1024]{1,0:T(8,128)(2,1)S(1)}, u32[]{:S(2)}, u32[]{:S(2)}) collective-permute-start(bf16[160,1024]{1,0:T(8,128)(2,1)} %copy-done.100), channel_id=1, source_target_pairs={{0,1},{1,0},{2,3},{3,2},{4,5},{5,4},{6,7},{7,6},{8,9},{9,8},{10,11... | collective-permute-start | bytes 983048 | tf_op jit(solution)/shard_map/ppermute | solution.py:84
  179.3 23.1 %collective-permute-start.59 = (bf16[160,1024]{1,0:T(8,128)(2,1)S(1)}, bf16[160,1024]{1,0:T(8,128)(2,1)S(1)}, u32[]{:S(2)}, u32[]{:S(2)}) collective-permute-start(bf16[160,1024]{1,0:T(8,128)(2,1)S(1)} %get-tuple-element.405.refs_5_), channel_id=1, source_target_pairs={{0,2},{1,3},{2,0},{3,1},{4,6},{5,7},{6,4},{7,5},{8,10},{9,11},{10,... | collective-permute-start | bytes 983048 | tf_op jit(solution)/shard_map/ppermute | solution.py:84
  180.6 28.8 %collective-permute-start.58 = (bf16[160,1024]{1,0:T(8,128)(2,1)S(1)}, bf16[160,1024]{1,0:T(8,128)(2,1)S(1)}, u32[]{:S(2)}, u32[]{:S(2)}) collective-permute-start(bf16[160,1024]{1,0:T(8,128)(2,1)S(1)} %get-tuple-element.405.refs_5_), channel_id=1, source_target_pairs={{0,1},{1,0},{2,3},{3,2},{4,5},{5,4},{6,7},{7,6},{8,9},{9,8},{10,11... | collective-permute-start | bytes 983048 | tf_op jit(solution)/shard_map/ppermute | solution.py:84
  182.6 22.4 %collective-permute-start.56 = (bf16[160,1024]{1,0:T(8,128)(2,1)S(1)}, bf16[160,1024]{1,0:T(8,128)(2,1)S(1)}, u32[]{:S(2)}, u32[]{:S(2)}) collective-permute-start(bf16[160,1024]{1,0:T(8,128)(2,1)S(1)} %get-tuple-element.397), channel_id=1, source_target_pairs={{0,2},{1,3},{2,0},{3,1},{4,6},{5,7},{6,4},{7,5},{8,10},{9,11},{10,... | collective-permute-start | bytes 983048 | tf_op jit(solution)/shard_map/ppermute | solution.py:84
  189.2 18.6 %collective-permute-start.54 = (bf16[160,1024]{1,0:T(8,128)(2,1)S(1)}, bf16[160,1024]{1,0:T(8,128)(2,1)S(1)}, u32[]{:S(2)}, u32[]{:S(2)}) collective-permute-start(bf16[160,1024]{1,0:T(8,128)(2,1)S(1)} %get-tuple-element.394), channel_id=1, source_target_pairs={{0,1},{1,0},{2,3},{3,2},{4,5},{5,4},{6,7},{7,6},{8,9},{9,8},{10,11... | collective-permute-start | bytes 983048 | tf_op jit(solution)/shard_map/ppermute | solution.py:84
  204.8 22.9 %collective-permute-start.53 = (bf16[160,1024]{1,0:T(8,128)(2,1)S(1)}, bf16[160,1024]{1,0:T(8,128)(2,1)S(1)}, u32[]{:S(2)}, u32[]{:S(2)}) collective-permute-start(bf16[160,1024]{1,0:T(8,128)(2,1)S(1)} %get-tuple-element.392), channel_id=1, source_target_pairs={{0,1},{1,0},{2,3},{3,2},{4,5},{5,4},{6,7},{7,6},{8,9},{9,8},{10,11... | collective-permute-start | bytes 983048 | tf_op jit(solution)/shard_map/ppermute | solution.py:84
  205.0 34.8 %collective-permute-start.68 = (bf16[512,1024]{1,0:T(8,128)(2,1)}, bf16[512,1024]{1,0:T(8,128)(2,1)}, u32[]{:S(2)}, u32[]{:S(2)}) collective-permute-start(bf16[512,1024]{1,0:T(8,128)(2,1)} %constant_dynamic-slice_fusion.1), channel_id=1, source_target_pairs={{0,4},{4,0},{8,12},{12,8},{16,20},{20,16},{24,28},{28,24},{1,5},{5... | collective-permute-start | bytes 3145736 | tf_op jit(solution)/shard_map/ppermute | solution.py:84
  207.7 36.2 %collective-permute-start.67 = (bf16[512,1024]{1,0:T(8,128)(2,1)}, bf16[512,1024]{1,0:T(8,128)(2,1)}, u32[]{:S(2)}, u32[]{:S(2)}) collective-permute-start(bf16[512,1024]{1,0:T(8,128)(2,1)} %constant_dynamic-slice_fusion.2), channel_id=1, source_target_pairs={{0,8},{4,12},{8,0},{12,4},{16,24},{20,28},{24,16},{28,20},{1,9},{5... | collective-permute-start | bytes 3145736 | tf_op jit(solution)/shard_map/ppermute | solution.py:84
  209.4 18.2 %collective-permute-start.57 = (bf16[160,1024]{1,0:T(8,128)(2,1)S(1)}, bf16[160,1024]{1,0:T(8,128)(2,1)S(1)}, u32[]{:S(2)}, u32[]{:S(2)}) collective-permute-start(bf16[160,1024]{1,0:T(8,128)(2,1)S(1)} %get-tuple-element.402), channel_id=1, source_target_pairs={{0,2},{1,3},{2,0},{3,1},{4,6},{5,7},{6,4},{7,5},{8,10},{9,11},{10,... | collective-permute-start | bytes 983048 | tf_op jit(solution)/shard_map/ppermute | solution.py:84
  210.7 20.1 %collective-permute-start.65 = (bf16[160,1024]{1,0:T(8,128)(2,1)}, bf16[160,1024]{1,0:T(8,128)(2,1)}, u32[]{:S(2)}, u32[]{:S(2)}) collective-permute-start(bf16[160,1024]{1,0:T(8,128)(2,1)} %get-tuple-element.413.refs_5_), channel_id=1, source_target_pairs={{0,2},{1,3},{2,0},{3,1},{4,6},{5,7},{6,4},{7,5},{8,10},{9,11},{10,... | collective-permute-start | bytes 983048 | tf_op jit(solution)/shard_map/ppermute | solution.py:84
  227.6 18.8 %collective-permute-start.64 = (bf16[160,1024]{1,0:T(8,128)(2,1)}, bf16[160,1024]{1,0:T(8,128)(2,1)}, u32[]{:S(2)}, u32[]{:S(2)}) collective-permute-start(bf16[160,1024]{1,0:T(8,128)(2,1)} %get-tuple-element.413.refs_5_), channel_id=1, source_target_pairs={{0,1},{1,0},{2,3},{3,2},{4,5},{5,4},{6,7},{7,6},{8,9},{9,8},{10,11... | collective-permute-start | bytes 983048 | tf_op jit(solution)/shard_map/ppermute | solution.py:84
  239.8 26.5 %collective-permute-start.61 = (bf16[160,1024]{1,0:T(8,128)(2,1)}, bf16[160,1024]{1,0:T(8,128)(2,1)S(1)}, u32[]{:S(2)}, u32[]{:S(2)}) collective-permute-start(bf16[160,1024]{1,0:T(8,128)(2,1)} %get-tuple-element.410.refs_5_), channel_id=1, source_target_pairs={{0,1},{1,0},{2,3},{3,2},{4,5},{5,4},{6,7},{7,6},{8,9},{9,8},{10,11... | collective-permute-start | bytes 983048 | tf_op jit(solution)/shard_map/ppermute | solution.py:84
  239.8 26.5 %collective-permute-start.63 = (bf16[160,1024]{1,0:T(8,128)(2,1)S(1)}, bf16[160,1024]{1,0:T(8,128)(2,1)S(1)}, u32[]{:S(2)}, u32[]{:S(2)}) collective-permute-start(bf16[160,1024]{1,0:T(8,128)(2,1)S(1)} %collective-permute-done.62.refs_7_), channel_id=1, source_target_pairs={{0,1},{1,0},{2,3},{3,2},{4,5},{5,4},{6,7},{7,6},{8,9},{9,8},{10,11... | collective-permute-start | bytes 983048 | tf_op jit(solution)/shard_map/ppermute | solution.py:84
  243.9 17.9 %collective-permute-start.70 = (bf16[256,1024]{1,0:T(8,128)(2,1)S(1)}, bf16[256,1024]{1,0:T(8,128)(2,1)S(1)}, u32[]{:S(2)}, u32[]{:S(2)}) collective-permute-start(bf16[256,1024]{1,0:T(8,128)(2,1)S(1)} %get-tuple-element.434), channel_id=1, source_target_pairs={{0,8},{4,12},{8,0},{12,4},{16,24},{20,28},{24,16},{28,20},{1,9},{5... | collective-permute-start | bytes 1572872 | tf_op jit(solution)/shard_map/ppermute | solution.py:84
  246.5 18.7 %collective-permute-start.69 = (bf16[256,1024]{1,0:T(8,128)(2,1)S(1)}, bf16[256,1024]{1,0:T(8,128)(2,1)S(1)}, u32[]{:S(2)}, u32[]{:S(2)}) collective-permute-start(bf16[256,1024]{1,0:T(8,128)(2,1)S(1)} %get-tuple-element.432), channel_id=1, source_target_pairs={{0,4},{4,0},{8,12},{12,8},{16,20},{20,16},{24,28},{28,24},{1,5},{5... | collective-permute-start | bytes 1572872 | tf_op jit(solution)/shard_map/ppermute | solution.py:84
  262.6 21.0 %collective-permute-start.75 = (bf16[128,1024]{1,0:T(8,128)(2,1)S(1)}, bf16[128,1024]{1,0:T(8,128)(2,1)S(1)}, u32[]{:S(2)}, u32[]{:S(2)}) collective-permute-start(bf16[128,1024]{1,0:T(8,128)(2,1)S(1)} %get-tuple-element.444), channel_id=1, source_target_pairs={{0,16},{4,20},{8,24},{12,28},{16,0},{20,4},{24,8},{28,12},{1,17},{... | collective-permute-start | bytes 786440 | tf_op jit(solution)/shard_map/ppermute | solution.py:84
  265.9 22.1 %collective-permute-start.74 = (bf16[128,1024]{1,0:T(8,128)(2,1)S(1)}, bf16[128,1024]{1,0:T(8,128)(2,1)S(1)}, u32[]{:S(2)}, u32[]{:S(2)}) collective-permute-start(bf16[128,1024]{1,0:T(8,128)(2,1)S(1)} %get-tuple-element.442), channel_id=1, source_target_pairs={{0,16},{4,20},{8,24},{12,28},{16,0},{20,4},{24,8},{28,12},{1,17},{... | collective-permute-start | bytes 786440 | tf_op jit(solution)/shard_map/ppermute | solution.py:84
  309.7 21.5 %collective-permute-start.73 = (bf16[512,768]{1,0:T(8,128)(2,1)}, bf16[512,768]{1,0:T(8,128)(2,1)}, u32[]{:S(2)}, u32[]{:S(2)}) collective-permute-start(bf16[512,768]{1,0:T(8,128)(2,1)} %constant_dynamic-slice_fusion.5), channel_id=1, source_target_pairs={{0,4},{4,0},{8,12},{12,8},{16,20},{20,16},{24,28},{28,24},{1,5},{5... | collective-permute-start | bytes 2359304 | tf_op jit(solution)/shard_map/ppermute | solution.py:84
  312.1 23.4 %collective-permute-start.72 = (bf16[512,768]{1,0:T(8,128)(2,1)}, bf16[512,768]{1,0:T(8,128)(2,1)}, u32[]{:S(2)}, u32[]{:S(2)}) collective-permute-start(bf16[512,768]{1,0:T(8,128)(2,1)} %constant_dynamic-slice_fusion.4), channel_id=1, source_target_pairs={{0,8},{4,12},{8,0},{12,4},{16,24},{20,28},{24,16},{28,20},{1,9},{5... | collective-permute-start | bytes 2359304 | tf_op jit(solution)/shard_map/ppermute | solution.py:84
  324.8 22.1 %collective-permute-start.83 = (bf16[128,1024]{1,0:T(8,128)(2,1)}, bf16[128,1024]{1,0:T(8,128)(2,1)}, u32[]{:S(2)}, u32[]{:S(2)}) collective-permute-start(bf16[128,1024]{1,0:T(8,128)(2,1)} %copy-done.50), channel_id=1, source_target_pairs={{0,16},{4,20},{8,24},{12,28},{16,0},{20,4},{24,8},{28,12},{1,17},{... | collective-permute-start | bytes 786440 | tf_op jit(solution)/shard_map/ppermute | solution.py:84
  328.2 24.0 %collective-permute-start.82 = (bf16[128,1024]{1,0:T(8,128)(2,1)S(1)}, bf16[128,1024]{1,0:T(8,128)(2,1)}, u32[]{:S(2)}, u32[]{:S(2)}) collective-permute-start(bf16[128,1024]{1,0:T(8,128)(2,1)S(1)} %get-tuple-element.468.refs_2_), channel_id=1, source_target_pairs={{0,16},{4,20},{8,24},{12,28},{16,0},{20,4},{24,8},{28,12},{1,17},{... | collective-permute-start | bytes 786440 | tf_op jit(solution)/shard_map/ppermute | solution.py:84
  333.6 21.9 %collective-permute-start.81 = (bf16[256,768]{1,0:T(8,128)(2,1)S(1)}, bf16[256,768]{1,0:T(8,128)(2,1)S(1)}, u32[]{:S(2)}, u32[]{:S(2)}) collective-permute-start(bf16[256,768]{1,0:T(8,128)(2,1)S(1)} %get-tuple-element.467), channel_id=1, source_target_pairs={{0,8},{4,12},{8,0},{12,4},{16,24},{20,28},{24,16},{28,20},{1,9},{5... | collective-permute-start | bytes 1179656 | tf_op jit(solution)/shard_map/ppermute | solution.py:84
  338.0 18.2 %collective-permute-start.80 = (bf16[256,768]{1,0:T(8,128)(2,1)S(1)}, bf16[256,768]{1,0:T(8,128)(2,1)S(1)}, u32[]{:S(2)}, u32[]{:S(2)}) collective-permute-start(bf16[256,768]{1,0:T(8,128)(2,1)S(1)} %get-tuple-element.465), channel_id=1, source_target_pairs={{0,4},{4,0},{8,12},{12,8},{16,20},{20,16},{24,28},{28,24},{1,5},{5... | collective-permute-start | bytes 1179656 | tf_op jit(solution)/shard_map/ppermute | solution.py:84
  348.8 17.9 %collective-permute-start.88 = (bf16[256,1024]{1,0:T(8,128)(2,1)S(1)}, bf16[256,1024]{1,0:T(8,128)(2,1)S(1)}, u32[]{:S(2)}, u32[]{:S(2)}) collective-permute-start(bf16[256,1024]{1,0:T(8,128)(2,1)S(1)} %bitcast.144), channel_id=1, source_target_pairs={{0,8},{4,12},{8,0},{12,4},{16,24},{20,28},{24,16},{28,20},{1,9},{5... | collective-permute-start | bytes 1572872 | tf_op jit(solution)/shard_map/ppermute | solution.py:84
  368.3 42.0 %collective-permute-start.93 = (bf16[512,1024]{1,0:T(8,128)(2,1)S(1)}, bf16[512,1024]{1,0:T(8,128)(2,1)S(1)}, u32[]{:S(2)}, u32[]{:S(2)}) collective-permute-start(bf16[512,1024]{1,0:T(8,128)(2,1)S(1)} %bitcast.176), channel_id=1, source_target_pairs={{0,4},{4,0},{8,12},{12,8},{16,20},{20,16},{24,28},{28,24},{1,5},{5... | collective-permute-start | bytes 3145736 | tf_op jit(solution)/shard_map/ppermute | solution.py:84
  372.1 40.5 %collective-permute-start.92 = (bf16[512,1024]{1,0:T(8,128)(2,1)S(1)}, bf16[512,1024]{1,0:T(8,128)(2,1)S(1)}, u32[]{:S(2)}, u32[]{:S(2)}) collective-permute-start(bf16[512,1024]{1,0:T(8,128)(2,1)S(1)} %bitcast.177), channel_id=1, source_target_pairs={{0,8},{4,12},{8,0},{12,4},{16,24},{20,28},{24,16},{28,20},{1,9},{5... | collective-permute-start | bytes 3145736 | tf_op jit(solution)/shard_map/ppermute | solution.py:84
  374.8 25.1 %collective-permute-start.86 = (bf16[128,768]{1,0:T(8,128)(2,1)S(1)}, bf16[128,768]{1,0:T(8,128)(2,1)S(1)}, u32[]{:S(2)}, u32[]{:S(2)}) collective-permute-start(bf16[128,768]{1,0:T(8,128)(2,1)S(1)} %get-tuple-element.482), channel_id=1, source_target_pairs={{0,16},{4,20},{8,24},{12,28},{16,0},{20,4},{24,8},{28,12},{1,17},{... | collective-permute-start | bytes 589832 | tf_op jit(solution)/shard_map/ppermute | solution.py:84
  379.1 25.6 %collective-permute-start.85 = (bf16[128,768]{1,0:T(8,128)(2,1)S(1)}, bf16[128,768]{1,0:T(8,128)(2,1)S(1)}, u32[]{:S(2)}, u32[]{:S(2)}) collective-permute-start(bf16[128,768]{1,0:T(8,128)(2,1)S(1)} %get-tuple-element.480), channel_id=1, source_target_pairs={{0,16},{4,20},{8,24},{12,28},{16,0},{20,4},{24,8},{28,12},{1,17},{... | collective-permute-start | bytes 589832 | tf_op jit(solution)/shard_map/ppermute | solution.py:84
  379.2 29.9 %collective-permute-start.84 = (bf16[32,1024]{1,0:T(8,128)(2,1)S(1)}, bf16[32,1024]{1,0:T(8,128)(2,1)S(1)}, u32[]{:S(2)}, u32[]{:S(2)}) collective-permute-start(bf16[32,1024]{1,0:T(8,128)(2,1)S(1)} %get-tuple-element.478), channel_id=1, source_target_pairs={{0,16},{4,20},{8,24},{12,28},{16,0},{20,4},{24,8},{28,12},{1,17},{... | collective-permute-start | bytes 196616 | tf_op jit(solution)/shard_map/ppermute | solution.py:84
  401.3 18.7 %collective-permute-start.91 = (bf16[128,768]{1,0:T(8,128)(2,1)S(1)}, bf16[128,768]{1,0:T(8,128)(2,1)S(1)}, u32[]{:S(2)}, u32[]{:S(2)}) collective-permute-start(bf16[128,768]{1,0:T(8,128)(2,1)S(1)} %get-tuple-element.496.refs_2_), channel_id=1, source_target_pairs={{0,16},{4,20},{8,24},{12,28},{16,0},{20,4},{24,8},{28,12},{1,17},{... | collective-permute-start | bytes 589832 | tf_op jit(solution)/shard_map/ppermute | solution.py:84
  406.0 18.2 %collective-permute-start.90 = (bf16[128,768]{1,0:T(8,128)(2,1)S(1)}, bf16[128,768]{1,0:T(8,128)(2,1)S(1)}, u32[]{:S(2)}, u32[]{:S(2)}) collective-permute-start(bf16[128,768]{1,0:T(8,128)(2,1)S(1)} %get-tuple-element.495.refs_2_), channel_id=1, source_target_pairs={{0,16},{4,20},{8,24},{12,28},{16,0},{20,4},{24,8},{28,12},{1,17},{... | collective-permute-start | bytes 589832 | tf_op jit(solution)/shard_map/ppermute | solution.py:84
  420.8 24.6 %collective-permute-start.96 = (bf16[256,768]{1,0:T(8,128)(2,1)S(1)}, bf16[256,768]{1,0:T(8,128)(2,1)S(1)}, u32[]{:S(2)}, u32[]{:S(2)}) collective-permute-start(bf16[256,768]{1,0:T(8,128)(2,1)S(1)} %bitcast.150), channel_id=1, source_target_pairs={{0,8},{4,12},{8,0},{12,4},{16,24},{20,28},{24,16},{28,20},{1,9},{5... | collective-permute-start | bytes 1179656 | tf_op jit(solution)/shard_map/ppermute | solution.py:84
  425.0 22.3 %collective-permute-start.95 = (bf16[256,768]{1,0:T(8,128)(2,1)S(1)}, bf16[256,768]{1,0:T(8,128)(2,1)S(1)}, u32[]{:S(2)}, u32[]{:S(2)}) collective-permute-start(bf16[256,768]{1,0:T(8,128)(2,1)S(1)} %bitcast.148), channel_id=1, source_target_pairs={{0,4},{4,0},{8,12},{12,8},{16,20},{20,16},{24,28},{28,24},{1,5},{5... | collective-permute-start | bytes 1179656 | tf_op jit(solution)/shard_map/ppermute | solution.py:84
  447.0 26.5 %collective-permute-start.99 = (bf16[512,768]{1,0:T(8,128)(2,1)S(1)}, bf16[512,768]{1,0:T(8,128)(2,1)S(1)}, u32[]{:S(2)}, u32[]{:S(2)}) collective-permute-start(bf16[512,768]{1,0:T(8,128)(2,1)S(1)} %bitcast.179), channel_id=1, source_target_pairs={{0,4},{4,0},{8,12},{12,8},{16,20},{20,16},{24,28},{28,24},{1,5},{5... | collective-permute-start | bytes 2359304 | tf_op jit(solution)/shard_map/ppermute | solution.py:84
  448.8 30.8 %collective-permute-start.98 = (bf16[512,768]{1,0:T(8,128)(2,1)S(1)}, bf16[512,768]{1,0:T(8,128)(2,1)S(1)}, u32[]{:S(2)}, u32[]{:S(2)}) collective-permute-start(bf16[512,768]{1,0:T(8,128)(2,1)S(1)} %bitcast.178), channel_id=1, source_target_pairs={{0,8},{4,12},{8,0},{12,4},{16,24},{20,28},{24,16},{28,20},{1,9},{5... | collective-permute-start | bytes 2359304 | tf_op jit(solution)/shard_map/ppermute | solution.py:84
  450.2 19.6 %collective-permute-start.42 = (bf16[160,1024]{1,0:T(8,128)(2,1)S(1)}, bf16[160,1024]{1,0:T(8,128)(2,1)S(1)}, u32[]{:S(2)}, u32[]{:S(2)}) collective-permute-start(bf16[160,1024]{1,0:T(8,128)(2,1)S(1)} %get-tuple-element.572), channel_id=1, source_target_pairs={{1,0},{0,1},{3,2},{2,3},{5,4},{4,5},{7,6},{6,7},{9,8},{8,9},{11,10... | collective-permute-start | bytes 983048 | tf_op jit(solution)/shard_map/ppermute | solution.py:932
  450.3 20.9 %collective-permute-start.41 = (bf16[160,1024]{1,0:T(8,128)(2,1)S(1)}, bf16[160,1024]{1,0:T(8,128)(2,1)S(1)}, u32[]{:S(2)}, u32[]{:S(2)}) collective-permute-start(bf16[160,1024]{1,0:T(8,128)(2,1)S(1)} %get-tuple-element.573), channel_id=1, source_target_pairs={{2,0},{3,1},{0,2},{1,3},{6,4},{7,5},{4,6},{5,7},{10,8},{11,9},{8,1... | collective-permute-start | bytes 983048 | tf_op jit(solution)/shard_map/ppermute | solution.py:932
  469.8 18.6 %collective-permute-start.105 = (bf16[160,1024]{1,0:T(8,128)(2,1)S(1)}, bf16[160,1024]{1,0:T(8,128)(2,1)S(1)}, u32[]{:S(2)}, u32[]{:S(2)}) collective-permute-start(bf16[160,1024]{1,0:T(8,128)(2,1)S(1)} %copy-done.85), channel_id=1, source_target_pairs={{0,2},{1,3},{2,0},{3,1},{4,6},{5,7},{6,4},{7,5},{8,10},{9,11},{10,... | collective-permute-start | bytes 983048 | tf_op jit(solution)/shard_map/ppermute | solution.py:84
  (192 other events, 2190.6 us)
